TPU v7x, 32 devices: a whole 2x2x4 slice. The times are simulated.
32 devices in a mesh: design: 2 (over y), gx: 4 (over z), gy: 2 (over x), src: 2 (over core).
Axes of the slice: x: 2, y: 2, z: 4, core: 2. Of those that a mesh axis runs over, the one named last changes fastest.
Arguments:
- field_state: float32 [4, 2, 2, 6, 32, 8, 512], P(('design', 'src'), None, None, None, None, 'gx', 'gy'), parts along dimension 0, may hold values from -6 to 6
- material_map: int32 [64, 8, 512], P('design', 'gx', 'gy'), parts along dimension 0, may hold values from 0 to 7
- eps_table: float32 [8], replicated, may hold values from 1 to 12
- bloch_phase: float32 [4], P('design'), parts along dimension 0, may hold values from -3.140625 to 3.140625
- source_cells: int32 [4, 2], P(('design', 'src')), parts along dimension 0, may hold values from 0 to 131071
- source_wave: float32 [4, 2, 2, 2], P(('design', 'src')), parts along dimension 0, may hold values from -8 to 8
Outputs:
- gradient: float32 [64, 8, 512], P('design', 'gx', 'gy'), parts along dimension 0
There are 2 independent parts, one for each index of `design`. A program takes and returns all parts, laid end to end along the dimension named above; an argument that names none is the same for every part. Nothing has to cross between parts.
All inputs are finite; a program needn't handle non-finite values.
Results may differ from a plain program's by a relative error of at most 0.0001.
Values sent between devices are 32-bit elements; how exact they have to be, the bound alone decides.
No kernel may reach another device: no remote copies, remote signals or barrier semaphores. Data moves between devices by JAX's collectives and lax.ppermute only.
A program may use at most 64 MiB of HBM per device.

v0:
```python
import jax
import jax.numpy as jnp
from jax import lax
from jax.sharding import PartitionSpec as P

STEPS = 2


COURANT = 0.5


def passed_along(value, axis, steps):
    count = lax.axis_size(axis)
    pairs = [(source, (source + steps) % count) for source in range(count)]
    return lax.ppermute(value, axis, pairs)


def rotate(values, cosine, sine_part):
    real_part = values[:, 0]
    imag_part = values[:, 1]
    return jnp.stack(
        [real_part * cosine - imag_part * sine_part, real_part * sine_part + imag_part * cosine],
        axis=1,
    )


def above_z(values):
    return jnp.concatenate([values[:, :, :, 1:], jnp.zeros_like(values[:, :, :, :1])], axis=3)


def below_z(values):
    return jnp.concatenate([jnp.zeros_like(values[:, :, :, :1]), values[:, :, :, :-1]], axis=3)


def advance_h(field_e, field_h, ahead_x, ahead_y):
    upper_e = above_z(field_e[:, :, 0:2])
    curl_x = ahead_y[:, :, 1] - field_e[:, :, 2] - (upper_e[:, :, 1] - field_e[:, :, 1])
    curl_y = upper_e[:, :, 0] - field_e[:, :, 0] - (ahead_x[:, :, 1] - field_e[:, :, 2])
    curl_z = ahead_x[:, :, 0] - field_e[:, :, 1] - (ahead_y[:, :, 0] - field_e[:, :, 0])
    return field_h - COURANT * jnp.stack([curl_x, curl_y, curl_z], axis=2)


def advance_e(field_e, field_h, behind_x, behind_y, eps_inv, source):
    lower_h = below_z(field_h[:, :, 0:2])
    curl_x = field_h[:, :, 2] - behind_y[:, :, 1] - (field_h[:, :, 1] - lower_h[:, :, 1])
    curl_y = field_h[:, :, 0] - lower_h[:, :, 0] - (field_h[:, :, 2] - behind_x[:, :, 1])
    curl_z = field_h[:, :, 1] - behind_x[:, :, 0] - (field_h[:, :, 0] - behind_y[:, :, 0])
    new_x = field_e[:, :, 0] + COURANT * eps_inv * curl_x
    new_y = field_e[:, :, 1] + COURANT * eps_inv * curl_y
    new_z = field_e[:, :, 2] + COURANT * eps_inv * curl_z + source
    return jnp.stack([new_x, new_y, new_z], axis=2)


def intersection(first_e, second_e):
    return jnp.sum(first_e[0] * second_e[0] - first_e[1] * second_e[1], axis=0)


def lookup(material_map, eps_table):
    levels = jnp.arange(eps_table.shape[0], dtype=jnp.int32)[:, None, None, None]
    return jnp.sum(
        jnp.where(material_map[None] == levels, eps_table[:, None, None, None], 0.0), axis=0
    )


def face_window(fields, eps_inv, source_mask, wave, bloch_phase, run_sign):
    angle_x = run_sign * bloch_phase[0]
    angle_y = run_sign * bloch_phase[1]
    cosine_x = jnp.cos(angle_x).reshape(2, 1, 1, 1, 1)
    sine_x = jnp.sin(angle_x).reshape(2, 1, 1, 1, 1)
    cosine_y = jnp.cos(angle_y).reshape(2, 1, 1, 1, 1)
    sine_y = jnp.sin(angle_y).reshape(2, 1, 1, 1, 1)
    last_x = lax.axis_index("gx") == lax.axis_size("gx") - 1
    last_y = lax.axis_index("gy") == lax.axis_size("gy") - 1
    first_x = lax.axis_index("gx") == 0
    first_y = lax.axis_index("gy") == 0
    field_e = fields[:, :, 0:3]
    field_h = fields[:, :, 3:6]
    stored = []
    for period in range(STEPS):
        face_x = passed_along(field_e[:, :, 1:3, :, 0:1, :], "gx", -1)
        face_x = jnp.where(last_x, rotate(face_x, cosine_x, sine_x), face_x)
        ahead_x = jnp.concatenate([field_e[:, :, 1:3, :, 1:, :], face_x], axis=4)
        face_y = passed_along(field_e[:, :, 0:3:2, :, :, 0:1], "gy", -1)
        face_y = jnp.where(last_y, rotate(face_y, cosine_y, sine_y), face_y)
        ahead_y = jnp.concatenate([field_e[:, :, 0:3:2, :, :, 1:], face_y], axis=5)
        field_h = advance_h(field_e, field_h, ahead_x, ahead_y)
        back_x = passed_along(field_h[:, :, 1:3, :, -1:, :], "gx", 1)
        back_x = jnp.where(first_x, rotate(back_x, cosine_x, -sine_x), back_x)
        behind_x = jnp.concatenate([back_x, field_h[:, :, 1:3, :, :-1, :]], axis=4)
        back_y = passed_along(field_h[:, :, 0:3:2, :, :, -1:], "gy", 1)
        back_y = jnp.where(first_y, rotate(back_y, cosine_y, -sine_y), back_y)
        behind_y = jnp.concatenate([back_y, field_h[:, :, 0:3:2, :, :, :-1]], axis=5)
        source = source_mask[:, None] * wave[:, :, period][:, :, None, None, None]
        field_e = advance_e(field_e, field_h, behind_x, behind_y, eps_inv, source)
        stored.append(field_e)
    return stored


def local(field_state, material_map, eps_table, bloch_phase, source_cells, source_wave):
    fields = field_state[0]
    cells = source_cells[0]
    wave = source_wave[0]
    cells_z, width_x, width_y = material_map.shape
    total_x = width_x * lax.axis_size("gx")
    total_y = width_y * lax.axis_size("gy")
    run_sign = jnp.array([1.0, -1.0], jnp.float32)
    eps_inv = 1.0 / lookup(material_map, eps_table)
    index_z = lax.broadcasted_iota(jnp.int32, (cells_z, width_x, width_y), 0)
    index_x = (
        lax.broadcasted_iota(jnp.int32, (cells_z, width_x, width_y), 1)
        + lax.axis_index("gx") * width_x
    )
    index_y = (
        lax.broadcasted_iota(jnp.int32, (cells_z, width_x, width_y), 2)
        + lax.axis_index("gy") * width_y
    )
    flat_index = (index_z * total_x + index_x) * total_y + index_y
    source_mask = (flat_index[None] == cells[:, None, None, None]).astype(jnp.float32)
    stored = face_window(fields, eps_inv, source_mask, wave, bloch_phase, run_sign)
    summed_terms = jnp.zeros(eps_inv.shape, jnp.float32)
    for period in range(STEPS):
        summed_terms = summed_terms + intersection(stored[period][0], stored[STEPS - 1 - period][1])
    summed_terms = lax.psum(summed_terms, "src")
    return -COURANT * eps_inv * summed_terms


def solution(mesh):
    return jax.shard_map(
        local,
        mesh=mesh,
        in_specs=(
            P(("design", "src"), None, None, None, None, "gx", "gy"),
            P("design", "gx", "gy"),
            P(),
            P("design"),
            P(("design", "src"), None),
            P(("design", "src"), None, None, None),
        ),
        out_specs=P("design", "gx", "gy"),
        check_vma=False,
    )
```

profile of v0, /device:TPU:0, one launch (start us, length us, event | category | flops | bytes accessed | tf_op | source)
XLA Modules:
  0.0 245.8 jit_solution(16172945712484827367)
XLA Ops:
  6.5 9.1 %copy.98 = f32[1,2,2,6,32,2,256]{4,5,6,3,2,1,0:T(2,128)} copy(f32[1,2,2,6,32,2,256]{6,5,4,3,2,1,0:T(2,128)} %param.7) | data formatting | bytes 3145728 | tf_op args[0]
  15.7 5.2 %fusion.34 = (f32[2,2,2,32,1,256]{3,4,5,2,1,0:T(1,128)}, f32[2,2,2,32,1,256]{3,4,5,2,1,0:T(1,128)S(1)}) fusion(f32[2,2,6,32,2,256]{3,4,5,2,1,0:T(2,128)} %bitcast.5), kind=kLoop, calls=%fused_computation.127 | loop fusion | bytes 1048576 | tf_op jit(solution)/shard_map/slice | solution.py:82
  20.9 1.6 copy.103
  22.6 5.3 %collective-permute-start.1 = (f32[2,2,2,32,1,256]{5,3,4,2,1,0:T(8,128)}, f32[2,2,2,32,1,256]{5,3,4,2,1,0:T(8,128)}, u32[]{:S(2)}, u32[]{:S(2)}) collective-permute-start(f32[2,2,2,32,1,256]{5,3,4,2,1,0:T(8,128)} %copy.103), channel_id=1, source_target_pairs={{0,12},{4,0},{8,4},{12,8},{1,13},{5,1},{9,5},{13,9},{2,14},{6,2},{... | collective-permute-start | bytes 786440 | tf_op jit(solution)/shard_map/ppermute | solution.py:15
  27.9 2.1 slice.383
  30.0 1.6 collective-permute-start
  35.9 1.6 slice.301
  37.5 3.9 %slice.389 = f32[2,2,2,31,2,256]{3,4,5,2,1,0:T(2,128)S(1)} slice(f32[2,2,6,32,2,256]{3,4,5,2,1,0:T(2,128)} %bitcast.7), slice={[0:2], [0:2], [0:2], [1:32], [0:2], [0:256]} | slice | bytes 1015808 | tf_op jit(solution)/shard_map/slice | solution.py:28
  41.4 1.7 copy.104
  43.1 2.7 %copy.100 = f32[2,2,2,32,2,255]{5,3,4,2,1,0:T(8,128)S(1)} copy(f32[2,2,2,32,2,255]{3,4,5,2,1,0:T(2,128)} %slice.301) | data formatting | bytes 1044480 | tf_op jit(solution)/shard_map/slice | solution.py:85
  48.5 2.1 copy.107
  52.7 1.8 fusion.23
  54.6 2.2 copy.105
  56.7 2.1 copy.106
  58.8 6.0 %fusion.1 = (f32[2,2,1,32,2,256]{3,4,5,2,1,0:T(2,128)}, f32[2,2,1,32,2,256]{3,4,5,2,1,0:T(2,128)}, f32[2,2,1,32,2,256]{3,4,5,2,1,0:T(2,128)}, f32[2,2,1,32,2,256]{3,4,5,2,1,0:T(2,128)}) fusion(f32[2,2,2,31,2,256]{3,4,5,2,1,0:T(2,128)S(1)} %slice.389, f32[2,2,1,32,2,256]{3,4,5,2,1,0:T(2,128)S(1)} %copy.102, f32[2,2,6,32,2,256]{3,4,5,2,1,0:T(2,128)} %bitcast.8, ...), kind=kLoop, calls=%fused_computation.10 | loop fusion | flops 524288 | bytes 3391488 | tf_op jit(solution)/shard_map/sub | solution.py:37
  64.9 1.5 copy.108
  68.9 3.4 %copy.113 = f32[2,2,3,32,2,256]{3,4,5,2,1,0:T(2,128)} copy(f32[2,2,3,32,2,256]{5,3,4,2,1,0:T(8,128)S(1)} %maximum_multiply_fusion) | data formatting | bytes 1572864 | tf_op jit(solution)/shard_map/mul | solution.py:40
  72.2 4.5 %slice_subtract_fusion = f32[2,2,3,32,2,256]{3,4,5,2,1,0:T(2,128)S(1)} fusion(f32[2,2,3,32,2,256]{3,4,5,2,1,0:T(2,128)} %copy.113, f32[2,2,6,32,2,256]{3,4,5,2,1,0:T(2,128)} %bitcast.9), kind=kLoop, calls=%fused_computation | loop fusion | flops 196608 | bytes 2359296 | tf_op jit(solution)/shard_map/sub | solution.py:40
  77.3 3.4 %fusion.37 = (f32[2,2,2,32,1,256]{3,4,5,2,1,0:T(1,128)}, f32[2,2,2,32,1,256]{3,4,5,2,1,0:T(1,128)}) fusion(f32[2,2,3,32,2,256]{3,4,5,2,1,0:T(2,128)S(1)} %slice_subtract_fusion), kind=kLoop, calls=%fused_computation.130 | loop fusion | bytes 1048576 | tf_op jit(solution)/shard_map/slice | solution.py:87
  80.7 1.5 slice.324
  82.2 1.5 slice.403
  83.7 3.4 %copy.161 = f32[2,2,2,32,1,256]{5,3,4,2,1,0:T(8,128)} copy(f32[2,2,2,32,1,256]{3,4,5,2,1,0:T(1,128)} %get-tuple-element.29) | data formatting | bytes 524288
  87.1 3.4 %copy.162 = f32[2,2,2,32,1,256]{5,3,4,2,1,0:T(8,128)} copy(f32[2,2,2,32,1,256]{3,4,5,2,1,0:T(1,128)} %get-tuple-element.30) | data formatting | bytes 524288
  90.5 3.8 %copy.160 = f32[2,2,2,32,2,255]{5,3,4,2,1,0:T(8,128)} copy(f32[2,2,2,32,2,255]{3,4,5,2,1,0:T(2,128)} %slice.324) | data formatting | bytes 1044480
  95.3 2.2 fusion.22
  97.4 2.1 copy.116
  99.6 2.1 copy.121
  102.8 1.8 fusion.21
  104.6 2.1 copy.119
  106.8 2.1 copy.120
  108.9 8.1 %multiply_add_fusion.2 = (f32[2,2,1,32,2,256]{3,4,5,2,1,0:T(2,128)}, f32[2,2,1,32,2,256]{3,4,5,2,1,0:T(2,128)}, f32[2,2,1,32,2,256]{3,4,5,2,1,0:T(2,128)}, f32[2,2,1,32,2,256]{3,4,5,2,1,0:T(2,128)}) fusion(f32[2,2,2,31,2,256]{3,4,5,2,1,0:T(2,128)} %slice.403, f32[2,2,1,32,2,256]{3,4,5,2,1,0:T(2,128)} %copy.116, ...), kind=kLoop, calls=%fused_computation.28 | loop fusion | flops 1179648 | bytes 4374560 | tf_op jit(solution)/shard_map/add | solution.py:48
  118.4 5.1 %select_maximum_fusion = f32[2,2,2,32,2,256]{3,4,5,2,1,0:T(2,128)} fusion(f32[2,2,1,32,2,256]{3,4,5,2,1,0:T(2,128)} %get-tuple-element.10, f32[2,2,1,32,2,256]{3,4,5,2,1,0:T(2,128)} %get-tuple-element.9), kind=kLoop, calls=%fused_computation.2 | loop fusion | flops 524288 | bytes 1048576 | tf_op jit(solution)/shard_map/stack | solution.py:51
  123.5 2.0 copy.126
  125.5 3.7 %pad_maximum_fusion = f32[2,2,3,32,2,256]{3,4,5,2,1,0:T(2,128)S(1)} fusion(f32[2,2,1,32,2,256]{3,4,5,2,1,0:T(2,128)} %get-tuple-element.11, f32[2,2,1,32,2,256]{3,4,5,2,1,0:T(2,128)} %get-tuple-element.10, f32[2,2,1,32,2,256]{3,4,5,2,1,0:T(2,128)} %get-tuple-element.9), kind=kLoop, calls=%fused_computation.1 | loop fusion | flops 393216 | bytes 1572864 | tf_op jit(solution)/shard_map/stack | solution.py:51
  129.3 1.7 fusion.35
  131.0 1.5 collective-permute-start.4
  133.3 1.5 slice.340
  134.8 2.0 copy.137
  136.8 4.8 %collective-permute-start.5 = (f32[2,2,2,32,1,256]{5,3,4,2,1,0:T(8,128)}, f32[2,2,2,32,1,256]{5,3,4,2,1,0:T(8,128)}, u32[]{:S(2)}, u32[]{:S(2)}) collective-permute-start(f32[2,2,2,32,1,256]{5,3,4,2,1,0:T(8,128)} %get-tuple-element.44), channel_id=1, source_target_pairs={{0,12},{4,0},{8,4},{12,8},{1,13},{5,1},{9,5},{13,9},{2,14},{6,2},{... | collective-permute-start | bytes 786440 | tf_op jit(solution)/shard_map/ppermute | solution.py:15
  141.6 3.8 %copy.122 = f32[2,2,2,32,2,255]{5,3,4,2,1,0:T(8,128)} copy(f32[2,2,2,32,2,255]{3,4,5,2,1,0:T(2,128)} %slice.340) | data formatting | bytes 1044480 | tf_op jit(solution)/shard_map/slice | solution.py:85
  145.4 2.0 copy.148
  147.4 1.9 copy.149
  149.4 1.9 copy.150
  151.3 2.0 copy.152
  153.2 1.9 copy.153
  158.2 2.3 fusion.20
  160.5 2.1 copy.124
  162.7 2.1 copy.127
  164.8 4.9 %fusion.13 = (f32[2,2,1,32,2,256]{3,4,5,2,1,0:T(2,128)}, f32[2,2,1,32,2,256]{3,4,5,2,1,0:T(2,128)}) fusion(f32[2,2,1,32,2,256]{3,4,5,2,1,0:T(2,128)} %get-tuple-element.10, f32[2,2,2,32,2,256]{3,4,5,2,1,0:T(2,128)} %select_maximum_fusion, f32[2,2,1,32,2,256]{3,4,5,2,1,0:T(2,128)} %copy.124, f32[2,2,1,32,2,256]{3,4,5,2,1,0:T(2,128)} %get-tuple-element.11, ...), kind=kLoop, calls=%fused_computation.24 | loop fusion | flops 393216 | bytes 2359296 | tf_op jit(solution)/shard_map/sub | solution.py:37
  169.7 2.1 copy.130
  171.8 2.0 copy.131
  173.8 2.1 maximum_multiply_fusion.1
  175.9 5.1 %copy.133 = f32[2,2,3,32,2,256]{3,4,5,2,1,0:T(2,128)} copy(f32[2,2,3,32,2,256]{5,3,4,2,1,0:T(8,128)} %maximum_multiply_fusion.1) | data formatting | bytes 1572864 | tf_op jit(solution)/shard_map/mul | solution.py:40
  181.0 3.5 %sub.267 = f32[2,2,3,32,2,256]{3,4,5,2,1,0:T(2,128)S(1)} subtract(f32[2,2,3,32,2,256]{3,4,5,2,1,0:T(2,128)S(1)} %slice_subtract_fusion, f32[2,2,3,32,2,256]{3,4,5,2,1,0:T(2,128)} %copy.133) | non-fusion elementwise | flops 196608 | bytes 2359296 | tf_op jit(solution)/shard_map/sub | solution.py:40
  185.2 2.6 %fusion.36 = (f32[2,2,2,32,1,256]{3,4,5,2,1,0:T(1,128)}, f32[2,2,2,32,1,256]{3,4,5,2,1,0:T(1,128)S(1)}) fusion(f32[2,2,3,32,2,256]{3,4,5,2,1,0:T(2,128)S(1)} %sub.267), kind=kLoop, calls=%fused_computation.129 | loop fusion | bytes 1048576 | tf_op jit(solution)/shard_map/slice | solution.py:87
  189.4 3.4 %copy.164 = f32[2,2,2,32,1,256]{5,3,4,2,1,0:T(8,128)} copy(f32[2,2,2,32,1,256]{3,4,5,2,1,0:T(1,128)} %get-tuple-element.25) | data formatting | bytes 524288
  192.8 1.7 copy.165
  198.4 2.9 %collective-permute-done.7 = f32[2,2,2,32,1,256]{5,3,4,2,1,0:T(8,128)} collective-permute-done((f32[2,2,2,32,1,256]{5,3,4,2,1,0:T(8,128)}, f32[2,2,2,32,1,256]{5,3,4,2,1,0:T(8,128)}, u32[]{:S(2)}, u32[]{:S(2)}) %collective-permute-start.7) | collective-permute-done | bytes 262176 | tf_op jit(solution)/shard_map/ppermute | solution.py:15
  202.4 2.0 fusion.16
  204.4 2.1 copy.141
  206.6 2.2 copy.144
  208.7 6.2 %fusion.15 = (f32[2,2,1,32,2,256]{3,4,5,2,1,0:T(2,128)}, f32[2,2,1,32,2,256]{3,4,5,2,1,0:T(2,128)}, f32[2,2,1,32,2,256]{3,4,5,2,1,0:T(2,128)}) fusion(f32[2,2,2,31,2,256]{3,4,5,2,1,0:T(2,128)} %slice.431, f32[2,2,1,32,2,256]{3,4,5,2,1,0:T(2,128)} %copy.136, f32[2,2,3,32,2,256]{3,4,5,2,1,0:T(2,128)S(1)} %copy-done.1, f32[32,2,256]{0,1,2:T(2,128)} %copy-done.7, ...), kind=kLoop, calls=%fused_computation.30 | loop fusion | flops 786432 | bytes 3194880 | tf_op jit(solution)/shard_map/mul | solution.py:48
  215.0 1.5 copy.138
  220.1 17.3 %all-reduce.6.cloned.1.call-done = f32[32,2,256]{2,0,1:T(8,128)} async-done(((f32[32,2,256]{2,0,1:T(8,128)}), f32[32,2,256]{2,0,1:T(8,128)}) %all-reduce.6.cloned.1.call-update) | async-done | bytes 65552 | tf_op jit(solution)/shard_map/psum | solution.py:123
  (120 shorter events, 31.7 us)
Async XLA Ops:
  6.5 230.9 %all-reduce.6.cloned.1.call-start = ((), (), s32[]{:S(2)}) async-start(), calls=%async_computation | async-start | bytes 131072 | tf_op jit(solution)/shard_map/psum | solution.py:123
  22.5 9.0 %copy-start.19 = (f32[2]{0:T(128)S(1)}, f32[2]{0:T(128)}, u32[]{:S(2)}) copy-start(f32[2]{0:T(128)} %param.10) | copy-start | bytes 28
  22.5 9.6 %copy-start.17 = (s32[32,2,256]{2,1,0:T(2,128)S(1)}, s32[32,2,256]{2,1,0:T(2,128)}, u32[]{:S(2)}) copy-start(s32[32,2,256]{2,1,0:T(2,128)} %param.8) | copy-start | bytes 196612
  22.5 9.6 %copy-start.20 = (f32[8]{0:T(128)S(1)}, f32[8]{0:T(128)}, u32[]{:S(2)}) copy-start(f32[8]{0:T(128)} %param.9) | copy-start | bytes 100
  22.5 10.7 %copy-start.22 = (s32[1,2]{1,0:T(1,128)S(1)}, s32[1,2]{1,0:T(1,128)}, u32[]{:S(2)}) copy-start(s32[1,2]{1,0:T(1,128)} %param.11) | copy-start | bytes 28
  22.6 11.8 %copy-start.21 = (f32[2]{0:T(128)S(1)}, f32[2]{0:T(128)}, u32[]{:S(2)}) copy-start(f32[2]{0:T(128)} %constant.35.clone) | copy-start | bytes 28
  22.6 13.2 %copy-start.18 = (f32[1,2,2,2]{3,2,1,0:T(2,128)S(1)}, f32[1,2,2,2]{3,2,1,0:T(2,128)}, u32[]{:S(2)}) copy-start(f32[1,2,2,2]{3,2,1,0:T(2,128)} %param.12) | copy-start | bytes 100
  22.6 28.1 %collective-permute-start.1 = (f32[2,2,2,32,1,256]{5,3,4,2,1,0:T(8,128)}, f32[2,2,2,32,1,256]{5,3,4,2,1,0:T(8,128)}, u32[]{:S(2)}, u32[]{:S(2)}) collective-permute-start(f32[2,2,2,32,1,256]{5,3,4,2,1,0:T(8,128)} %copy.103), channel_id=1, source_target_pairs={{0,12},{4,0},{8,4},{12,8},{1,13},{5,1},{9,5},{13,9},{2,14},{6,2},{... | collective-permute-start | bytes 786440 | tf_op jit(solution)/shard_map/ppermute | solution.py:15
  30.0 15.9 %collective-permute-start = (f32[2,2,2,32,2,1]{3,4,5,2,1,0:T(2,128)S(1)}, f32[2,2,2,32,2,1]{3,4,5,2,1,0:T(2,128)S(1)}, u32[]{:S(2)}, u32[]{:S(2)}) collective-permute-start(f32[2,2,2,32,2,1]{3,4,5,2,1,0:T(2,128)S(1)} %slice.302), channel_id=1, source_target_pairs={{0,2},{2,0},{1,3},{3,1},{4,6},{6,4},{5,7},{7,5},{8,10},{10,8},{9,1... | collective-permute-start | bytes 6152 | tf_op jit(solution)/shard_map/ppermute | solution.py:15
  32.3 0.6 copy-start.15
  37.5 3.9 %copy-start.4 = (f32[2,2,2,32,1,256]{3,4,5,2,1,0:T(1,128)S(1)}, f32[2,2,2,32,1,256]{3,4,5,2,1,0:T(1,128)}, u32[]{:S(2)}) copy-start(f32[2,2,2,32,1,256]{3,4,5,2,1,0:T(1,128)} %get-tuple-element.16) | copy-start | bytes 786436
  45.9 63.0 %copy-start.7 = (f32[32,2,256]{0,1,2:T(2,128)}, f32[32,2,256]{0,1,2:T(2,128)S(1)}, u32[]{:S(2)}) copy-start(f32[32,2,256]{0,1,2:T(2,128)S(1)} %copy.99) | copy-start | bytes 196612
  64.9 3.0 %copy-start.6 = (f32[2,2,1,32,2,256]{3,4,5,2,1,0:T(2,128)S(1)}, f32[2,2,1,32,2,256]{3,4,5,2,1,0:T(2,128)}, u32[]{:S(2)}) copy-start(f32[2,2,1,32,2,256]{3,4,5,2,1,0:T(2,128)} %get-tuple-element.12) | copy-start | bytes 786436
  64.9 3.4 %copy-start.5 = (f32[2,2,1,32,2,256]{3,4,5,2,1,0:T(2,128)S(1)}, f32[2,2,1,32,2,256]{3,4,5,2,1,0:T(2,128)}, u32[]{:S(2)}) copy-start(f32[2,2,1,32,2,256]{3,4,5,2,1,0:T(2,128)} %get-tuple-element.13) | copy-start | bytes 786436
  76.7 17.6 %collective-permute-start.2 = (f32[2,2,2,32,2,1]{3,4,5,2,1,0:T(2,128)S(1)}, f32[2,2,2,32,2,1]{3,4,5,2,1,0:T(2,128)S(1)}, u32[]{:S(2)}, u32[]{:S(2)}) collective-permute-start(f32[2,2,2,32,2,1]{3,4,5,2,1,0:T(2,128)S(1)} %slice.321), channel_id=1, source_target_pairs={{0,2},{2,0},{1,3},{3,1},{4,6},{6,4},{5,7},{7,5},{8,10},{10,8},{9,1... | collective-permute-start | bytes 6152 | tf_op jit(solution)/shard_map/ppermute | solution.py:15
  87.1 14.6 %collective-permute-start.3 = (f32[2,2,2,32,1,256]{5,3,4,2,1,0:T(8,128)}, f32[2,2,2,32,1,256]{5,3,4,2,1,0:T(8,128)}, u32[]{:S(2)}, u32[]{:S(2)}) collective-permute-start(f32[2,2,2,32,1,256]{5,3,4,2,1,0:T(8,128)} %copy.161), channel_id=1, source_target_pairs={{0,4},{4,8},{8,12},{12,0},{1,5},{5,9},{9,13},{13,1},{2,6},{6,10},{... | collective-permute-start | bytes 786440 | tf_op jit(solution)/shard_map/ppermute | solution.py:15
  129.3 3.2 %copy-start.8 = (f32[2,2,1,32,2,256]{5,3,4,2,1,0:T(8,128)S(1)}, f32[2,2,1,32,2,256]{5,3,4,2,1,0:T(8,128)}, u32[]{:S(2)}) copy-start(f32[2,2,1,32,2,256]{5,3,4,2,1,0:T(8,128)} %copy.126) | copy-start | bytes 786436
  131.0 24.2 %collective-permute-start.4 = (f32[2,2,2,32,2,1]{3,4,5,2,1,0:T(2,128)S(1)}, f32[2,2,2,32,2,1]{3,4,5,2,1,0:T(2,128)S(1)}, u32[]{:S(2)}, u32[]{:S(2)}) collective-permute-start(f32[2,2,2,32,2,1]{3,4,5,2,1,0:T(2,128)S(1)} %slice.341), channel_id=1, source_target_pairs={{0,2},{2,0},{1,3},{3,1},{4,6},{6,4},{5,7},{7,5},{8,10},{10,8},{9,1... | collective-permute-start | bytes 6152 | tf_op jit(solution)/shard_map/ppermute | solution.py:15
  136.8 19.3 %collective-permute-start.5 = (f32[2,2,2,32,1,256]{5,3,4,2,1,0:T(8,128)}, f32[2,2,2,32,1,256]{5,3,4,2,1,0:T(8,128)}, u32[]{:S(2)}, u32[]{:S(2)}) collective-permute-start(f32[2,2,2,32,1,256]{5,3,4,2,1,0:T(8,128)} %get-tuple-element.44), channel_id=1, source_target_pairs={{0,12},{4,0},{8,4},{12,8},{1,13},{5,1},{9,5},{13,9},{2,14},{6,2},{... | collective-permute-start | bytes 786440 | tf_op jit(solution)/shard_map/ppermute | solution.py:15
  184.6 3.4 %copy-start = (f32[2,2,3,32,2,256]{3,4,5,2,1,0:T(2,128)}, f32[2,2,3,32,2,256]{3,4,5,2,1,0:T(2,128)S(1)}, u32[]{:S(2)}) copy-start(f32[2,2,3,32,2,256]{3,4,5,2,1,0:T(2,128)S(1)} %sub.267) | copy-start | bytes 2359300
  184.6 10.8 %collective-permute-start.6 = (f32[2,2,2,32,2,1]{3,4,5,2,1,0:T(2,128)S(1)}, f32[2,2,2,32,2,1]{3,4,5,2,1,0:T(2,128)S(1)}, u32[]{:S(2)}, u32[]{:S(2)}) collective-permute-start(f32[2,2,2,32,2,1]{3,4,5,2,1,0:T(2,128)S(1)} %slice.356), channel_id=1, source_target_pairs={{0,2},{2,0},{1,3},{3,1},{4,6},{6,4},{5,7},{7,5},{8,10},{10,8},{9,1... | collective-permute-start | bytes 6152 | tf_op jit(solution)/shard_map/ppermute | solution.py:15
  192.8 8.5 %collective-permute-start.7 = (f32[2,2,2,32,1,256]{5,3,4,2,1,0:T(8,128)}, f32[2,2,2,32,1,256]{5,3,4,2,1,0:T(8,128)}, u32[]{:S(2)}, u32[]{:S(2)}) collective-permute-start(f32[2,2,2,32,1,256]{5,3,4,2,1,0:T(8,128)} %copy.164), channel_id=1, source_target_pairs={{0,4},{4,8},{8,12},{12,0},{1,5},{5,9},{9,13},{13,1},{2,6},{6,10},{... | collective-permute-start | bytes 786440 | tf_op jit(solution)/shard_map/ppermute | solution.py:15
  202.4 6.4 %copy-start.1 = (f32[2,2,3,32,2,256]{3,4,5,2,1,0:T(2,128)S(1)}, f32[2,2,3,32,2,256]{3,4,5,2,1,0:T(2,128)}, u32[]{:S(2)}) copy-start(f32[2,2,3,32,2,256]{3,4,5,2,1,0:T(2,128)} %copy-done) | copy-start | bytes 2359300
  214.9 2.6 %copy-start.3 = (f32[2,2,1,32,2,256]{3,4,5,2,1,0:T(2,128)S(1)}, f32[2,2,1,32,2,256]{3,4,5,2,1,0:T(2,128)}, u32[]{:S(2)}) copy-start(f32[2,2,1,32,2,256]{3,4,5,2,1,0:T(2,128)} %get-tuple-element.19) | copy-start | bytes 786436
  214.9 3.2 %copy-start.2 = (f32[2,2,1,32,2,256]{3,4,5,2,1,0:T(2,128)S(1)}, f32[2,2,1,32,2,256]{3,4,5,2,1,0:T(2,128)}, u32[]{:S(2)}) copy-start(f32[2,2,1,32,2,256]{3,4,5,2,1,0:T(2,128)} %get-tuple-element.20) | copy-start | bytes 786436
  216.5 2.1 copy-start.9
  216.5 2.1 copy-start.10
  218.1 0.9 copy-start.11
  218.1 1.0 copy-start.12
  218.1 1.1 copy-start.13
  218.1 1.2 copy-start.14
  218.6 18.8 %copy-start.16 = (f32[32,2,256]{2,0,1:T(8,128)S(1)}, f32[32,2,256]{2,0,1:T(8,128)}, u32[]{:S(2)}) copy-start(f32[32,2,256]{2,0,1:T(8,128)} %copy-done.15) | copy-start | bytes 196612
Sparse Core Ops, SparseCore 0:
  220.2 17.1 all-reduce.5
where the time goes:
time: 248 us; the launch traced here: 246 us
  local copies, waits for them, and re-layouts  128 us (52%)
  other arithmetic  68.8 us (28%)
  waiting for transfers between devices  20.3 us (8%)
  starting transfers between devices  14.3 us (6%)
  between operations  13.9 us (6%)
    unnamed x54, local copies, waits for them, and re-layouts  26.9 us
    psum x1, waiting for transfers between devices, local(): summed_terms = lax.psum(summed_terms, 'src')  17.3 us
    ppermute x8, starting transfers between devices, passed_along(): return lax.ppermute(value, axis, pairs)  14.3 us
    sub x2, other arithmetic, advance_h(): ahead_y[:, :, 1] - field_e[:, :, 2] - (upper_e[:, :, 1] - field_e[:, :, 1])  10.9 us
    another operation x4, other arithmetic, advance_e(): return jnp.stack([new_x, new_y, new_z], axis=2)  9.66 us
    slice x4, local copies, waits for them, and re-layouts, face_window(): ahead_y = jnp.concatenate([field_e[:, :, 0:3:2, :, :, 1:], face_y], axis=5)  9.47 us
    slice x5, local copies, waits for them, and re-layouts, intersection(): return jnp.sum(first_e[0] * second_e[0] - first_e[1] * second_e[1], axis=0)  9.44 us
    add x2, other arithmetic, advance_e(): new_x = field_e[:, :, 0] + COURANT * eps_inv * curl_x  9.19 us
  transfers between devices with their start and end apart: 9, of which 2 were waited for; matrix products, arithmetic and copies ran while one was open for 31% of the time, Pallas kernels for 0%

commit v1 on v0

v1 whole, which is shorter than its diff:
```python
import functools

import jax
import jax.numpy as jnp
from jax import lax
from jax.experimental import pallas as pl
from jax.experimental.pallas import tpu as pltpu
from jax.sharding import PartitionSpec as P

COURANT = 0.5
LANES = 128
EDGE = 4
HIGHEST = 64 * 1024 * 1024


def lane_iota(nz):
    return lax.broadcasted_iota(jnp.int32, (nz, LANES), 1)


def row_iota(nz):
    return lax.broadcasted_iota(jnp.int32, (nz, LANES), 0)


def pack_edges(values, lane):
    packed = jnp.zeros_like(values[0])
    for spot, value in enumerate(values):
        moved = pltpu.roll(value, EDGE * spot + 2, 1)
        packed = jnp.where(lane // EDGE == spot, moved, packed)
    return packed


def unpack_edge(packed, spot):
    return pltpu.roll(packed, LANES - EDGE * spot - 2, 1)


class Shifts:
    def __init__(self, nz):
        self.nz = nz
        self.row = row_iota(nz)
        self.lane = lane_iota(nz)

    def z_up(self, value):
        return jnp.where(self.row == self.nz - 1, 0.0, pltpu.roll(value, self.nz - 1, 0))

    def z_down(self, value):
        return jnp.where(self.row == 0, 0.0, pltpu.roll(value, 1, 0))

    def y_up(self, tiles):
        moved = [pltpu.roll(value, LANES - 1, 1) for value in tiles]
        count = len(tiles)
        return [jnp.where(self.lane == LANES - 1, moved[(t + 1) % count], moved[t]) for t in range(count)]

    def y_down(self, tiles):
        moved = [pltpu.roll(value, 1, 1) for value in tiles]
        count = len(tiles)
        return [jnp.where(self.lane == 0, moved[(t - 1) % count], moved[t]) for t in range(count)]


def turn(real_part, imag_part, cosine, sine):
    return real_part * cosine - imag_part * sine, real_part * sine + imag_part * cosine


def phases(phase_ref):
    row = lax.broadcasted_iota(jnp.int32, (8, LANES), 0)
    angle = jnp.where(row == 0, phase_ref[0], phase_ref[1])
    cosine, sine = jnp.cos(angle), jnp.sin(angle)
    return cosine[0:1], sine[0:1], cosine[1:2], sine[1:2]


def y_turn(cosine_y, sine_y, lane):
    first = lax.axis_index("gy") == 0
    last = lax.axis_index("gy") == lax.axis_size("gy") - 1
    upper = lane < LANES // 2
    cosine = jnp.where(upper, jnp.where(last, cosine_y, 1.0), jnp.where(first, cosine_y, 1.0))
    return cosine, jnp.where(upper, jnp.where(last, sine_y, 0.0), jnp.where(first, -sine_y, 0.0))


def inverse_eps(material, table_ref):
    level = jnp.full(material.shape, table_ref[0], jnp.float32)
    for index in range(1, table_ref.shape[0]):
        level = jnp.where(material == index, table_ref[index], level)
    return 1.0 / level


def spot_of(run, part, comp):
    return (run * 2 + part) * 6 + comp


class Local:
    def __init__(self, dims, field_ref, edge_ref, table_ref, material_ref, cells_ref, wave_ref):
        self.nz, self.width_x, self.tiles = dims
        self.field_ref, self.edge_ref = field_ref, edge_ref
        self.table_ref, self.material_ref = table_ref, material_ref
        self.cells_ref, self.wave_ref = cells_ref, wave_ref
        self.shifts = Shifts(self.nz)

    def rows(self, x, t):
        return pl.ds(t * self.width_x + x, self.nz, stride=self.tiles * self.width_x)

    def own(self, run, part, comp, x, t):
        return self.field_ref[spot_of(run, part, comp), self.rows(x, t), :]

    def edge(self, x):
        return self.edge_ref[x * self.nz:(x + 1) * self.nz, :]

    def load(self, run, comp, x, turn_y):
        cosine, sine = turn_y
        packed = self.edge(x)
        parts = [[self.own(run, part, comp, x, t) for t in range(self.tiles)] for part in range(2)]
        edges = [unpack_edge(packed, spot_of(run, part, comp)) for part in range(2)]
        edges = turn(edges[0], edges[1], cosine, sine if run == 0 else -sine)
        return [parts[part] + [edges[part]] for part in range(2)]

    def eps(self, x):
        own = [inverse_eps(self.material_ref[self.rows(x, t), :], self.table_ref) for t in range(self.tiles)]
        return own + [unpack_edge(self.edge(x), 24)]

    def hits(self, run, x):
        total_x = self.width_x * lax.axis_size("gx")
        width_y = self.tiles * LANES
        total_y = width_y * lax.axis_size("gy")
        begin_y = lax.axis_index("gy") * width_y
        plane = self.shifts.row * total_x + lax.axis_index("gx") * self.width_x + x
        masks = []
        for t in range(self.tiles + 1):
            lane = self.shifts.lane
            if t < self.tiles:
                column = begin_y + t * LANES + lane
            else:
                column = begin_y + jnp.where(lane < LANES // 2, lane + width_y, lane - LANES)
                column = jnp.where(column < 0, column + total_y, column)
                column = jnp.where(column >= total_y, column - total_y, column)
            masks.append(plane * total_y + column == self.cells_ref[run])
        return masks

    def source(self, run, step, masks, turn_y):
        cosine, sine = turn_y
        amplitude = [self.wave_ref[(run * 2 + part) * 2 + step] for part in range(2)]
        turned = turn(amplitude[0], amplitude[1], cosine, sine if run == 0 else -sine)
        return [
            [jnp.where(mask, amplitude[part] if t < self.tiles else turned[part], 0.0) for t, mask in enumerate(masks)]
            for part in range(2)
        ]


def first_kernel(dims, field_ref, material_ref, table_ref, face_ref, edge_ref):
    nz, width_x, tiles = dims
    local = Local(dims, field_ref, None, table_ref, material_ref, None, None)
    lane = lane_iota(nz)
    for run in range(2):
        for part in range(2):
            for which in range(2):
                for t in range(tiles):
                    at = (((run * 2 + part) * 2 + which) * tiles + t) * nz
                    face_ref[at:at + nz, :] = local.own(run, part, 1 + which, 0, t)
    for x in range(width_x):
        values = []
        for run in range(2):
            for part in range(2):
                for comp in range(6):
                    values.append(
                        jnp.where(
                            lane < LANES // 2,
                            local.own(run, part, comp, x, 0),
                            local.own(run, part, comp, x, tiles - 1),
                        )
                    )
        material = jnp.where(
            lane < LANES // 2, material_ref[local.rows(x, 0), :], material_ref[local.rows(x, tiles - 1), :]
        )
        values.append(inverse_eps(material, table_ref))
        edge_ref[x * nz:(x + 1) * nz, :] = pack_edges(values, lane)


def merged_edges(below_ref, above_ref, edge_ref):
    if above_ref is None:
        return below_ref
    lane = lax.broadcasted_iota(jnp.int32, below_ref.shape, 1)
    edge_ref[...] = jnp.where(lane % EDGE < 2, below_ref[...], above_ref[...])
    return edge_ref


def second_kernel(
    dims, two, field_ref, material_ref, table_ref, phase_ref, cells_ref, wave_ref, below_ref, above_ref, down_ref, up_ref,
    edge_ref,
):
    nz, width_x, tiles = dims
    edges = merged_edges(below_ref, None if two else above_ref, edge_ref)
    local = Local(dims, field_ref, edges, table_ref, material_ref, cells_ref, wave_ref)
    shifts = local.shifts
    _, _, cosine_y, sine_y = phases(phase_ref)
    turn_y = y_turn(cosine_y, sine_y, shifts.lane)
    every = range(tiles + 1)
    eps = local.eps(0)
    half = [COURANT * value for value in eps]
    down_edges = [None] * 17
    up_edges = []
    for run in range(2):
        low = [local.load(run, comp, 0, turn_y) for comp in range(6)]
        nearer = [local.load(run, comp, 1, turn_y) for comp in (1, 2)]
        source = local.source(run, 0, local.hits(run, 0), turn_y)
        for part in range(2):
            ex, ey, ez, hx, hy, hz = [low[comp][part] for comp in range(6)]
            ey_x, ez_x = nearer[0][part], nearer[1][part]
            ez_y, ex_y = shifts.y_up(ez), shifts.y_up(ex)
            hx = [hx[t] - COURANT * (ez_y[t] - ez[t] - (shifts.z_up(ey[t]) - ey[t])) for t in every]
            hy = [hy[t] - COURANT * (shifts.z_up(ex[t]) - ex[t] - (ez_x[t] - ez[t])) for t in every]
            hz = [hz[t] - COURANT * (ey_x[t] - ey[t] - (ex_y[t] - ex[t])) for t in every]
            hx_y = shifts.y_down(hx)
            new_y = [ey[t] + half[t] * (hx[t] - shifts.z_down(hx[t]) - hz[t]) for t in every]
            new_z = [ez[t] + half[t] * (hy[t] - (hx[t] - hx_y[t])) + source[part][t] for t in every]
            for which, value, initial in ((0, new_y, ey), (1, new_z, ez)):
                unit = (run * 2 + part) * 2 + which
                for t in range(tiles):
                    at = (unit * tiles + t) * nz
                    down_ref[at:at + nz, :] = value[t]
                down_edges[unit] = initial[tiles]
                down_edges[8 + unit] = value[tiles]
        high = [local.load(run, comp, width_x - 1, turn_y) for comp in (0, 1, 2, 4, 5)]
        for part in range(2):
            ex, ey, ez, hy, hz = [values[part] for values in high]
            ex_y = shifts.y_up(ex)
            hy = [hy[t] - COURANT * (shifts.z_up(ex[t]) - ex[t] + ez[t]) for t in every]
            hz = [hz[t] + COURANT * (ey[t] + (ex_y[t] - ex[t])) for t in every]
            for which, value in ((0, hy), (1, hz)):
                unit = (run * 2 + part) * 2 + which
                for t in range(tiles):
                    at = (unit * tiles + t) * nz
                    up_ref[at:at + nz, :] = value[t]
                up_edges.append(value[tiles])
    for t in range(tiles):
        at = (8 * tiles + t) * nz
        down_ref[at:at + nz, :] = eps[t]
    down_edges[16] = eps[tiles]
    at = 9 * tiles * nz
    down_ref[at:at + nz, :] = pack_edges(down_edges, shifts.lane)
    at = 8 * tiles * nz
    up_ref[at:at + nz, :] = pack_edges(up_edges, shifts.lane)


def third_kernel(
    dims, two, field_ref, material_ref, table_ref, phase_ref, cells_ref, wave_ref, below_ref, above_ref,
    face_ref, down_ref, up_ref, cross_ref, share_ref, edge_ref,
):
    nz, width_x, tiles = dims
    edges = merged_edges(below_ref, None if two else above_ref, edge_ref)
    local = Local(dims, field_ref, edges, table_ref, material_ref, cells_ref, wave_ref)
    shifts = local.shifts
    cosine_x, sine_x, cosine_y, sine_y = phases(phase_ref)
    turn_y = y_turn(cosine_y, sine_y, shifts.lane)
    first = lax.axis_index("gx") == 0
    last = lax.axis_index("gx") == lax.axis_size("gx") - 1
    ahead = (jnp.where(last, cosine_x, 1.0), jnp.where(last, sine_x, 0.0))
    back = (jnp.where(first, cosine_x, 1.0), jnp.where(first, -sine_x, 0.0))
    every = range(tiles + 1)
    own = range(tiles)
    layers = range(width_x)

    def block(ref, index):
        return ref[index * nz:(index + 1) * nz, :]

    eps = [local.eps(x) for x in layers]
    half = [[COURANT * value for value in eps[x]] for x in layers]
    down_edge = block(down_ref, 9 * tiles)
    up_edge = block(up_ref, 8 * tiles)
    eps_next = [block(down_ref, 8 * tiles + t) for t in own] + [unpack_edge(down_edge, 16)]
    half_next = [COURANT * value for value in eps_next]

    def halo(ref, edge, first_spot, run, which, cosine, sine):
        units = [(run * 2 + part) * 2 + which for part in range(2)]
        values = [
            [block(ref, unit * tiles + t) for t in own] + [unpack_edge(edge, first_spot + unit)] for unit in units
        ]
        signed = sine if run == 0 else -sine
        turned = [turn(values[0][t], values[1][t], cosine, signed) for t in every]
        return [[turned[t][part] for t in every] for part in range(2)]

    kept_one, kept_two, kept_next, kept_high = {}, {}, {}, {}
    for run in range(2):
        masks = [local.hits(run, x) for x in layers]
        sources = [[local.source(run, step, masks[x], turn_y) for x in layers] for step in range(2)]
        fields = [[local.load(run, comp, x, turn_y) for x in layers] for comp in range(6)]
        ahead_y0 = halo(face_ref, down_edge, 0, run, 0, *ahead)
        ahead_z0 = halo(face_ref, down_edge, 0, run, 1, *ahead)
        ahead_y1 = halo(down_ref, down_edge, 8, run, 0, *ahead)
        ahead_z1 = halo(down_ref, down_edge, 8, run, 1, *ahead)
        back_y = halo(up_ref, up_edge, 0, run, 0, *back)
        back_z = halo(up_ref, up_edge, 0, run, 1, *back)
        for part in range(2):
            ex, ey, ez, hx, hy, hz = [[fields[comp][x][part] for x in layers] for comp in range(6)]
            below_y = [back_y[part][t] + COURANT * ez[0][t] for t in every]
            below_z = [back_z[part][t] - COURANT * ey[0][t] for t in every]
            next_y, next_z = ahead_y0[part], ahead_z0[part]
            for step in range(2):
                ey_x, ez_x = ey[1:] + [next_y], ez[1:] + [next_z]
                for x in layers:
                    ez_y, ex_y = shifts.y_up(ez[x]), shifts.y_up(ex[x])
                    hx[x] = [hx[x][t] - COURANT * (ez_y[t] - ez[x][t] - (shifts.z_up(ey[x][t]) - ey[x][t])) for t in every]
                    hy[x] = [hy[x][t] - COURANT * (shifts.z_up(ex[x][t]) - ex[x][t] - (ez_x[x][t] - ez[x][t])) for t in every]
                    hz[x] = [hz[x][t] - COURANT * (ey_x[x][t] - ey[x][t] - (ex_y[t] - ex[x][t])) for t in every]
                if step == 0:
                    next_y = [ahead_y1[part][t] + half_next[t] * hz[-1][t] for t in every]
                    next_z = [ahead_z1[part][t] - half_next[t] * hy[-1][t] for t in every]
                for x in layers:
                    hz_y, hx_y = shifts.y_down(hz[x]), shifts.y_down(hx[x])
                    span = every if step == 0 else own
                    if x > 0:
                        hy_x, hz_x = hy[x - 1], hz[x - 1]
                    elif step == 0:
                        hy_x, hz_x = below_y, below_z
                    else:
                        hy_x, hz_x = None, None
                    new_x, new_y, new_z = [], [], []
                    for t in span:
                        diff_y = hz[x][t] if hz_x is None else hz[x][t] - hz_x[t]
                        diff_z = hy[x][t] if hy_x is None else hy[x][t] - hy_x[t]
                        new_x.append(ex[x][t] + half[x][t] * (hz[x][t] - hz_y[t] - (hy[x][t] - shifts.z_down(hy[x][t]))))
                        new_y.append(ey[x][t] + half[x][t] * (hx[x][t] - shifts.z_down(hx[x][t]) - diff_y))
                        new_z.append(
                            ez[x][t] + half[x][t] * (diff_z - (hx[x][t] - hx_y[t])) + sources[step][x][part][t]
                        )
                    ex[x], ey[x], ez[x] = new_x, new_y, new_z
                if step == 0:
                    kept_one[run, part] = (list(ex), list(ey), list(ez))
                    kept_next[run, part] = (next_y, next_z)
                else:
                    kept_two[run, part] = (ex, ey, ez)
                    kept_high[run, part] = (hy[-1], hz[-1])

    for t in own:
        for x in layers:
            total = None
            for comp in range(3):
                for now, later in ((kept_one, kept_two), (kept_two, kept_one)):
                    term = (
                        now[0, 0][comp][x][t] * later[1, 0][comp][x][t] - now[0, 1][comp][x][t] * later[1, 1][comp][x][t]
                    )
                    total = term if total is None else total + term
            cross_ref[local.rows(x, t), :] = total
        total = None
        for run in range(2):
            for which, sign in ((0, 1.0), (1, -1.0)):
                term = (
                    kept_next[run, 0][which][t] * kept_high[1 - run, 0][1 - which][t]
                    - kept_next[run, 1][which][t] * kept_high[1 - run, 1][1 - which][t]
                )
                term = term if sign > 0 else -term
                total = term if total is None else total + term
        share_ref[t * nz:(t + 1) * nz, :] = half_next[t] * total


def last_kernel(dims, material_ref, table_ref, cross_ref, other_ref, same_share_ref, other_share_ref, out_ref):
    nz, width_x, tiles = dims
    local = Local(dims, None, None, table_ref, material_ref, None, None)
    for x in range(width_x):
        for t in range(tiles):
            rows = local.rows(x, t)
            total = cross_ref[rows, :] + other_ref[rows, :]
            if x == 0:
                span = slice(t * nz, (t + 1) * nz)
                total = total + (same_share_ref[span, :] + other_share_ref[span, :])
            out_ref[rows, :] = -COURANT * inverse_eps(material_ref[rows, :], table_ref) * total


VMEM = pl.BlockSpec(memory_space=pltpu.VMEM)
SMEM = pl.BlockSpec(memory_space=pltpu.SMEM)


def call(kernel, name, in_specs, shapes, cost, scratch=()):
    return pl.pallas_call(
        kernel,
        name=name,
        out_shape=[jax.ShapeDtypeStruct(shape, jnp.float32) for shape in shapes],
        in_specs=in_specs,
        out_specs=[VMEM] * len(shapes),
        scratch_shapes=list(scratch),
        compiler_params=pltpu.CompilerParams(vmem_limit_bytes=48 * 1024 * 1024),
        cost_estimate=pl.CostEstimate(flops=cost, bytes_accessed=cost, transcendentals=0),
    )


def moved(value, axis, steps):
    count = lax.axis_size(axis)
    return lax.ppermute(value, axis, [(source, (source + steps) % count) for source in range(count)])


def local(field_state, material_map, eps_table, bloch_phase, source_cells, source_wave):
    nz, width_x, width_y = material_map.shape
    tiles = width_y // LANES
    dims = (nz, width_x, tiles)
    rows = nz * tiles * width_x
    fields = field_state.reshape(24, nz, width_x, tiles, LANES).transpose(0, 1, 3, 2, 4).reshape(24, rows, LANES)
    material = material_map.reshape(nz, width_x, tiles, LANES).transpose(0, 2, 1, 3).reshape(rows, LANES)
    cells = source_cells.reshape(2)
    wave = source_wave.reshape(8)
    unit = nz * tiles
    two = lax.axis_size("gy") == 2
    count_x, count_src = lax.axis_size("gx"), lax.axis_size("src")

    face, edge = call(
        functools.partial(first_kernel, dims), "faces", [VMEM, VMEM, SMEM],
        [(8 * unit, LANES), (width_x * nz, LANES)], 2_000_000,
    )(fields, material, eps_table)
    face = moved(face, "gx", -1)
    below = moved(edge, "gy", 1)
    above = below if two else moved(edge, "gy", -1)
    scratch = (pltpu.VMEM((width_x * nz, LANES), jnp.float32),)
    down, up = call(
        functools.partial(second_kernel, dims, two), "partials", [VMEM, VMEM, SMEM, SMEM, SMEM, SMEM, VMEM, VMEM],
        [(9 * unit + nz, LANES), (8 * unit + nz, LANES)], 4_000_000, scratch,
    )(fields, material, eps_table, bloch_phase, cells, wave, below, above)
    down = moved(down, "gx", -1)
    up = moved(up, "gx", 1)
    cross, share = call(
        functools.partial(third_kernel, dims, two), "steps",
        [VMEM, VMEM, SMEM, SMEM, SMEM, SMEM, VMEM, VMEM, VMEM, VMEM, VMEM],
        [(rows, LANES), (unit, LANES)], 8_000_000, scratch,
    )(fields, material, eps_table, bloch_phase, cells, wave, below, above, face, down, up)
    same_share = moved(share, "gx", 1)
    other_share = lax.ppermute(
        share, ("gx", "src"),
        [
            (x * count_src + s, ((x + 1) % count_x) * count_src + (s + 1) % count_src)
            for x in range(count_x)
            for s in range(count_src)
        ],
    )
    other = moved(cross, "src", 1)
    (out,) = call(
        functools.partial(last_kernel, dims), "gradient", [VMEM, SMEM, VMEM, VMEM, VMEM, VMEM],
        [(rows, LANES)], 500_000,
    )(material, eps_table, cross, other, same_share, other_share)
    return out.reshape(nz, tiles, width_x, LANES).transpose(0, 2, 1, 3).reshape(nz, width_x, width_y)


def solution(mesh):
    return jax.shard_map(
        local,
        mesh=mesh,
        in_specs=(
            P(("design", "src"), None, None, None, None, "gx", "gy"),
            P("design", "gx", "gy"),
            P(),
            P("design"),
            P(("design", "src"), None),
            P(("design", "src"), None, None, None),
        ),
        out_specs=P("design", "gx", "gy"),
        check_vma=False,
    )
```

time: 248 us -> 42.5 us (0.17)
  local copies, waits for them, and re-layouts: 128 us -> 3.03 us
  other arithmetic: 68.8 us -> 0 us
  between operations: 13.9 us -> 0.06 us
  Pallas kernels: 0 us -> 5.97 us
    slice x40 -> x0, local copies, waits for them, and re-layouts: 72.3 us -> none  [the longest x4 9.47 us: face_window(): ahead_y = jnp.concatenate([field_e[:, :, 0:3:2, :, :, 1:], face_y], axis=5)]
    unnamed x54 -> x18, local copies, waits for them, and re-layouts: 26.9 us -> 2.94 us
    sub x13 -> x0, other arithmetic: 23.5 us -> none  [the longest x2 10.9 us: advance_h(): ahead_y[:, :, 1] - field_e[:, :, 2] - (upper_e[:, :, 1] - field_e[:, :, 1])]
    psum x1 -> x0, waiting for transfers between devices: 17.3 us -> none  [local(): summed_terms = lax.psum(summed_terms, 'src')]
    ppermute x8 -> x7, waiting for transfers between devices: 2.95 us -> 20 us  [the longest x6 16 us: moved(): lax.ppermute(value, axis, [(source, (source + steps) % count) for source...]
    mul x8 -> x0, local copies, waits for them, and re-layouts: 13.8 us -> none  [the longest x2 8.5 us: advance_h(): return field_h - COURANT * jnp.stack([curl_x, curl_y, curl_z], axis=2)]
    concatenate x7 -> x0, other arithmetic: 11.3 us -> none  [the longest x2 3.81 us: face_window(): behind_x = jnp.concatenate([back_x, field_h[:, :, 1:3, :, :-1, :]], axis=4)]
    add x8 -> x0, other arithmetic: 10.3 us -> none  [the longest x2 9.19 us: advance_e(): new_x = field_e[:, :, 0] + COURANT * eps_inv * curl_x]
  transfers between devices with their start and end apart: 9 -> 7, of which waited for: 2 -> 4; matrix products, arithmetic and copies ran while one was open for 31% -> 0% of each run, Pallas kernels for 0% -> 0%
where the time goes in v1:
time: 42.5 us; the launch traced here: 42.3 us
  waiting for transfers between devices  20 us (47%)
  starting transfers between devices  13.2 us (31%)
  Pallas kernels  5.97 us (14%)
  local copies, waits for them, and re-layouts  3.03 us (7%)
    ppermute x6, waiting for transfers between devices, moved(): lax.ppermute(value, axis, [(source, (source + steps) % count) for source...  16 us
    ppermute x6, starting transfers between devices, moved(): lax.ppermute(value, axis, [(source, (source + steps) % count) for source...  12.7 us
    ppermute x1, waiting for transfers between devices, local(): lax.ppermute(share, ('gx', 'src'), [(x * count_src + s, (x + 1) % count_x...  3.94 us
    unnamed x18, local copies, waits for them, and re-layouts  2.94 us
    pallas_call x1, Pallas kernels, local(): call(functools.partial(third_kernel, dims, two), 'steps', [VMEM, VMEM, SM...  2.48 us
    pallas_call x1, Pallas kernels, local(): call(functools.partial(second_kernel, dims, two), 'partials', [VMEM, VMEM...  1.45 us
    pallas_call x1, Pallas kernels, local(): call(functools.partial(last_kernel, dims), 'gradient', [VMEM, SMEM, VMEM,...  1.22 us
  transfers between devices with their start and end apart: 7, of which 4 were waited for; matrix products, arithmetic and copies ran while one was open for 0% of the time, Pallas kernels for 0%

profile of v1, /device:TPU:0, one launch (start us, length us, event | category | flops | bytes accessed | tf_op | source)
XLA Modules:
  0.0 42.3 jit_solution(10518180437813509319)
XLA Ops:
  0.0 0.0 copy-start.5
  0.0 0.0 copy-start.8
  0.0 0.0 copy-start.6
  0.0 0.0 copy-start.7
  0.0 0.0 copy-start
  0.0 1.4 %copy-done = f32[1,2,2,6,32,2,256]{6,5,4,3,2,1,0:T(2,128)S(1)} copy-done((f32[1,2,2,6,32,2,256]{6,5,4,3,2,1,0:T(2,128)S(1)}, f32[1,2,2,6,32,2,256]{6,5,4,3,2,1,0:T(2,128)}, u32[]{:S(2)}) %copy-start) | copy-done | bytes 1572888
  1.4 0.0 copy-start.2
  1.4 0.8 %copy-done.2 = s32[32,2,256]{2,1,0:T(2,128)S(1)} copy-done((s32[32,2,256]{2,1,0:T(2,128)S(1)}, s32[32,2,256]{2,1,0:T(2,128)}, u32[]{:S(2)}) %copy-start.2) | copy-done | bytes 65560
  2.3 0.0 copy-start.4
  2.3 0.7 %copy-done.4 = f32[8]{0:T(128)S(1)} copy-done((f32[8]{0:T(128)S(1)}, f32[8]{0:T(128)}, u32[]{:S(2)}) %copy-start.4) | copy-done | bytes 56
  2.9 0.0 copy-start.1
  2.9 0.0 copy-start.3
  2.9 0.8 %faces.1 = (f32[512,128]{1,0:T(8,128)S(1)}, f32[64,128]{1,0:T(8,128)S(1)}) custom-call(f32[24,128,128]{2,1,0:T(8,128)S(1)} %bitcast.16, s32[128,128]{1,0:T(8,128)S(1)} %bitcast.19, f32[8]{0:T(128)S(1)} %copy-done.4), custom_call_target="tpu_custom_call" | custom-call | flops 2000000 | bytes 2000000 | tf_op jit(solution)/shard_map/faces/pallas_call | solution.py:400
  3.8 3.0 %collective-permute-start = (f32[64,128]{1,0:T(8,128)S(1)}, f32[64,128]{1,0:T(8,128)S(1)}, u32[]{:S(2)}, u32[]{:S(2)}) collective-permute-start(f32[64,128]{1,0:T(8,128)S(1)} %get-tuple-element.11), channel_id=1, source_target_pairs={{0,2},{2,0},{1,3},{3,1},{4,6},{6,4},{5,7},{7,5},{8,10},{10,8},{9,1... | collective-permute-start | bytes 98312 | tf_op jit(solution)/shard_map/ppermute | solution.py:384
  6.8 0.0 copy-done.8
  6.8 0.1 reshape.29.wave_ref
  6.8 1.8 %collective-permute-done.below_ref.above_ref = f32[64,128]{1,0:T(8,128)S(1)} collective-permute-done((f32[64,128]{1,0:T(8,128)S(1)}, f32[64,128]{1,0:T(8,128)S(1)}, u32[]{:S(2)}, u32[]{:S(2)}) %collective-permute-start) | collective-permute-done | bytes 32800 | tf_op jit(solution)/shard_map/ppermute | solution.py:384
  8.7 0.0 copy-done.5
  8.7 0.0 copy-done.6
  8.7 0.0 copy-done.7
  8.7 0.0 copy-done.1
  8.7 0.0 copy-done.3
  8.7 1.4 %partials.1 = (f32[608,128]{1,0:T(8,128)S(1)}, f32[544,128]{1,0:T(8,128)S(1)}) custom-call(f32[24,128,128]{2,1,0:T(8,128)S(1)} %bitcast.17, s32[128,128]{1,0:T(8,128)S(1)} %bitcast.20, f32[8]{0:T(128)S(1)} %copy-done.5, f32[2]{0:T(128)S(1)} %copy-done.6, s32[2]{0:T(128)S(1)} %bitcast.23, f32[8]{0:T(128)S(1)} %reshape.29.wave_ref, ...), custom_call_target="tpu_custom_call" | custom-call | flops 4000000 | bytes 4000000 | tf_op jit(solution)/shard_map/partials/pallas_call | solution.py:408
  10.1 4.2 %collective-permute-start.2 = (f32[608,128]{1,0:T(8,128)S(1)}, f32[608,128]{1,0:T(8,128)S(1)}, u32[]{:S(2)}, u32[]{:S(2)}) collective-permute-start(f32[608,128]{1,0:T(8,128)S(1)} %get-tuple-element.13), channel_id=1, source_target_pairs={{0,12},{4,0},{8,4},{12,8},{1,13},{5,1},{9,5},{13,9},{2,14},{6,2},{... | collective-permute-start | bytes 933896 | tf_op jit(solution)/shard_map/ppermute | solution.py:384
  14.3 0.0 collective-permute-start.3
  14.3 3.8 %collective-permute-start.1 = (f32[512,128]{1,0:T(8,128)S(1)}, f32[512,128]{1,0:T(8,128)S(1)}, u32[]{:S(2)}, u32[]{:S(2)}) collective-permute-start(f32[512,128]{1,0:T(8,128)S(1)} %get-tuple-element.12), channel_id=1, source_target_pairs={{0,12},{4,0},{8,4},{12,8},{1,13},{5,1},{9,5},{13,9},{2,14},{6,2},{... | collective-permute-start | bytes 786440 | tf_op jit(solution)/shard_map/ppermute | solution.py:384
  18.2 13.3 %collective-permute-done.1.face_ref = f32[512,128]{1,0:T(8,128)S(1)} collective-permute-done((f32[512,128]{1,0:T(8,128)S(1)}, f32[512,128]{1,0:T(8,128)S(1)}, u32[]{:S(2)}, u32[]{:S(2)}) %collective-permute-start.1) | collective-permute-done | bytes 262176 | tf_op jit(solution)/shard_map/ppermute | solution.py:384
  31.4 0.0 collective-permute-done.3.up_ref
  31.4 0.0 collective-permute-done.2.down_ref
  31.4 2.5 %steps.1 = (f32[128,128]{1,0:T(8,128)S(1)}, f32[64,128]{1,0:T(8,128)S(1)}) custom-call(f32[24,128,128]{2,1,0:T(8,128)S(1)} %bitcast.18, s32[128,128]{1,0:T(8,128)S(1)} %bitcast.21, f32[8]{0:T(128)S(1)} %copy-done.5, f32[2]{0:T(128)S(1)} %copy-done.6, s32[2]{0:T(128)S(1)} %bitcast.24, f32[8]{0:T(128)S(1)} %reshape.29.wave_ref, ...), custom_call_target="tpu_custom_call" | custom-call | flops 8000000 | bytes 8000000 | tf_op jit(solution)/shard_map/steps/pallas_call | solution.py:414
  33.9 0.1 collective-permute-start.4
  34.0 0.5 %collective-permute-start.6 = (f32[64,128]{1,0:T(8,128)S(1)}, f32[64,128]{1,0:T(8,128)S(1)}, u32[]{:S(2)}, u32[]{:S(2)}) collective-permute-start(f32[64,128]{1,0:T(8,128)S(1)} %get-tuple-element.16), channel_id=1, source_target_pairs={{0,5},{1,4},{4,9},{5,8},{8,13},{9,12},{12,1},{13,0},{2,7},{3,6},{6... | collective-permute-start | bytes 98312 | tf_op jit(solution)/shard_map/ppermute | solution.py:420
  34.5 1.6 %collective-permute-start.5 = (f32[64,128]{1,0:T(8,128)S(1)}, f32[64,128]{1,0:T(8,128)S(1)}, u32[]{:S(2)}, u32[]{:S(2)}) collective-permute-start(f32[64,128]{1,0:T(8,128)S(1)} %get-tuple-element.16), channel_id=1, source_target_pairs={{0,4},{4,8},{8,12},{12,0},{1,5},{5,9},{9,13},{13,1},{2,6},{6,10},{... | collective-permute-start | bytes 98312 | tf_op jit(solution)/shard_map/ppermute | solution.py:384
  36.1 3.9 %collective-permute-done.6.other_share_ref = f32[64,128]{1,0:T(8,128)S(1)} collective-permute-done((f32[64,128]{1,0:T(8,128)S(1)}, f32[64,128]{1,0:T(8,128)S(1)}, u32[]{:S(2)}, u32[]{:S(2)}) %collective-permute-start.6) | collective-permute-done | bytes 32800 | tf_op jit(solution)/shard_map/ppermute | solution.py:420
  40.1 1.0 %collective-permute-done.5.same_share_ref = f32[64,128]{1,0:T(8,128)S(1)} collective-permute-done((f32[64,128]{1,0:T(8,128)S(1)}, f32[64,128]{1,0:T(8,128)S(1)}, u32[]{:S(2)}, u32[]{:S(2)}) %collective-permute-start.5) | collective-permute-done | bytes 32800 | tf_op jit(solution)/shard_map/ppermute | solution.py:384
  41.0 0.0 collective-permute-done.4.other_ref
  41.0 1.2 %gradient.1 = f32[128,128]{1,0:T(8,128)} custom-call(s32[128,128]{1,0:T(8,128)S(1)} %bitcast.22, f32[8]{0:T(128)S(1)} %copy-done.5, f32[128,128]{1,0:T(8,128)S(1)} %get-tuple-element.15.cross_ref, f32[128,128]{1,0:T(8,128)S(1)} %collective-permute-done.4.other_ref, f32[64,128]{1,0:T(8,128)S(1)} %collective-permute-done.5.same_share_ref, ...), custom_call_target="tpu_custom_call" | custom-call | flops 500000 | bytes 500000 | tf_op jit(solution)/shard_map/gradient/pallas_call | solution.py:429
Async XLA Ops:
  0.0 8.7 %copy-start.5 = (f32[8]{0:T(128)S(1)}, f32[8]{0:T(128)}, u32[]{:S(2)}) copy-start(f32[8]{0:T(128)} %table_ref.7) | copy-start | bytes 100
  0.0 6.8 %copy-start.8 = (f32[1,2,2,2]{3,2,1,0:T(2,128)S(1)}, f32[1,2,2,2]{3,2,1,0:T(2,128)}, u32[]{:S(2)}) copy-start(f32[1,2,2,2]{3,2,1,0:T(2,128)} %param.11) | copy-start | bytes 100
  0.0 8.7 %copy-start.6 = (f32[2]{0:T(128)S(1)}, f32[2]{0:T(128)}, u32[]{:S(2)}) copy-start(f32[2]{0:T(128)} %phase_ref.3) | copy-start | bytes 28
  0.0 8.7 %copy-start.7 = (s32[1,2]{1,0:T(1,128)S(1)}, s32[1,2]{1,0:T(1,128)}, u32[]{:S(2)}) copy-start(s32[1,2]{1,0:T(1,128)} %param.10) | copy-start | bytes 28
  0.0 1.4 %copy-start = (f32[1,2,2,6,32,2,256]{6,5,4,3,2,1,0:T(2,128)S(1)}, f32[1,2,2,6,32,2,256]{6,5,4,3,2,1,0:T(2,128)}, u32[]{:S(2)}) copy-start(f32[1,2,2,6,32,2,256]{6,5,4,3,2,1,0:T(2,128)} %param.6) | copy-start | bytes 4718596
  1.4 0.8 %copy-start.2 = (s32[32,2,256]{2,1,0:T(2,128)S(1)}, s32[32,2,256]{2,1,0:T(2,128)}, u32[]{:S(2)}) copy-start(s32[32,2,256]{2,1,0:T(2,128)} %param.7) | copy-start | bytes 196612
  2.3 0.7 %copy-start.4 = (f32[8]{0:T(128)S(1)}, f32[8]{0:T(128)}, u32[]{:S(2)}) copy-start(f32[8]{0:T(128)} %table_ref.7) | copy-start | bytes 100
  2.9 5.7 %copy-start.1 = (f32[1,2,2,6,32,2,256]{6,5,4,3,2,1,0:T(2,128)S(1)}, f32[1,2,2,6,32,2,256]{6,5,4,3,2,1,0:T(2,128)}, u32[]{:S(2)}) copy-start(f32[1,2,2,6,32,2,256]{6,5,4,3,2,1,0:T(2,128)} %param.6) | copy-start | bytes 4718596
  2.9 5.7 %copy-start.3 = (s32[32,2,256]{2,1,0:T(2,128)S(1)}, s32[32,2,256]{2,1,0:T(2,128)}, u32[]{:S(2)}) copy-start(s32[32,2,256]{2,1,0:T(2,128)} %param.7) | copy-start | bytes 196612
  3.8 4.9 %collective-permute-start = (f32[64,128]{1,0:T(8,128)S(1)}, f32[64,128]{1,0:T(8,128)S(1)}, u32[]{:S(2)}, u32[]{:S(2)}) collective-permute-start(f32[64,128]{1,0:T(8,128)S(1)} %get-tuple-element.11), channel_id=1, source_target_pairs={{0,2},{2,0},{1,3},{3,1},{4,6},{6,4},{5,7},{7,5},{8,10},{10,8},{9,1... | collective-permute-start | bytes 98312 | tf_op jit(solution)/shard_map/ppermute | solution.py:384
  10.1 21.3 %collective-permute-start.2 = (f32[608,128]{1,0:T(8,128)S(1)}, f32[608,128]{1,0:T(8,128)S(1)}, u32[]{:S(2)}, u32[]{:S(2)}) collective-permute-start(f32[608,128]{1,0:T(8,128)S(1)} %get-tuple-element.13), channel_id=1, source_target_pairs={{0,12},{4,0},{8,4},{12,8},{1,13},{5,1},{9,5},{13,9},{2,14},{6,2},{... | collective-permute-start | bytes 933896 | tf_op jit(solution)/shard_map/ppermute | solution.py:384
  14.3 17.1 %collective-permute-start.3 = (f32[544,128]{1,0:T(8,128)S(1)}, f32[544,128]{1,0:T(8,128)S(1)}, u32[]{:S(2)}, u32[]{:S(2)}) collective-permute-start(f32[544,128]{1,0:T(8,128)S(1)} %get-tuple-element.14), channel_id=1, source_target_pairs={{0,4},{4,8},{8,12},{12,0},{1,5},{5,9},{9,13},{13,1},{2,6},{6,10},{... | collective-permute-start | bytes 835592 | tf_op jit(solution)/shard_map/ppermute | solution.py:384
  14.3 17.1 %collective-permute-start.1 = (f32[512,128]{1,0:T(8,128)S(1)}, f32[512,128]{1,0:T(8,128)S(1)}, u32[]{:S(2)}, u32[]{:S(2)}) collective-permute-start(f32[512,128]{1,0:T(8,128)S(1)} %get-tuple-element.12), channel_id=1, source_target_pairs={{0,12},{4,0},{8,4},{12,8},{1,13},{5,1},{9,5},{13,9},{2,14},{6,2},{... | collective-permute-start | bytes 786440 | tf_op jit(solution)/shard_map/ppermute | solution.py:384
  33.9 7.1 %collective-permute-start.4 = (f32[128,128]{1,0:T(8,128)S(1)}, f32[128,128]{1,0:T(8,128)S(1)}, u32[]{:S(2)}, u32[]{:S(2)}) collective-permute-start(f32[128,128]{1,0:T(8,128)S(1)} %get-tuple-element.15.cross_ref), channel_id=1, source_target_pairs={{0,1},{1,0},{2,3},{3,2},{4,5},{5,4},{6,7},{7,6},{8,9},{9,8},{10,11... | collective-permute-start | bytes 196616 | tf_op jit(solution)/shard_map/ppermute | solution.py:384
  34.0 6.1 %collective-permute-start.6 = (f32[64,128]{1,0:T(8,128)S(1)}, f32[64,128]{1,0:T(8,128)S(1)}, u32[]{:S(2)}, u32[]{:S(2)}) collective-permute-start(f32[64,128]{1,0:T(8,128)S(1)} %get-tuple-element.16), channel_id=1, source_target_pairs={{0,5},{1,4},{4,9},{5,8},{8,13},{9,12},{12,1},{13,0},{2,7},{3,6},{6... | collective-permute-start | bytes 98312 | tf_op jit(solution)/shard_map/ppermute | solution.py:420
  34.5 6.5 %collective-permute-start.5 = (f32[64,128]{1,0:T(8,128)S(1)}, f32[64,128]{1,0:T(8,128)S(1)}, u32[]{:S(2)}, u32[]{:S(2)}) collective-permute-start(f32[64,128]{1,0:T(8,128)S(1)} %get-tuple-element.16), channel_id=1, source_target_pairs={{0,4},{4,8},{8,12},{12,0},{1,5},{5,9},{9,13},{13,1},{2,6},{6,10},{... | collective-permute-start | bytes 98312 | tf_op jit(solution)/shard_map/ppermute | solution.py:384

commit v2 on v1

v2 whole, which is shorter than its diff:
```python
import functools

import jax
import jax.numpy as jnp
from jax import lax
from jax.experimental import pallas as pl
from jax.experimental.pallas import tpu as pltpu
from jax.sharding import PartitionSpec as P

COURANT = 0.5
LANES = 128
EDGE = 4


def lane_iota(nz):
    return lax.broadcasted_iota(jnp.int32, (nz, LANES), 1)


def row_iota(nz):
    return lax.broadcasted_iota(jnp.int32, (nz, LANES), 0)


def pack_edges(values, lane):
    packed = jnp.zeros_like(values[0])
    for spot, value in enumerate(values):
        moved = pltpu.roll(value, EDGE * spot + 2, 1)
        packed = jnp.where(lane // EDGE == spot, moved, packed)
    return packed


def unpack_edge(packed, spot):
    return pltpu.roll(packed, LANES - EDGE * spot - 2, 1)


class Shifts:
    def __init__(self, nz):
        self.nz = nz
        self.row = row_iota(nz)
        self.lane = lane_iota(nz)

    def z_up(self, value):
        return jnp.where(self.row == self.nz - 1, 0.0, pltpu.roll(value, self.nz - 1, 0))

    def z_down(self, value):
        return jnp.where(self.row == 0, 0.0, pltpu.roll(value, 1, 0))

    def y_up(self, tiles):
        moved = [pltpu.roll(value, LANES - 1, 1) for value in tiles]
        count = len(tiles)
        return [jnp.where(self.lane == LANES - 1, moved[(t + 1) % count], moved[t]) for t in range(count)]

    def y_down(self, tiles):
        moved = [pltpu.roll(value, 1, 1) for value in tiles]
        count = len(tiles)
        return [jnp.where(self.lane == 0, moved[(t - 1) % count], moved[t]) for t in range(count)]


def turn(real_part, imag_part, cosine, sine):
    return real_part * cosine - imag_part * sine, real_part * sine + imag_part * cosine


def phases(phase_ref):
    row = lax.broadcasted_iota(jnp.int32, (8, LANES), 0)
    angle = jnp.where(row == 0, phase_ref[0], phase_ref[1])
    cosine, sine = jnp.cos(angle), jnp.sin(angle)
    return cosine[0:1], sine[0:1], cosine[1:2], sine[1:2]


def y_turn(cosine_y, sine_y, lane):
    first = lax.axis_index("gy") == 0
    last = lax.axis_index("gy") == lax.axis_size("gy") - 1
    upper = lane < LANES // 2
    cosine = jnp.where(upper, jnp.where(last, cosine_y, 1.0), jnp.where(first, cosine_y, 1.0))
    return cosine, jnp.where(upper, jnp.where(last, sine_y, 0.0), jnp.where(first, -sine_y, 0.0))


def inverse_eps(material, table_ref):
    level = jnp.full(material.shape, table_ref[0], jnp.float32)
    for index in range(1, table_ref.shape[0]):
        level = jnp.where(material == index, table_ref[index], level)
    return 1.0 / level


def spot_of(run, part, comp):
    return (run * 2 + part) * 6 + comp


class Local:
    def __init__(self, dims, field_ref, edge_ref, table_ref, material_ref, cells_ref, wave_ref):
        self.nz, self.width_x, self.tiles = dims
        self.field_ref, self.edge_ref = field_ref, edge_ref
        self.table_ref, self.material_ref = table_ref, material_ref
        self.cells_ref, self.wave_ref = cells_ref, wave_ref
        self.shifts = Shifts(self.nz)

    def rows(self, x, t):
        return pl.ds(t * self.width_x + x, self.nz, stride=self.tiles * self.width_x)

    def own(self, run, part, comp, x, t):
        return self.field_ref[spot_of(run, part, comp), self.rows(x, t), :]

    def edge(self, x):
        return self.edge_ref[x * self.nz:(x + 1) * self.nz, :]

    def load(self, run, comp, x, turn_y):
        cosine, sine = turn_y
        packed = self.edge(x)
        parts = [[self.own(run, part, comp, x, t) for t in range(self.tiles)] for part in range(2)]
        edges = [unpack_edge(packed, spot_of(run, part, comp)) for part in range(2)]
        edges = turn(edges[0], edges[1], cosine, sine if run == 0 else -sine)
        return [parts[part] + [edges[part]] for part in range(2)]

    def eps(self, x):
        own = [inverse_eps(self.material_ref[self.rows(x, t), :], self.table_ref) for t in range(self.tiles)]
        return own + [inverse_eps(unpack_edge(self.edge(x), 24), self.table_ref)]

    def hits(self, run, x):
        total_x = self.width_x * lax.axis_size("gx")
        width_y = self.tiles * LANES
        total_y = width_y * lax.axis_size("gy")
        begin_y = lax.axis_index("gy") * width_y
        plane = self.shifts.row * total_x + lax.axis_index("gx") * self.width_x + x
        masks = []
        for t in range(self.tiles + 1):
            lane = self.shifts.lane
            if t < self.tiles:
                column = begin_y + t * LANES + lane
            else:
                column = begin_y + jnp.where(lane < LANES // 2, lane + width_y, lane - LANES)
                column = jnp.where(column < 0, column + total_y, column)
                column = jnp.where(column >= total_y, column - total_y, column)
            masks.append(plane * total_y + column == self.cells_ref[run])
        return masks

    def source(self, run, step, masks, turn_y):
        cosine, sine = turn_y
        amplitude = [self.wave_ref[(run * 2 + part) * 2 + step] for part in range(2)]
        turned = turn(amplitude[0], amplitude[1], cosine, sine if run == 0 else -sine)
        return [
            [jnp.where(mask, amplitude[part] if t < self.tiles else turned[part], 0.0) for t, mask in enumerate(masks)]
            for part in range(2)
        ]


def face_kernel(dims, field_ref, material_ref, face_ref, planes_ref, layer_ref, sems):
    nz, width_x, tiles = dims
    copies = [
        pltpu.make_async_copy(field_ref.at[pl.ds(6 * pair + 1, 2)], planes_ref.at[pair], sems.at[pair])
        for pair in range(4)
    ]
    copies.append(pltpu.make_async_copy(material_ref, layer_ref, sems.at[4]))
    for copy in copies:
        copy.start()
    for pair in range(4):
        copies[pair].wait()
        for which in range(2):
            for t in range(tiles):
                at = ((pair * 2 + which) * tiles + t) * nz
                face_ref[at:at + nz, :] = planes_ref[pair, which, pl.ds(t * width_x, nz, stride=tiles * width_x), :]
    copies[4].wait()
    for t in range(tiles):
        at = (8 * tiles + t) * nz
        face_ref[at:at + nz, :] = layer_ref[pl.ds(t * width_x, nz, stride=tiles * width_x), :].astype(jnp.float32)


def edge_kernel(dims, field_ref, material_ref, edge_ref):
    nz, width_x, tiles = dims
    local = Local(dims, field_ref, None, None, material_ref, None, None)
    lane = lane_iota(nz)
    for x in range(width_x):
        values = []
        for run in range(2):
            for part in range(2):
                for comp in range(6):
                    values.append(
                        jnp.where(
                            lane < LANES // 2,
                            local.own(run, part, comp, x, 0),
                            local.own(run, part, comp, x, tiles - 1),
                        )
                    )
        material = jnp.where(
            lane < LANES // 2, material_ref[local.rows(x, 0), :], material_ref[local.rows(x, tiles - 1), :]
        )
        values.append(material.astype(jnp.float32))
        edge_ref[x * nz:(x + 1) * nz, :] = pack_edges(values, lane)


def merged_edges(below_ref, above_ref, edge_ref):
    if above_ref is None:
        return below_ref
    lane = lax.broadcasted_iota(jnp.int32, below_ref.shape, 1)
    edge_ref[...] = jnp.where(lane % EDGE < 2, below_ref[...], above_ref[...])
    return edge_ref


def small_steps(local, ex, ey, ez, hx, hy, hz, ey_x, ez_x):
    shifts = local.shifts
    every = range(len(ex))
    ez_y, ex_y = shifts.y_up(ez), shifts.y_up(ex)
    new_x = None
    if hx is not None:
        new_x = [hx[t] - COURANT * (ez_y[t] - ez[t] - (shifts.z_up(ey[t]) - ey[t])) for t in every]
    diff_z = [-ez[t] if ez_x is None else ez_x[t] - ez[t] for t in every]
    diff_y = [-ey[t] if ey_x is None else ey_x[t] - ey[t] for t in every]
    new_y = [hy[t] - COURANT * (shifts.z_up(ex[t]) - ex[t] - diff_z[t]) for t in every]
    new_z = [hz[t] - COURANT * (diff_y[t] - (ex_y[t] - ex[t])) for t in every]
    return new_x, new_y, new_z


def grown(local, ex, ey, ez, hx, hy, hz, hy_x, hz_x, half, source, count):
    shifts = local.shifts
    hz_y, hx_y = shifts.y_down(hz), shifts.y_down(hx)
    new_x, new_y, new_z = [], [], []
    for t in range(count):
        diff_y = hz[t] if hz_x is None else hz[t] - hz_x[t]
        diff_z = hy[t] if hy_x is None else hy[t] - hy_x[t]
        if ex is not None:
            new_x.append(ex[t] + half[t] * (hz[t] - hz_y[t] - (hy[t] - shifts.z_down(hy[t]))))
        new_y.append(ey[t] + half[t] * (hx[t] - shifts.z_down(hx[t]) - diff_y))
        new_z.append(ez[t] + half[t] * (diff_z - (hx[t] - hx_y[t])) + source[t])
    return new_x, new_y, new_z


def started(dims, two, field_ref, material_ref, table_ref, phase_ref, cells_ref, wave_ref, below_ref, above_ref, edge_ref):
    edges = merged_edges(below_ref, None if two else above_ref, edge_ref)
    local = Local(dims, field_ref, edges, table_ref, material_ref, cells_ref, wave_ref)
    cosine_x, sine_x, cosine_y, sine_y = phases(phase_ref)
    first = lax.axis_index("gx") == 0
    last = lax.axis_index("gx") == lax.axis_size("gx") - 1
    ahead = (jnp.where(last, cosine_x, 1.0), jnp.where(last, sine_x, 0.0))
    back = (jnp.where(first, cosine_x, 1.0), jnp.where(first, -sine_x, 0.0))
    return local, y_turn(cosine_y, sine_y, local.shifts.lane), ahead, back


def store_tiles(ref, unit, values, tiles, nz):
    for t in range(tiles):
        at = (unit * tiles + t) * nz
        ref[at:at + nz, :] = values[t]


def lower_kernel(dims, two, *refs):
    nz, _, tiles = dims
    *given, down_ref, edge_ref = refs
    local, turn_y, _, _ = started(dims, two, *given, edge_ref)
    half = [COURANT * value for value in local.eps(0)]
    edges = [None] * 17
    for run in range(2):
        low = [local.load(run, comp, 0, turn_y) for comp in range(6)]
        nearer = [local.load(run, comp, 1, turn_y) for comp in (1, 2)]
        source = local.source(run, 0, local.hits(run, 0), turn_y)
        for part in range(2):
            ex, ey, ez, hx, hy, hz = [low[comp][part] for comp in range(6)]
            hx, hy, hz = small_steps(local, ex, ey, ez, hx, hy, hz, nearer[0][part], nearer[1][part])
            _, new_y, new_z = grown(local, None, ey, ez, hx, hy, hz, None, None, half, source[part], tiles + 1)
            for which, value, initial in ((0, new_y, ey), (1, new_z, ez)):
                unit = (run * 2 + part) * 2 + which
                store_tiles(down_ref, unit, value, tiles, nz)
                edges[unit] = initial[tiles]
                edges[8 + unit] = value[tiles]
    edges[16] = unpack_edge(local.edge(0), 24)
    at = 8 * tiles * nz
    down_ref[at:at + nz, :] = pack_edges(edges, local.shifts.lane)


def upper_kernel(dims, two, *refs):
    nz, width_x, tiles = dims
    *given, up_ref, edge_ref = refs
    local, turn_y, _, _ = started(dims, two, *given, edge_ref)
    edges = []
    for run in range(2):
        high = [local.load(run, comp, width_x - 1, turn_y) for comp in (0, 1, 2, 4, 5)]
        for part in range(2):
            ex, ey, ez, hy, hz = [values[part] for values in high]
            _, hy, hz = small_steps(local, ex, ey, ez, None, hy, hz, None, None)
            for which, value in ((0, hy), (1, hz)):
                store_tiles(up_ref, (run * 2 + part) * 2 + which, value, tiles, nz)
                edges.append(value[tiles])
    at = 8 * tiles * nz
    up_ref[at:at + nz, :] = pack_edges(edges, local.shifts.lane)


def halo(dims, ref, edge, first_spot, run, which, angle):
    nz, _, tiles = dims
    cosine, sine = angle
    units = [(run * 2 + part) * 2 + which for part in range(2)]
    values = [
        [ref[(unit * tiles + t) * nz:(unit * tiles + t + 1) * nz, :] for t in range(tiles)]
        + [unpack_edge(edge, first_spot + unit)]
        for unit in units
    ]
    signed = sine if run == 0 else -sine
    turned = [turn(values[0][t], values[1][t], cosine, signed) for t in range(tiles + 1)]
    return [[value[part] for value in turned] for part in range(2)]


def eps_above(local, face_ref, edge):
    nz, tiles = local.nz, local.tiles
    own = [face_ref[(8 * tiles + t) * nz:(8 * tiles + t + 1) * nz, :] for t in range(tiles)]
    return [inverse_eps(value, local.table_ref) for value in own + [unpack_edge(edge, 16)]]


def share_kernel(dims, two, *refs):
    nz, width_x, tiles = dims
    *given, face_ref, down_ref, share_ref, edge_ref = refs
    local, turn_y, ahead, _ = started(dims, two, *given, edge_ref)
    edge = down_ref[8 * tiles * nz:(8 * tiles + 1) * nz, :]
    half = [COURANT * value for value in local.eps(width_x - 1)]
    half_above = [COURANT * value for value in eps_above(local, face_ref, edge)]
    kept_e, kept_h = {}, {}
    every = range(tiles + 1)
    for run in range(2):
        low = [local.load(run, comp, width_x - 2, turn_y) for comp in range(6)]
        high = [local.load(run, comp, width_x - 1, turn_y) for comp in range(6)]
        source = local.source(run, 0, local.hits(run, width_x - 1), turn_y)
        early = [halo(dims, face_ref, edge, 0, run, which, ahead) for which in range(2)]
        later = [halo(dims, down_ref, edge, 8, run, which, ahead) for which in range(2)]
        for part in range(2):
            ex, ey, ez, hx, hy, hz = [high[comp][part] for comp in range(6)]
            low_x, low_y, low_z, _, low_hy, low_hz = [low[comp][part] for comp in range(6)]
            _, low_hy, low_hz = small_steps(local, low_x, low_y, low_z, None, low_hy, low_hz, ey, ez)
            hx, hy, hz = small_steps(local, ex, ey, ez, hx, hy, hz, early[0][part], early[1][part])
            ex, ey, ez = grown(local, ex, ey, ez, hx, hy, hz, low_hy, low_hz, half, source[part], tiles + 1)
            above_y = [later[0][part][t] + half_above[t] * hz[t] for t in every]
            above_z = [later[1][part][t] - half_above[t] * hy[t] for t in every]
            _, hy, hz = small_steps(local, ex, ey, ez, None, hy, hz, above_y, above_z)
            kept_e[run, part] = (above_y, above_z)
            kept_h[run, part] = (hy, hz)
    for t in range(tiles):
        total = 0.0
        for run in range(2):
            for which, sign in ((0, 1.0), (1, -1.0)):
                term = (
                    kept_e[run, 0][which][t] * kept_h[1 - run, 0][1 - which][t]
                    - kept_e[run, 1][which][t] * kept_h[1 - run, 1][1 - which][t]
                )
                total = total + sign * term
        share_ref[t * nz:(t + 1) * nz, :] = half_above[t] * total


def steps_kernel(dims, two, *refs):
    nz, width_x, tiles = dims
    *given, face_ref, down_ref, up_ref, share_ref, cross_ref, edge_ref = refs
    local, turn_y, ahead, back = started(dims, two, *given, edge_ref)
    every, own, layers = range(tiles + 1), range(tiles), range(width_x)
    down_edge = down_ref[8 * tiles * nz:(8 * tiles + 1) * nz, :]
    up_edge = up_ref[8 * tiles * nz:(8 * tiles + 1) * nz, :]
    half = [[COURANT * value for value in local.eps(x)] for x in layers]
    half_above = [COURANT * value for value in eps_above(local, face_ref, down_edge)]
    kept_one, kept_two = {}, {}
    for run in range(2):
        masks = [local.hits(run, x) for x in layers]
        sources = [[local.source(run, step, masks[x], turn_y) for x in layers] for step in range(2)]
        fields = [[local.load(run, comp, x, turn_y) for x in layers] for comp in range(6)]
        early = [halo(dims, face_ref, down_edge, 0, run, which, ahead) for which in range(2)]
        later = [halo(dims, down_ref, down_edge, 8, run, which, ahead) for which in range(2)]
        under = [halo(dims, up_ref, up_edge, 0, run, which, back) for which in range(2)]
        for part in range(2):
            ex, ey, ez, hx, hy, hz = [[fields[comp][x][part] for x in layers] for comp in range(6)]
            under_y = [under[0][part][t] + COURANT * ez[0][t] for t in every]
            under_z = [under[1][part][t] - COURANT * ey[0][t] for t in every]
            above_y, above_z = early[0][part], early[1][part]
            for step in range(2):
                ey_x, ez_x = ey[1:] + [above_y], ez[1:] + [above_z]
                for x in layers:
                    hx[x], hy[x], hz[x] = small_steps(
                        local, ex[x], ey[x], ez[x], hx[x], hy[x], hz[x], ey_x[x], ez_x[x]
                    )
                if step == 0:
                    above_y = [later[0][part][t] + half_above[t] * hz[-1][t] for t in every]
                    above_z = [later[1][part][t] - half_above[t] * hy[-1][t] for t in every]
                else:
                    under_y, under_z = None, None
                for x in layers:
                    hy_x, hz_x = (under_y, under_z) if x == 0 else (hy[x - 1], hz[x - 1])
                    ex[x], ey[x], ez[x] = grown(
                        local, ex[x], ey[x], ez[x], hx[x], hy[x], hz[x], hy_x, hz_x, half[x], sources[step][x][part],
                        tiles if step else tiles + 1,
                    )
                (kept_two if step else kept_one)[run, part] = (list(ex), list(ey), list(ez))
    for t in own:
        for x in layers:
            total = share_ref[t * nz:(t + 1) * nz, :] if x == 0 else 0.0
            for comp in range(3):
                for now, later in ((kept_one, kept_two), (kept_two, kept_one)):
                    total = total + (
                        now[0, 0][comp][x][t] * later[1, 0][comp][x][t] - now[0, 1][comp][x][t] * later[1, 1][comp][x][t]
                    )
            cross_ref[local.rows(x, t), :] = -half[x][t] * total


def sum_kernel(own_ref, other_ref, out_ref):
    out_ref[...] = own_ref[...] + other_ref[...]


VMEM = pl.BlockSpec(memory_space=pltpu.VMEM)
SMEM = pl.BlockSpec(memory_space=pltpu.SMEM)


ANY = pl.BlockSpec(memory_space=pltpu.HBM)


def call(kernel, name, in_specs, rows, cost, scratch=()):
    return pl.pallas_call(
        kernel,
        name=name,
        out_shape=jax.ShapeDtypeStruct((rows, LANES), jnp.float32),
        in_specs=in_specs,
        out_specs=VMEM,
        scratch_shapes=list(scratch),
        compiler_params=pltpu.CompilerParams(vmem_limit_bytes=48 * 1024 * 1024),
        cost_estimate=pl.CostEstimate(flops=0, bytes_accessed=cost, transcendentals=0),
    )


def moved(value, axis, steps):
    count = lax.axis_size(axis)
    return lax.ppermute(value, axis, [(source, (source + steps) % count) for source in range(count)])


def local(field_state, material_map, eps_table, bloch_phase, source_cells, source_wave):
    nz, width_x, width_y = material_map.shape
    tiles = width_y // LANES
    dims = (nz, width_x, tiles)
    rows = nz * tiles * width_x
    fields = field_state.reshape(24, nz, width_x, tiles, LANES).transpose(0, 1, 3, 2, 4).reshape(24, rows, LANES)
    material = material_map.reshape(nz, width_x, tiles, LANES).transpose(0, 2, 1, 3).reshape(rows, LANES)
    cells = source_cells.reshape(2)
    wave = source_wave.reshape(8)
    unit = nz * tiles
    two = lax.axis_size("gy") == 2

    face = call(
        functools.partial(face_kernel, dims), "faces", [ANY, ANY], 9 * unit, 1_000_000,
        (
            pltpu.VMEM((4, 2, rows, LANES), jnp.float32),
            pltpu.VMEM((rows, LANES), jnp.int32),
            pltpu.SemaphoreType.DMA((5,)),
        ),
    )(fields, material)
    face = moved(face, "gx", -1)
    edge = call(functools.partial(edge_kernel, dims), "edges", [VMEM, VMEM], width_x * nz, 20_000_000)(fields, material)
    below = moved(edge, "gy", 1)
    above = below if two else moved(edge, "gy", -1)
    given = (fields, material, eps_table, bloch_phase, cells, wave, below, above)
    specs = [VMEM, VMEM, SMEM, SMEM, SMEM, SMEM, VMEM, VMEM]
    scratch = (pltpu.VMEM((width_x * nz, LANES), jnp.float32),)
    down = call(functools.partial(lower_kernel, dims, two), "lower", specs, 8 * unit + nz, 20_000_000, scratch)(*given)
    down = moved(down, "gx", -1)
    up = call(functools.partial(upper_kernel, dims, two), "upper", specs, 8 * unit + nz, 20_000_000, scratch)(*given)
    up = moved(up, "gx", 1)
    share = call(
        functools.partial(share_kernel, dims, two), "share", specs + [VMEM] * 2, unit, 20_000_000, scratch
    )(*given, face, down)
    share = moved(share, "gx", 1)
    cross = call(
        functools.partial(steps_kernel, dims, two), "steps", specs + [VMEM] * 4, rows, 20_000_000, scratch
    )(*given, face, down, up, share)
    other = moved(cross, "src", 1)
    out = call(sum_kernel, "gradient", [VMEM, VMEM], rows, 500_000)(cross, other)
    return out.reshape(nz, tiles, width_x, LANES).transpose(0, 2, 1, 3).reshape(nz, width_x, width_y)


def solution(mesh):
    return jax.shard_map(
        local,
        mesh=mesh,
        in_specs=(
            P(("design", "src"), None, None, None, None, "gx", "gy"),
            P("design", "gx", "gy"),
            P(),
            P("design"),
            P(("design", "src"), None),
            P(("design", "src"), None, None, None),
        ),
        out_specs=P("design", "gx", "gy"),
        check_vma=False,
    )
```

time: 42.5 us -> 35.8 us (0.84)
  starting transfers between devices: 13.2 us -> 8.92 us
  waiting for transfers between devices: 20 us -> 16.5 us
  Pallas kernels: 5.97 us -> 7.72 us
  local copies, waits for them, and re-layouts: 3.03 us -> 2.35 us
    ppermute x1 -> x0, waiting for transfers between devices: 3.94 us -> none  [local(): lax.ppermute(share, ('gx', 'src'), [(x * count_src + s, (x + 1) % count_x...]
    ppermute x6, starting transfers between devices: 12.7 us -> 8.92 us  [moved(): lax.ppermute(value, axis, [(source, (source + steps) % count) for source...]
    pallas_call x4 -> x7, Pallas kernels: 5.97 us -> 7.72 us  [the longest x1 2.47 us: local(): call(functools.partial(steps_kernel, dims, two), 'steps', specs + [VMEM]...]
    unnamed x18 -> x16, local copies, waits for them, and re-layouts: 2.94 us -> 2.27 us
    ppermute x1 -> x0, starting transfers between devices: 0.51 us -> none  [local(): lax.ppermute(share, ('gx', 'src'), [(x * count_src + s, (x + 1) % count_x...]
    ppermute x6, waiting for transfers between devices: 16 us -> 16.5 us  [moved(): lax.ppermute(value, axis, [(source, (source + steps) % count) for source...]
  transfers between devices with their start and end apart: 7 -> 6, of which waited for: 4 -> 5; matrix products, arithmetic and copies ran while one was open for 0% -> 0% of each run, Pallas kernels for 0% -> 12%
where the time goes in v2:
time: 35.8 us; the launch traced here: 35.6 us
  waiting for transfers between devices  16.5 us (46%)
  starting transfers between devices  8.92 us (25%)
  Pallas kernels  7.72 us (22%)
  local copies, waits for them, and re-layouts  2.35 us (7%)
    ppermute x6, waiting for transfers between devices, moved(): lax.ppermute(value, axis, [(source, (source + steps) % count) for source...  16.5 us
    ppermute x6, starting transfers between devices, moved(): lax.ppermute(value, axis, [(source, (source + steps) % count) for source...  8.92 us
    pallas_call x1, Pallas kernels, local(): call(functools.partial(steps_kernel, dims, two), 'steps', specs + [VMEM]...  2.47 us
    unnamed x16, local copies, waits for them, and re-layouts  2.27 us
    pallas_call x1, Pallas kernels, local(): call(functools.partial(share_kernel, dims, two), 'share', specs + [VMEM]...  1.44 us
    pallas_call x1, Pallas kernels, local(): call(functools.partial(lower_kernel, dims, two), 'lower', specs, 8 * unit...  1.24 us
    pallas_call x1, Pallas kernels, local(): call(functools.partial(upper_kernel, dims, two), 'upper', specs, 8 * unit...  0.86 us
    pallas_call x1, Pallas kernels, local(): call(functools.partial(face_kernel, dims), 'faces', [ANY, ANY], 9 * unit,...  0.8 us
  transfers between devices with their start and end apart: 6, of which 5 were waited for; matrix products, arithmetic and copies ran while one was open for 0% of the time, Pallas kernels for 12%

profile of v2, /device:TPU:0, one launch (start us, length us, event | category | flops | bytes accessed | tf_op | source)
XLA Modules:
  0.0 35.6 jit_solution(17417885112103189133)
XLA Ops:
  0.0 0.0 copy-start
  0.0 1.4 %copy-done = f32[1,2,2,6,32,2,256]{6,5,4,3,2,1,0:T(2,128)S(1)} copy-done((f32[1,2,2,6,32,2,256]{6,5,4,3,2,1,0:T(2,128)S(1)}, f32[1,2,2,6,32,2,256]{6,5,4,3,2,1,0:T(2,128)}, u32[]{:S(2)}) %copy-start) | copy-done | bytes 1572888
  1.4 0.0 copy-start.2
  1.4 0.8 %copy-done.2 = s32[32,2,256]{2,1,0:T(2,128)S(1)} copy-done((s32[32,2,256]{2,1,0:T(2,128)S(1)}, s32[32,2,256]{2,1,0:T(2,128)}, u32[]{:S(2)}) %copy-start.2) | copy-done | bytes 65560
  2.2 0.0 copy-start.7
  2.3 0.0 copy-start.1
  2.3 0.0 copy-start.3
  2.3 0.0 copy-start.4
  2.3 0.0 copy-start.5
  2.3 0.0 copy-start.6
  2.3 0.3 edges.1
  2.6 3.0 %collective-permute-start = (f32[64,128]{1,0:T(8,128)S(1)}, f32[64,128]{1,0:T(8,128)S(1)}, u32[]{:S(2)}, u32[]{:S(2)}) collective-permute-start(f32[64,128]{1,0:T(8,128)S(1)} %edges.1), channel_id=1, source_target_pairs={{0,2},{2,0},{1,3},{3,1},{4,6},{6,4},{5,7},{7,5},{8,10},{10,8},{9,1... | collective-permute-start | bytes 98312 | tf_op jit(solution)/shard_map/ppermute | solution.py:418
  5.6 0.8 %faces.1 = f32[576,128]{1,0:T(8,128)S(1)} custom-call(f32[24,128,128]{2,1,0:T(8,128)S(1)} %bitcast.17, s32[128,128]{1,0:T(8,128)S(1)} %bitcast.23), custom_call_target="tpu_custom_call" | custom-call | bytes 1000000 | tf_op jit(solution)/shard_map/faces/pallas_call | solution.py:433
  6.4 3.7 %collective-permute-start.1 = (f32[576,128]{1,0:T(8,128)S(1)}, f32[576,128]{1,0:T(8,128)S(1)}, u32[]{:S(2)}, u32[]{:S(2)}) collective-permute-start(f32[576,128]{1,0:T(8,128)S(1)} %faces.1), channel_id=1, source_target_pairs={{0,12},{4,0},{8,4},{12,8},{1,13},{5,1},{9,5},{13,9},{2,14},{6,2},{... | collective-permute-start | bytes 884744 | tf_op jit(solution)/shard_map/ppermute | solution.py:418
  10.0 0.0 copy-done.7
  10.0 0.1 reshape.29.refs_5_
  10.1 0.0 collective-permute-done.refs_6_.refs_7_
  10.1 0.0 copy-done.1
  10.1 0.0 copy-done.3
  10.1 0.0 copy-done.4
  10.1 0.0 copy-done.5
  10.1 0.0 copy-done.6
  10.1 1.2 %lower.1 = f32[544,128]{1,0:T(8,128)S(1)} custom-call(f32[24,128,128]{2,1,0:T(8,128)S(1)} %bitcast.18, s32[128,128]{1,0:T(8,128)S(1)} %bitcast.24, f32[8]{0:T(128)S(1)} %copy-done.4, f32[2]{0:T(128)S(1)} %copy-done.5, s32[2]{0:T(128)S(1)} %bitcast.28, f32[8]{0:T(128)S(1)} %reshape.29.refs_5_, f32[64,128]{1,0:T(8,128)S(1)} %collective-permute-done.refs_6_.refs_7_, ...), custom_call_target="tpu_custom_call" | custom-call | bytes 20000000 | tf_op jit(solution)/shard_map/lower/pallas_call | solution.py:448
  11.4 1.5 %collective-permute-start.2 = (f32[544,128]{1,0:T(8,128)S(1)}, f32[544,128]{1,0:T(8,128)S(1)}, u32[]{:S(2)}, u32[]{:S(2)}) collective-permute-start(f32[544,128]{1,0:T(8,128)S(1)} %lower.1), channel_id=1, source_target_pairs={{0,12},{4,0},{8,4},{12,8},{1,13},{5,1},{9,5},{13,9},{2,14},{6,2},{... | collective-permute-start | bytes 835592 | tf_op jit(solution)/shard_map/ppermute | solution.py:418
  12.9 0.9 %upper.1 = f32[544,128]{1,0:T(8,128)S(1)} custom-call(f32[24,128,128]{2,1,0:T(8,128)S(1)} %bitcast.19, s32[128,128]{1,0:T(8,128)S(1)} %bitcast.25, f32[8]{0:T(128)S(1)} %copy-done.4, f32[2]{0:T(128)S(1)} %copy-done.5, s32[2]{0:T(128)S(1)} %bitcast.29, f32[8]{0:T(128)S(1)} %reshape.29.refs_5_, f32[64,128]{1,0:T(8,128)S(1)} %collective-permute-done.refs_6_.refs_7_, ...), custom_call_target="tpu_custom_call" | custom-call | bytes 20000000 | tf_op jit(solution)/shard_map/upper/pallas_call | solution.py:450
  13.8 0.6 %collective-permute-start.3 = (f32[544,128]{1,0:T(8,128)S(1)}, f32[544,128]{1,0:T(8,128)S(1)}, u32[]{:S(2)}, u32[]{:S(2)}) collective-permute-start(f32[544,128]{1,0:T(8,128)S(1)} %upper.1), channel_id=1, source_target_pairs={{0,4},{4,8},{8,12},{12,0},{1,5},{5,9},{9,13},{13,1},{2,6},{6,10},{... | collective-permute-start | bytes 835592 | tf_op jit(solution)/shard_map/ppermute | solution.py:418
  14.4 3.1 %collective-permute-done.1.refs_8_ = f32[576,128]{1,0:T(8,128)S(1)} collective-permute-done((f32[576,128]{1,0:T(8,128)S(1)}, f32[576,128]{1,0:T(8,128)S(1)}, u32[]{:S(2)}, u32[]{:S(2)}) %collective-permute-start.1) | collective-permute-done | bytes 294944 | tf_op jit(solution)/shard_map/ppermute | solution.py:418
  17.5 6.0 %collective-permute-done.2.refs_9_ = f32[544,128]{1,0:T(8,128)S(1)} collective-permute-done((f32[544,128]{1,0:T(8,128)S(1)}, f32[544,128]{1,0:T(8,128)S(1)}, u32[]{:S(2)}, u32[]{:S(2)}) %collective-permute-start.2) | collective-permute-done | bytes 278560 | tf_op jit(solution)/shard_map/ppermute | solution.py:418
  23.5 1.4 %share.1 = f32[64,128]{1,0:T(8,128)S(1)} custom-call(f32[24,128,128]{2,1,0:T(8,128)S(1)} %bitcast.20, s32[128,128]{1,0:T(8,128)S(1)} %bitcast.26, f32[8]{0:T(128)S(1)} %copy-done.4, f32[2]{0:T(128)S(1)} %copy-done.5, s32[2]{0:T(128)S(1)} %bitcast.30, f32[8]{0:T(128)S(1)} %reshape.29.refs_5_, f32[64,128]{1,0:T(8,128)S(1)} %collective-permute-done.refs_6_.refs_7_, ...), custom_call_target="tpu_custom_call" | custom-call | bytes 20000000 | tf_op jit(solution)/shard_map/share/pallas_call | solution.py:452
  24.9 0.1 collective-permute-start.4
  25.0 4.2 %collective-permute-done.3.refs_10_ = f32[544,128]{1,0:T(8,128)S(1)} collective-permute-done((f32[544,128]{1,0:T(8,128)S(1)}, f32[544,128]{1,0:T(8,128)S(1)}, u32[]{:S(2)}, u32[]{:S(2)}) %collective-permute-start.3) | collective-permute-done | bytes 278560 | tf_op jit(solution)/shard_map/ppermute | solution.py:418
  29.2 2.0 %collective-permute-done.4.refs_11_ = f32[64,128]{1,0:T(8,128)S(1)} collective-permute-done((f32[64,128]{1,0:T(8,128)S(1)}, f32[64,128]{1,0:T(8,128)S(1)}, u32[]{:S(2)}, u32[]{:S(2)}) %collective-permute-start.4) | collective-permute-done | bytes 32800 | tf_op jit(solution)/shard_map/ppermute | solution.py:418
  31.2 2.5 %steps.1.own_ref = f32[128,128]{1,0:T(8,128)S(1)} custom-call(f32[24,128,128]{2,1,0:T(8,128)S(1)} %bitcast.21, s32[128,128]{1,0:T(8,128)S(1)} %bitcast.27, f32[8]{0:T(128)S(1)} %copy-done.4, f32[2]{0:T(128)S(1)} %copy-done.5, s32[2]{0:T(128)S(1)} %bitcast.31, f32[8]{0:T(128)S(1)} %reshape.29.refs_5_, f32[64,128]{1,0:T(8,128)S(1)} %collective-permute-done.refs_6_.refs_7_, ...), custom_call_target="tpu_custom_call" | custom-call | bytes 20000000 | tf_op jit(solution)/shard_map/steps/pallas_call | solution.py:456
  33.6 0.1 collective-permute-start.5
  33.7 1.2 %collective-permute-done.5.other_ref = f32[128,128]{1,0:T(8,128)S(1)} collective-permute-done((f32[128,128]{1,0:T(8,128)S(1)}, f32[128,128]{1,0:T(8,128)S(1)}, u32[]{:S(2)}, u32[]{:S(2)}) %collective-permute-start.5) | collective-permute-done | bytes 65568 | tf_op jit(solution)/shard_map/ppermute | solution.py:418
  35.0 0.6 %gradient.1 = f32[128,128]{1,0:T(8,128)} custom-call(f32[128,128]{1,0:T(8,128)S(1)} %steps.1.own_ref, f32[128,128]{1,0:T(8,128)S(1)} %collective-permute-done.5.other_ref), custom_call_target="tpu_custom_call" | custom-call | bytes 500000 | tf_op jit(solution)/shard_map/gradient/pallas_call | solution.py:460
Async XLA Ops:
  0.0 1.4 %copy-start = (f32[1,2,2,6,32,2,256]{6,5,4,3,2,1,0:T(2,128)S(1)}, f32[1,2,2,6,32,2,256]{6,5,4,3,2,1,0:T(2,128)}, u32[]{:S(2)}) copy-start(f32[1,2,2,6,32,2,256]{6,5,4,3,2,1,0:T(2,128)} %param.6) | copy-start | bytes 4718596
  1.4 0.8 %copy-start.2 = (s32[32,2,256]{2,1,0:T(2,128)S(1)}, s32[32,2,256]{2,1,0:T(2,128)}, u32[]{:S(2)}) copy-start(s32[32,2,256]{2,1,0:T(2,128)} %param.7) | copy-start | bytes 196612
  2.2 7.8 %copy-start.7 = (f32[1,2,2,2]{3,2,1,0:T(2,128)S(1)}, f32[1,2,2,2]{3,2,1,0:T(2,128)}, u32[]{:S(2)}) copy-start(f32[1,2,2,2]{3,2,1,0:T(2,128)} %param.11) | copy-start | bytes 100
  2.3 7.9 %copy-start.1 = (f32[1,2,2,6,32,2,256]{6,5,4,3,2,1,0:T(2,128)S(1)}, f32[1,2,2,6,32,2,256]{6,5,4,3,2,1,0:T(2,128)}, u32[]{:S(2)}) copy-start(f32[1,2,2,6,32,2,256]{6,5,4,3,2,1,0:T(2,128)} %param.6) | copy-start | bytes 4718596
  2.3 7.9 %copy-start.3 = (s32[32,2,256]{2,1,0:T(2,128)S(1)}, s32[32,2,256]{2,1,0:T(2,128)}, u32[]{:S(2)}) copy-start(s32[32,2,256]{2,1,0:T(2,128)} %param.7) | copy-start | bytes 196612
  2.3 7.9 %copy-start.4 = (f32[8]{0:T(128)S(1)}, f32[8]{0:T(128)}, u32[]{:S(2)}) copy-start(f32[8]{0:T(128)} %refs_2_.7) | copy-start | bytes 100
  2.3 7.9 %copy-start.5 = (f32[2]{0:T(128)S(1)}, f32[2]{0:T(128)}, u32[]{:S(2)}) copy-start(f32[2]{0:T(128)} %refs_3_.7) | copy-start | bytes 28
  2.3 7.9 %copy-start.6 = (s32[1,2]{1,0:T(1,128)S(1)}, s32[1,2]{1,0:T(1,128)}, u32[]{:S(2)}) copy-start(s32[1,2]{1,0:T(1,128)} %param.10) | copy-start | bytes 28
  2.6 7.6 %collective-permute-start = (f32[64,128]{1,0:T(8,128)S(1)}, f32[64,128]{1,0:T(8,128)S(1)}, u32[]{:S(2)}, u32[]{:S(2)}) collective-permute-start(f32[64,128]{1,0:T(8,128)S(1)} %edges.1), channel_id=1, source_target_pairs={{0,2},{2,0},{1,3},{3,1},{4,6},{6,4},{5,7},{7,5},{8,10},{10,8},{9,1... | collective-permute-start | bytes 98312 | tf_op jit(solution)/shard_map/ppermute | solution.py:418
  6.4 11.1 %collective-permute-start.1 = (f32[576,128]{1,0:T(8,128)S(1)}, f32[576,128]{1,0:T(8,128)S(1)}, u32[]{:S(2)}, u32[]{:S(2)}) collective-permute-start(f32[576,128]{1,0:T(8,128)S(1)} %faces.1), channel_id=1, source_target_pairs={{0,12},{4,0},{8,4},{12,8},{1,13},{5,1},{9,5},{13,9},{2,14},{6,2},{... | collective-permute-start | bytes 884744 | tf_op jit(solution)/shard_map/ppermute | solution.py:418
  11.4 12.1 %collective-permute-start.2 = (f32[544,128]{1,0:T(8,128)S(1)}, f32[544,128]{1,0:T(8,128)S(1)}, u32[]{:S(2)}, u32[]{:S(2)}) collective-permute-start(f32[544,128]{1,0:T(8,128)S(1)} %lower.1), channel_id=1, source_target_pairs={{0,12},{4,0},{8,4},{12,8},{1,13},{5,1},{9,5},{13,9},{2,14},{6,2},{... | collective-permute-start | bytes 835592 | tf_op jit(solution)/shard_map/ppermute | solution.py:418
  13.8 15.4 %collective-permute-start.3 = (f32[544,128]{1,0:T(8,128)S(1)}, f32[544,128]{1,0:T(8,128)S(1)}, u32[]{:S(2)}, u32[]{:S(2)}) collective-permute-start(f32[544,128]{1,0:T(8,128)S(1)} %upper.1), channel_id=1, source_target_pairs={{0,4},{4,8},{8,12},{12,0},{1,5},{5,9},{9,13},{13,1},{2,6},{6,10},{... | collective-permute-start | bytes 835592 | tf_op jit(solution)/shard_map/ppermute | solution.py:418
  24.9 6.2 %collective-permute-start.4 = (f32[64,128]{1,0:T(8,128)S(1)}, f32[64,128]{1,0:T(8,128)S(1)}, u32[]{:S(2)}, u32[]{:S(2)}) collective-permute-start(f32[64,128]{1,0:T(8,128)S(1)} %share.1), channel_id=1, source_target_pairs={{0,4},{4,8},{8,12},{12,0},{1,5},{5,9},{9,13},{13,1},{2,6},{6,10},{... | collective-permute-start | bytes 98312 | tf_op jit(solution)/shard_map/ppermute | solution.py:418
  33.6 1.3 %collective-permute-start.5 = (f32[128,128]{1,0:T(8,128)S(1)}, f32[128,128]{1,0:T(8,128)S(1)}, u32[]{:S(2)}, u32[]{:S(2)}) collective-permute-start(f32[128,128]{1,0:T(8,128)S(1)} %steps.1.own_ref), channel_id=1, source_target_pairs={{0,1},{1,0},{2,3},{3,2},{4,5},{5,4},{6,7},{7,6},{8,9},{9,8},{10,11... | collective-permute-start | bytes 196616 | tf_op jit(solution)/shard_map/ppermute | solution.py:418

commit v3 on v2

v3 whole, which is shorter than its diff:
```python
import functools

import jax
import jax.numpy as jnp
from jax import lax
from jax.experimental import pallas as pl
from jax.experimental.pallas import tpu as pltpu
from jax.sharding import PartitionSpec as P

COURANT = 0.5
LANES = 128
EDGE = 4


def lane_iota(nz):
    return lax.broadcasted_iota(jnp.int32, (nz, LANES), 1)


def row_iota(nz):
    return lax.broadcasted_iota(jnp.int32, (nz, LANES), 0)


def pack_edges(values, lane):
    packed = jnp.zeros_like(values[0])
    for spot, value in enumerate(values):
        moved = pltpu.roll(value, EDGE * spot + 2, 1)
        packed = jnp.where(lane // EDGE == spot, moved, packed)
    return packed


def unpack_edge(packed, spot):
    return pltpu.roll(packed, LANES - EDGE * spot - 2, 1)


class Shifts:
    def __init__(self, nz):
        self.nz = nz
        self.row = row_iota(nz)
        self.lane = lane_iota(nz)

    def z_up(self, value):
        return jnp.where(self.row == self.nz - 1, 0.0, pltpu.roll(value, self.nz - 1, 0))

    def z_down(self, value):
        return jnp.where(self.row == 0, 0.0, pltpu.roll(value, 1, 0))

    def y_up(self, tiles):
        moved = [pltpu.roll(value, LANES - 1, 1) for value in tiles]
        count = len(tiles)
        return [jnp.where(self.lane == LANES - 1, moved[(t + 1) % count], moved[t]) for t in range(count)]

    def y_down(self, tiles):
        moved = [pltpu.roll(value, 1, 1) for value in tiles]
        count = len(tiles)
        return [jnp.where(self.lane == 0, moved[(t - 1) % count], moved[t]) for t in range(count)]


def turn(real_part, imag_part, cosine, sine):
    return real_part * cosine - imag_part * sine, real_part * sine + imag_part * cosine


def inverse_eps(material, levels):
    level = levels[0]
    for index in range(1, len(levels)):
        level = jnp.where(material == index, levels[index], level)
    return 1.0 / level


AHEAD, BACK, EDGES, WAVE, TURNED, LEVELS = 0, 2, 4, 8, 16, 24


def spot_of(run, part, comp):
    return (run * 2 + part) * 6 + comp


class Local:
    def __init__(self, dims, field_ref, edge_ref, small_ref, half_ref, mask_ref):
        self.nz, self.width_x, self.tiles = dims
        self.field_ref, self.edge_ref = field_ref, edge_ref
        self.small_ref, self.half_ref, self.mask_ref = small_ref, half_ref, mask_ref
        self.shifts = Shifts(self.nz)

    def rows(self, x, t):
        return pl.ds(t * self.width_x + x, self.nz, stride=self.tiles * self.width_x)

    def own(self, run, part, comp, x, t):
        return self.field_ref[spot_of(run, part, comp), self.rows(x, t), :]

    def edge(self, x):
        return self.edge_ref[x * self.nz:(x + 1) * self.nz, :]

    def small(self, row):
        return self.small_ref[row:row + 1, :]

    def angle(self, row, run):
        sine = self.small(row + 1)
        return self.small(row), sine if run == 0 else -sine

    def levels(self):
        return [self.small(row) for row in range(LEVELS, self.small_ref.shape[0])]

    def load(self, run, comp, x):
        packed = self.edge(x)
        parts = [[self.own(run, part, comp, x, t) for t in range(self.tiles)] for part in range(2)]
        edges = [unpack_edge(packed, spot_of(run, part, comp)) for part in range(2)]
        edges = turn(edges[0], edges[1], *self.angle(EDGES, run))
        return [parts[part] + [edges[part]] for part in range(2)]

    def half(self, x):
        starts = [(x * self.tiles + t) * self.nz for t in range(self.tiles)]
        own = [self.half_ref[at:at + self.nz, :] for at in starts]
        return own + [COURANT * inverse_eps(unpack_edge(self.edge(x), 24), self.levels())]

    def source(self, run, step, x):
        parts = []
        for part in range(2):
            values = []
            for t in range(self.tiles + 1):
                at = ((run * self.width_x + x) * (self.tiles + 1) + t) * self.nz
                row = (WAVE if t < self.tiles else TURNED) + (run * 2 + part) * 2 + step
                values.append(self.mask_ref[at:at + self.nz, :] * self.small(row))
            parts.append(values)
        return parts


def face_kernel(dims, field_hbm, face_ref, planes_ref, sems):
    nz, width_x, tiles = dims
    copies = [
        pltpu.make_async_copy(field_hbm.at[pl.ds(6 * pair + 1, 2)], planes_ref.at[pair], sems.at[pair])
        for pair in range(4)
    ]
    for copy in copies:
        copy.start()
    for pair in range(4):
        copies[pair].wait()
        for which in range(2):
            values = [planes_ref[pair, which, pl.ds(t * width_x, nz, stride=tiles * width_x), :] for t in range(tiles)]
            store_tiles(face_ref, pair * 2 + which, values, tiles, nz)


def edge_kernel(dims, order_ref, field_ref, material_ref, edge_ref):
    nz, width_x, tiles = dims
    local = Local(dims, field_ref, None, None, None, None)
    lane = lane_iota(nz)
    for x in range(width_x):
        values = []
        for run in range(2):
            for part in range(2):
                for comp in range(6):
                    values.append(
                        jnp.where(
                            lane < LANES // 2,
                            local.own(run, part, comp, x, 0),
                            local.own(run, part, comp, x, tiles - 1),
                        )
                    )
        material = jnp.where(
            lane < LANES // 2, material_ref[local.rows(x, 0), :], material_ref[local.rows(x, tiles - 1), :]
        )
        values.append(material.astype(jnp.float32))
        edge_ref[x * nz:(x + 1) * nz, :] = pack_edges(values, lane)


def prepare_kernel(
    dims, order_ref, material_ref, table_ref, phase_ref, cells_ref, wave_ref, small_ref, half_ref, mask_ref,
):
    nz, width_x, tiles = dims
    row = lax.broadcasted_iota(jnp.int32, (8, LANES), 0)
    angle = jnp.where(row == 0, phase_ref[0], phase_ref[1])
    cosine, sine = jnp.cos(angle), jnp.sin(angle)
    cosine_x, sine_x, cosine_y, sine_y = cosine[0:1], sine[0:1], cosine[1:2], sine[1:2]
    first_x, first_y = lax.axis_index("gx") == 0, lax.axis_index("gy") == 0
    last_x = lax.axis_index("gx") == lax.axis_size("gx") - 1
    last_y = lax.axis_index("gy") == lax.axis_size("gy") - 1
    small_ref[AHEAD:AHEAD + 1, :] = jnp.where(last_x, cosine_x, 1.0)
    small_ref[AHEAD + 1:AHEAD + 2, :] = jnp.where(last_x, sine_x, 0.0)
    small_ref[BACK:BACK + 1, :] = jnp.where(first_x, cosine_x, 1.0)
    small_ref[BACK + 1:BACK + 2, :] = jnp.where(first_x, -sine_x, 0.0)
    upper = lax.broadcasted_iota(jnp.int32, (1, LANES), 1) < LANES // 2
    cosine = jnp.where(upper, jnp.where(last_y, cosine_y, 1.0), jnp.where(first_y, cosine_y, 1.0))
    sine = jnp.where(upper, jnp.where(last_y, sine_y, 0.0), jnp.where(first_y, -sine_y, 0.0))
    small_ref[EDGES:EDGES + 1, :] = cosine
    small_ref[EDGES + 1:EDGES + 2, :] = sine
    small_ref[EDGES + 2:WAVE, :] = jnp.zeros((WAVE - EDGES - 2, LANES), jnp.float32)
    for run in range(2):
        for step in range(2):
            spots = [(run * 2 + part) * 2 + step for part in range(2)]
            amplitude = [wave_ref[0, run, part, step] for part in range(2)]
            turned = turn(amplitude[0], amplitude[1], cosine, sine if run == 0 else -sine)
            for part in range(2):
                row = WAVE + spots[part]
                small_ref[row:row + 1, :] = jnp.full((1, LANES), amplitude[part], jnp.float32)
                row = TURNED + spots[part]
                small_ref[row:row + 1, :] = turned[part]
    for index in range(table_ref.shape[0]):
        small_ref[LEVELS + index:LEVELS + index + 1, :] = jnp.full((1, LANES), table_ref[index], jnp.float32)
    levels = [table_ref[index] for index in range(table_ref.shape[0])]
    total_x = width_x * lax.axis_size("gx")
    width_y = tiles * LANES
    total_y = width_y * lax.axis_size("gy")
    begin_y = lax.axis_index("gy") * width_y
    z, lane = row_iota(nz), lane_iota(nz)
    for x in range(width_x):
        plane = z * total_x + lax.axis_index("gx") * width_x + x
        for t in range(tiles + 1):
            if t < tiles:
                column = begin_y + t * LANES + lane
                material = material_ref[pl.ds(t * width_x + x, nz, stride=tiles * width_x), :]
                at = (x * tiles + t) * nz
                half_ref[at:at + nz, :] = COURANT * inverse_eps(material, levels)
            else:
                column = begin_y + jnp.where(lane < LANES // 2, lane + width_y, lane - LANES)
                column = jnp.where(column < 0, column + total_y, column)
                column = jnp.where(column >= total_y, column - total_y, column)
            index = plane * total_y + column
            for run in range(2):
                at = ((run * width_x + x) * (tiles + 1) + t) * nz
                mask_ref[at:at + nz, :] = jnp.where(index == cells_ref[0, run], 1.0, 0.0)


def merged_edges(below_ref, above_ref, edge_ref):
    if above_ref is None:
        return below_ref
    lane = lax.broadcasted_iota(jnp.int32, below_ref.shape, 1)
    edge_ref[...] = jnp.where(lane % EDGE < 2, below_ref[...], above_ref[...])
    return edge_ref


def small_steps(local, ex, ey, ez, hx, hy, hz, ey_x, ez_x):
    shifts = local.shifts
    every = range(len(ex))
    ez_y, ex_y = shifts.y_up(ez), shifts.y_up(ex)
    new_x = None
    if hx is not None:
        new_x = [hx[t] - COURANT * (ez_y[t] - ez[t] - (shifts.z_up(ey[t]) - ey[t])) for t in every]
    diff_z = [-ez[t] if ez_x is None else ez_x[t] - ez[t] for t in every]
    diff_y = [-ey[t] if ey_x is None else ey_x[t] - ey[t] for t in every]
    new_y = [hy[t] - COURANT * (shifts.z_up(ex[t]) - ex[t] - diff_z[t]) for t in every]
    new_z = [hz[t] - COURANT * (diff_y[t] - (ex_y[t] - ex[t])) for t in every]
    return new_x, new_y, new_z


def grown(local, ex, ey, ez, hx, hy, hz, hy_x, hz_x, half, source, count):
    shifts = local.shifts
    hz_y, hx_y = shifts.y_down(hz), shifts.y_down(hx)
    new_x, new_y, new_z = [], [], []
    for t in range(count):
        diff_y = hz[t] if hz_x is None else hz[t] - hz_x[t]
        diff_z = hy[t] if hy_x is None else hy[t] - hy_x[t]
        if ex is not None:
            new_x.append(ex[t] + half[t] * (hz[t] - hz_y[t] - (hy[t] - shifts.z_down(hy[t]))))
        new_y.append(ey[t] + half[t] * (hx[t] - shifts.z_down(hx[t]) - diff_y))
        new_z.append(ez[t] + half[t] * (diff_z - (hx[t] - hx_y[t])) + source[t])
    return new_x, new_y, new_z


def started(dims, two, field_ref, below_ref, above_ref, small_ref, half_ref, mask_ref, edge_ref):
    edges = merged_edges(below_ref, None if two else above_ref, edge_ref)
    return Local(dims, field_ref, edges, small_ref, half_ref, mask_ref)


def store_tiles(ref, unit, values, tiles, nz):
    for t in range(tiles):
        at = (unit * tiles + t) * nz
        ref[at:at + nz, :] = values[t]


def lower_kernel(dims, two, *refs):
    nz, _, tiles = dims
    *given, material_ref, down_ref, edge_ref = refs
    local = started(dims, two, *given, edge_ref)
    local.material = [material_ref[local.rows(0, t), :].astype(jnp.float32) for t in range(tiles)]
    half = local.half(0)
    edges = [None] * 17
    for run in range(2):
        low = [local.load(run, comp, 0) for comp in range(6)]
        nearer = [local.load(run, comp, 1) for comp in (1, 2)]
        source = local.source(run, 0, 0)
        for part in range(2):
            ex, ey, ez, hx, hy, hz = [low[comp][part] for comp in range(6)]
            hx, hy, hz = small_steps(local, ex, ey, ez, hx, hy, hz, nearer[0][part], nearer[1][part])
            _, new_y, new_z = grown(local, None, ey, ez, hx, hy, hz, None, None, half, source[part], tiles + 1)
            for which, value, initial in ((0, new_y, ey), (1, new_z, ez)):
                unit = (run * 2 + part) * 2 + which
                store_tiles(down_ref, unit, value, tiles, nz)
                edges[unit] = initial[tiles]
                edges[8 + unit] = value[tiles]
    edges[16] = unpack_edge(local.edge(0), 24)
    store_tiles(down_ref, 8, local.material, tiles, nz)
    at = 9 * tiles * nz
    down_ref[at:at + nz, :] = pack_edges(edges, local.shifts.lane)


def upper_kernel(dims, two, *refs):
    nz, width_x, tiles = dims
    *given, _, up_ref, edge_ref = refs
    local = started(dims, two, *given, edge_ref)
    edges = []
    for run in range(2):
        high = [local.load(run, comp, width_x - 1) for comp in (0, 1, 2, 4, 5)]
        for part in range(2):
            ex, ey, ez, hy, hz = [values[part] for values in high]
            _, hy, hz = small_steps(local, ex, ey, ez, None, hy, hz, None, None)
            for which, value in ((0, hy), (1, hz)):
                store_tiles(up_ref, (run * 2 + part) * 2 + which, value, tiles, nz)
                edges.append(value[tiles])
    at = 8 * tiles * nz
    up_ref[at:at + nz, :] = pack_edges(edges, local.shifts.lane)


def halo(local, ref, edge, first_spot, run, which, row):
    nz, tiles = local.nz, local.tiles
    units = [(run * 2 + part) * 2 + which for part in range(2)]
    values = [
        [ref[(unit * tiles + t) * nz:(unit * tiles + t + 1) * nz, :] for t in range(tiles)]
        + [unpack_edge(edge, first_spot + unit)]
        for unit in units
    ]
    turned = [turn(values[0][t], values[1][t], *local.angle(row, run)) for t in range(tiles + 1)]
    return [[value[part] for value in turned] for part in range(2)]


def half_above(local, down_ref, edge):
    nz, tiles = local.nz, local.tiles
    own = [down_ref[(8 * tiles + t) * nz:(8 * tiles + t + 1) * nz, :] for t in range(tiles)]
    levels = local.levels()
    return [COURANT * inverse_eps(value, levels) for value in own + [unpack_edge(edge, 16)]]


def share_kernel(dims, two, *refs):
    nz, width_x, tiles = dims
    *given, face_ref, down_ref, share_ref, edge_ref = refs
    local = started(dims, two, *given, edge_ref)
    edge = down_ref[9 * tiles * nz:(9 * tiles + 1) * nz, :]
    half = local.half(width_x - 1)
    above = half_above(local, down_ref, edge)
    kept_e, kept_h = {}, {}
    every = range(tiles + 1)
    for run in range(2):
        low = [local.load(run, comp, width_x - 2) for comp in range(6)]
        high = [local.load(run, comp, width_x - 1) for comp in range(6)]
        source = local.source(run, 0, width_x - 1)
        early = [halo(local, face_ref, edge, 0, run, which, AHEAD) for which in range(2)]
        later = [halo(local, down_ref, edge, 8, run, which, AHEAD) for which in range(2)]
        for part in range(2):
            ex, ey, ez, hx, hy, hz = [high[comp][part] for comp in range(6)]
            low_x, low_y, low_z, _, low_hy, low_hz = [low[comp][part] for comp in range(6)]
            _, low_hy, low_hz = small_steps(local, low_x, low_y, low_z, None, low_hy, low_hz, ey, ez)
            hx, hy, hz = small_steps(local, ex, ey, ez, hx, hy, hz, early[0][part], early[1][part])
            ex, ey, ez = grown(local, ex, ey, ez, hx, hy, hz, low_hy, low_hz, half, source[part], tiles + 1)
            above_y = [later[0][part][t] + above[t] * hz[t] for t in every]
            above_z = [later[1][part][t] - above[t] * hy[t] for t in every]
            _, hy, hz = small_steps(local, ex, ey, ez, None, hy, hz, above_y, above_z)
            kept_e[run, part] = (above_y, above_z)
            kept_h[run, part] = (hy, hz)
    for t in range(tiles):
        total = 0.0
        for run in range(2):
            for which, sign in ((0, 1.0), (1, -1.0)):
                term = (
                    kept_e[run, 0][which][t] * kept_h[1 - run, 0][1 - which][t]
                    - kept_e[run, 1][which][t] * kept_h[1 - run, 1][1 - which][t]
                )
                total = total + sign * term
        share_ref[t * nz:(t + 1) * nz, :] = above[t] * total


def product(now, later, t):
    return now[0, 0][t] * later[1, 0][t] - now[0, 1][t] * later[1, 1][t]


def both(one, two, t):
    return product(one, two, t) + product(two, one, t)


def interior_kernel(dims, two, *refs):
    nz, width_x, tiles = dims
    *given, face_ref, down_ref, kept_ref, cross_ref, edge_ref = refs
    local = started(dims, two, *given, edge_ref)
    every, own, layers = range(tiles + 1), range(tiles), range(width_x)
    edge = down_ref[9 * tiles * nz:(9 * tiles + 1) * nz, :]
    half = [local.half(x) for x in layers]
    above = half_above(local, down_ref, edge)
    kept_one, kept_two = {}, {}
    for run in range(2):
        sources = [[local.source(run, step, x) for x in layers] for step in range(2)]
        fields = [[local.load(run, comp, x) for x in layers] for comp in range(6)]
        early = [halo(local, face_ref, edge, 0, run, which, AHEAD) for which in range(2)]
        later = [halo(local, down_ref, edge, 8, run, which, AHEAD) for which in range(2)]
        for part in range(2):
            ex, ey, ez, hx, hy, hz = [[fields[comp][x][part] for x in layers] for comp in range(6)]
            under_y = [COURANT * ez[0][t] for t in every]
            under_z = [-COURANT * ey[0][t] for t in every]
            above_y, above_z = early[0][part], early[1][part]
            for step in range(2):
                ey_x, ez_x = ey[1:] + [above_y], ez[1:] + [above_z]
                for x in layers:
                    hx[x], hy[x], hz[x] = small_steps(
                        local, ex[x], ey[x], ez[x], hx[x], hy[x], hz[x], ey_x[x], ez_x[x]
                    )
                if step == 0:
                    above_y = [later[0][part][t] + above[t] * hz[-1][t] for t in every]
                    above_z = [later[1][part][t] - above[t] * hy[-1][t] for t in every]
                else:
                    under_y, under_z = None, None
                for x in layers:
                    hy_x, hz_x = (under_y, under_z) if x == 0 else (hy[x - 1], hz[x - 1])
                    ex[x], ey[x], ez[x] = grown(
                        local, ex[x], ey[x], ez[x], hx[x], hy[x], hz[x], hy_x, hz_x, half[x], sources[step][x][part],
                        tiles if step else tiles + 1,
                    )
                for x in layers:
                    for comp, value in enumerate((ex[x], ey[x], ez[x])):
                        (kept_two if step else kept_one).setdefault((comp, x), {})[run, part] = value
    for pair in range(4):
        where = (pair // 2, pair % 2)
        for comp in range(3):
            store_tiles(kept_ref, pair * 8 + comp, kept_one[comp, 0][where], tiles, nz)
            store_tiles(kept_ref, pair * 8 + 3 + comp, kept_two[comp, 0][where], tiles, nz)
        for comp in (1, 2):
            store_tiles(kept_ref, pair * 8 + 5 + comp, kept_one[comp, 1][where], tiles, nz)
    store_tiles(kept_ref, 32, half[0], tiles, nz)
    at = 33 * tiles * nz
    kept_ref[at:at + nz, :] = half[0][tiles]
    for x in range(1, width_x):
        for t in own:
            total = 0.0
            for comp in range(3):
                total = total + both(kept_one[comp, x], kept_two[comp, x], t)
            cross_ref[local.rows(x, t), :] = -half[x][t] * total
    for t in own:
        cross_ref[local.rows(0, t), :] = half[0][t]


def final_kernel(dims, small_ref, half_ref, kept_ref, inner_ref, up_ref, share_ref, cross_ref):
    nz, width_x, tiles = dims
    local = Local(dims, None, None, small_ref, half_ref, None)
    shifts = local.shifts
    every, own = range(tiles + 1), range(tiles)

    def tile(ref, unit, t):
        return ref[(unit * tiles + t) * nz:(unit * tiles + t + 1) * nz, :]

    half = [tile(kept_ref, 32, t) for t in every]
    next_half = [tile(half_ref, 1, t) for t in own]
    edge = up_ref[8 * tiles * nz:(8 * tiles + 1) * nz, :]
    one, two, next_one, next_add = [[{} for _ in range(3)] for _ in range(4)]
    for run in range(2):
        under = [halo(local, up_ref, edge, 0, run, which, BACK) for which in range(2)]
        for part in range(2):
            pair = run * 2 + part
            add_y = [half[t] * under[1][part][t] for t in every]
            add_z = [-half[t] * under[0][part][t] for t in every]
            add_z_y = shifts.y_up(add_z)
            hx = [-COURANT * (add_z_y[t] - add_z[t] - (shifts.z_up(add_y[t]) - add_y[t])) for t in every]
            hy = [-COURANT * add_z[t] for t in every]
            hz = [COURANT * add_y[t] for t in every]
            hz_y, hx_y = shifts.y_down(hz), shifts.y_down(hx)
            more = [
                [half[t] * (hz[t] - hz_y[t] - (hy[t] - shifts.z_down(hy[t]))) for t in own],
                [add_y[t] + half[t] * (hx[t] - shifts.z_down(hx[t]) - hz[t]) for t in own],
                [add_z[t] + half[t] * (hy[t] - (hx[t] - hx_y[t])) for t in own],
            ]
            first = [None, add_y, add_z]
            for comp in range(3):
                value = [tile(kept_ref, pair * 8 + comp, t) for t in own]
                one[comp][run, part] = value if comp == 0 else [value[t] + first[comp][t] for t in own]
                two[comp][run, part] = [tile(kept_ref, pair * 8 + 3 + comp, t) + more[comp][t] for t in own]
            for comp, value in ((1, hz), (2, [-hy[t] for t in own])):
                next_one[comp][run, part] = [tile(kept_ref, pair * 8 + 5 + comp, t) for t in own]
                next_add[comp][run, part] = [next_half[t] * value[t] for t in own]
    for t in own:
        total = share_ref[t * nz:(t + 1) * nz, :]
        for comp in range(3):
            total = total + both(one[comp], two[comp], t)
        cross_ref[local.rows(0, t), :] = -half[t] * total
        total = both(next_one[1], next_add[1], t) + both(next_one[2], next_add[2], t)
        cross_ref[local.rows(1, t), :] = inner_ref[local.rows(1, t), :] - next_half[t] * total
        for x in range(2, width_x):
            cross_ref[local.rows(x, t), :] = inner_ref[local.rows(x, t), :]


def sum_kernel(own_ref, other_ref, out_ref):
    out_ref[...] = own_ref[...] + other_ref[...]


VMEM = pl.BlockSpec(memory_space=pltpu.VMEM)
SMEM = pl.BlockSpec(memory_space=pltpu.SMEM)


HBM = pl.BlockSpec(memory_space=pltpu.HBM)
MIB = 1024 * 1024


def call(kernel, name, in_specs, rows, cost, scratch=(), limit=48 * MIB):
    shapes = [jax.ShapeDtypeStruct((count, LANES), jnp.float32) for count in rows]
    return pl.pallas_call(
        kernel,
        name=name,
        out_shape=shapes,
        in_specs=in_specs,
        out_specs=[VMEM] * len(shapes),
        scratch_shapes=list(scratch),
        compiler_params=pltpu.CompilerParams(vmem_limit_bytes=limit),
        cost_estimate=pl.CostEstimate(flops=0, bytes_accessed=cost, transcendentals=0),
    )


def moved(value, axis, steps):
    count = lax.axis_size(axis)
    return lax.ppermute(value, axis, [(source, (source + steps) % count) for source in range(count)])


def local(field_state, material_map, eps_table, bloch_phase, source_cells, source_wave):
    nz, width_x, width_y = material_map.shape
    tiles = width_y // LANES
    dims = (nz, width_x, tiles)
    rows = nz * tiles * width_x
    fields = field_state.reshape(24, nz, width_x, tiles, LANES).transpose(0, 1, 3, 2, 4).reshape(24, rows, LANES)
    material = material_map.reshape(nz, width_x, tiles, LANES).transpose(0, 2, 1, 3).reshape(rows, LANES)
    unit = nz * tiles
    two = lax.axis_size("gy") == 2
    levels = eps_table.shape[0]

    (face,) = call(
        functools.partial(face_kernel, dims), "faces", [HBM], [8 * unit], 100_000,
        (pltpu.VMEM((4, 2, rows, LANES), jnp.float32), pltpu.SemaphoreType.DMA((4,))),
        53 * MIB,
    )(fields)
    (edge,) = call(functools.partial(edge_kernel, dims), "edges", [VMEM] * 3, [width_x * nz], 80_000_000)(
        face, fields, material
    )
    small, half, mask = call(
        functools.partial(prepare_kernel, dims), "prepare", [VMEM] * 2 + [SMEM] * 4,
        [LEVELS + levels, rows, 2 * width_x * (tiles + 1) * nz], 20_000_000,
    )(edge, material, eps_table, bloch_phase, source_cells, source_wave)
    face = moved(face, "gx", -1)
    below = moved(edge, "gy", 1)
    above = below if two else moved(edge, "gy", -1)
    given = (fields, below, above, small, half, mask)
    specs = [VMEM] * len(given)
    scratch = (pltpu.VMEM((width_x * nz, LANES), jnp.float32),)

    def stage(kernel, name, cost, rows, *more):
        return call(
            functools.partial(kernel, dims, two), name, specs + [VMEM] * len(more), rows, cost, scratch
        )(*given, *more)

    down = moved(stage(lower_kernel, "lower", 20_000_000, [9 * unit + nz], material)[0], "gx", -1)
    up = moved(stage(upper_kernel, "upper", 20_000_000, [8 * unit + nz], face)[0], "gx", 1)
    share = moved(stage(share_kernel, "share", 20_000_000, [unit], face, down)[0], "gx", 1)
    kept, inner = stage(interior_kernel, "interior", 20_000_000, [33 * unit + nz, rows], face, down)
    (cross,) = call(functools.partial(final_kernel, dims), "final", [VMEM] * 6, [rows], 2_000_000)(
        small, half, kept, inner, up, share
    )
    other = moved(cross, "src", 1)
    (out,) = call(sum_kernel, "gradient", [VMEM, VMEM], [rows], 500_000)(cross, other)
    return out.reshape(nz, tiles, width_x, LANES).transpose(0, 2, 1, 3).reshape(nz, width_x, width_y)


def solution(mesh):
    return jax.shard_map(
        local,
        mesh=mesh,
        in_specs=(
            P(("design", "src"), None, None, None, None, "gx", "gy"),
            P("design", "gx", "gy"),
            P(),
            P("design"),
            P(("design", "src"), None),
            P(("design", "src"), None, None, None),
        ),
        out_specs=P("design", "gx", "gy"),
        check_vma=False,
    )
```

time: 35.8 us -> 29.5 us (0.82)
  local copies, waits for them, and re-layouts: 2.35 us -> 0.02 us
  waiting for transfers between devices: 16.5 us -> 14.5 us
  starting transfers between devices: 8.92 us -> 7.81 us
  Pallas kernels: 7.72 us -> 6.87 us
    unnamed x16 -> x12, local copies, waits for them, and re-layouts: 2.27 us -> 0.02 us
    ppermute x6, waiting for transfers between devices: 16.5 us -> 14.5 us  [moved(): lax.ppermute(value, axis, [(source, (source + steps) % count) for source...]
    ppermute x6, starting transfers between devices: 8.92 us -> 7.81 us  [moved(): lax.ppermute(value, axis, [(source, (source + steps) % count) for source...]
    pallas_call x7 -> x9, Pallas kernels: 7.72 us -> 6.87 us  [the longest x4 3.66 us: stage(): call(functools.partial(kernel, dims, two), name, specs + [VMEM] * len(mor...]
  transfers between devices with their start and end apart: 6 -> 6, of which waited for: 5 -> 5; matrix products, arithmetic and copies ran while one was open for 0% -> 0% of each run, Pallas kernels for 12% -> 16%
where the time goes in v3:
time: 29.5 us; the launch traced here: 29.3 us
  waiting for transfers between devices  14.5 us (49%)
  starting transfers between devices  7.81 us (26%)
  Pallas kernels  6.87 us (23%)
    ppermute x6, waiting for transfers between devices, moved(): lax.ppermute(value, axis, [(source, (source + steps) % count) for source...  14.5 us
    ppermute x6, starting transfers between devices, moved(): lax.ppermute(value, axis, [(source, (source + steps) % count) for source...  7.81 us
    pallas_call x4, Pallas kernels, stage(): call(functools.partial(kernel, dims, two), name, specs + [VMEM] * len(mor...  3.66 us
    pallas_call x1, Pallas kernels, local(): call(functools.partial(face_kernel, dims), 'faces', [HBM], [8 * unit], 10...  1.25 us
    pallas_call x1, Pallas kernels, local(): call(functools.partial(prepare_kernel, dims), 'prepare', [VMEM] * 2 + [SM...  0.67 us
    pallas_call x1, Pallas kernels, local(): call(sum_kernel, 'gradient', [VMEM, VMEM], [rows], 500000)(cross, other)  0.64 us
  transfers between devices with their start and end apart: 6, of which 5 were waited for; matrix products, arithmetic and copies ran while one was open for 0% of the time, Pallas kernels for 16%

profile of v3, /device:TPU:0, one launch (start us, length us, event | category | flops | bytes accessed | tf_op | source)
XLA Modules:
  0.0 29.3 jit_solution(3896355263637631446)
XLA Ops:
  0.0 0.0 copy-start
  0.0 0.0 copy-start.1
  0.0 0.0 copy-start.2
  0.0 0.0 copy-start.3
  0.0 0.0 copy-start.4
  0.0 0.0 copy-start.5
  0.0 1.3 %faces.1.order_ref = f32[512,128]{1,0:T(8,128)S(1)} custom-call(f32[24,128,128]{2,1,0:T(8,128)} %bitcast.15), custom_call_target="tpu_custom_call" | custom-call | bytes 100000 | tf_op jit(solution)/shard_map/faces/pallas_call | solution.py:525
  1.3 5.1 %collective-permute-start.1 = (f32[512,128]{1,0:T(8,128)S(1)}, f32[512,128]{1,0:T(8,128)S(1)}, u32[]{:S(2)}, u32[]{:S(2)}) collective-permute-start(f32[512,128]{1,0:T(8,128)S(1)} %faces.1.order_ref), channel_id=1, source_target_pairs={{0,12},{4,0},{8,4},{12,8},{1,13},{5,1},{9,5},{13,9},{2,14},{6,2},{... | collective-permute-start | bytes 786440 | tf_op jit(solution)/shard_map/ppermute | solution.py:511
  6.4 0.0 copy-done
  6.4 0.0 copy-done.1
  6.4 0.3 edges.1.order_ref
  6.7 1.6 %collective-permute-start = (f32[64,128]{1,0:T(8,128)S(1)}, f32[64,128]{1,0:T(8,128)S(1)}, u32[]{:S(2)}, u32[]{:S(2)}) collective-permute-start(f32[64,128]{1,0:T(8,128)S(1)} %edges.1.order_ref), channel_id=1, source_target_pairs={{0,2},{2,0},{1,3},{3,1},{4,6},{6,4},{5,7},{7,5},{8,10},{10,8},{9,1... | collective-permute-start | bytes 98312 | tf_op jit(solution)/shard_map/ppermute | solution.py:511
  8.2 0.0 copy-done.2
  8.2 0.0 copy-done.3
  8.2 0.0 copy-done.4
  8.2 0.0 copy-done.5
  8.3 0.7 %prepare.1 = (f32[32,128]{1,0:T(8,128)S(1)}, f32[128,128]{1,0:T(8,128)S(1)}, f32[384,128]{1,0:T(8,128)S(1)}) custom-call(f32[64,128]{1,0:T(8,128)S(1)} %edges.1.order_ref, s32[128,128]{1,0:T(8,128)S(1)} %bitcast.22, f32[8]{0:T(128)S(1)} %copy-done.3, f32[2]{0:T(128)S(1)} %copy-done.4, s32[1,2]{1,0:T(1,128)S(1)} %copy-done.5, f32[1,2,2,2]{3,2,1,0:T(2,128)S(1)} %copy-done.2), custom_call_target="tpu_custom_call" | custom-call | bytes 20000000 | tf_op jit(solution)/shard_map/prepare/pallas_call | solution.py:533
  8.9 1.7 %collective-permute-done.refs_1_.refs_2_ = f32[64,128]{1,0:T(8,128)S(1)} collective-permute-done((f32[64,128]{1,0:T(8,128)S(1)}, f32[64,128]{1,0:T(8,128)S(1)}, u32[]{:S(2)}, u32[]{:S(2)}) %collective-permute-start) | collective-permute-done | bytes 32800 | tf_op jit(solution)/shard_map/ppermute | solution.py:511
  10.7 0.7 %lower.1 = f32[608,128]{1,0:T(8,128)S(1)} custom-call(f32[24,128,128]{2,1,0:T(8,128)S(1)} %bitcast.17, f32[64,128]{1,0:T(8,128)S(1)} %collective-permute-done.refs_1_.refs_2_, f32[64,128]{1,0:T(8,128)S(1)} %collective-permute-done.refs_1_.refs_2_, f32[32,128]{1,0:T(8,128)S(1)} %get-tuple-element.10.refs_3_.small_ref, ...), custom_call_target="tpu_custom_call" | custom-call | bytes 20000000 | tf_op jit(solution)/shard_map/lower/pallas_call | solution.py:545
  11.3 0.5 %collective-permute-start.2 = (f32[608,128]{1,0:T(8,128)S(1)}, f32[608,128]{1,0:T(8,128)S(1)}, u32[]{:S(2)}, u32[]{:S(2)}) collective-permute-start(f32[608,128]{1,0:T(8,128)S(1)} %lower.1), channel_id=1, source_target_pairs={{0,12},{4,0},{8,4},{12,8},{1,13},{5,1},{9,5},{13,9},{2,14},{6,2},{... | collective-permute-start | bytes 933896 | tf_op jit(solution)/shard_map/ppermute | solution.py:511
  11.8 1.3 %collective-permute-done.1.refs_6_ = f32[512,128]{1,0:T(8,128)S(1)} collective-permute-done((f32[512,128]{1,0:T(8,128)S(1)}, f32[512,128]{1,0:T(8,128)S(1)}, u32[]{:S(2)}, u32[]{:S(2)}) %collective-permute-start.1) | collective-permute-done | bytes 262176 | tf_op jit(solution)/shard_map/ppermute | solution.py:511
  13.1 0.3 %upper.1 = f32[544,128]{1,0:T(8,128)S(1)} custom-call(f32[24,128,128]{2,1,0:T(8,128)S(1)} %bitcast.18, f32[64,128]{1,0:T(8,128)S(1)} %collective-permute-done.refs_1_.refs_2_, f32[64,128]{1,0:T(8,128)S(1)} %collective-permute-done.refs_1_.refs_2_, f32[32,128]{1,0:T(8,128)S(1)} %get-tuple-element.10.refs_3_.small_ref, ...), custom_call_target="tpu_custom_call" | custom-call | bytes 20000000 | tf_op jit(solution)/shard_map/upper/pallas_call | solution.py:545
  13.4 0.5 %collective-permute-start.3 = (f32[544,128]{1,0:T(8,128)S(1)}, f32[544,128]{1,0:T(8,128)S(1)}, u32[]{:S(2)}, u32[]{:S(2)}) collective-permute-start(f32[544,128]{1,0:T(8,128)S(1)} %upper.1), channel_id=1, source_target_pairs={{0,4},{4,8},{8,12},{12,0},{1,5},{5,9},{9,13},{13,1},{2,6},{6,10},{... | collective-permute-start | bytes 835592 | tf_op jit(solution)/shard_map/ppermute | solution.py:511
  13.9 6.4 %collective-permute-done.2.refs_7_ = f32[608,128]{1,0:T(8,128)S(1)} collective-permute-done((f32[608,128]{1,0:T(8,128)S(1)}, f32[608,128]{1,0:T(8,128)S(1)}, u32[]{:S(2)}, u32[]{:S(2)}) %collective-permute-start.2) | collective-permute-done | bytes 311328 | tf_op jit(solution)/shard_map/ppermute | solution.py:511
  20.3 0.9 %share.1 = f32[64,128]{1,0:T(8,128)S(1)} custom-call(f32[24,128,128]{2,1,0:T(8,128)S(1)} %bitcast.19, f32[64,128]{1,0:T(8,128)S(1)} %collective-permute-done.refs_1_.refs_2_, f32[64,128]{1,0:T(8,128)S(1)} %collective-permute-done.refs_1_.refs_2_, f32[32,128]{1,0:T(8,128)S(1)} %get-tuple-element.10.refs_3_.small_ref, ...), custom_call_target="tpu_custom_call" | custom-call | bytes 20000000 | tf_op jit(solution)/shard_map/share/pallas_call | solution.py:545
  21.2 0.1 collective-permute-start.4
  21.3 1.8 %interior.1 = (f32[2144,128]{1,0:T(8,128)S(1)}, f32[128,128]{1,0:T(8,128)S(1)}) custom-call(f32[24,128,128]{2,1,0:T(8,128)S(1)} %bitcast.20, f32[64,128]{1,0:T(8,128)S(1)} %collective-permute-done.refs_1_.refs_2_, f32[64,128]{1,0:T(8,128)S(1)} %collective-permute-done.refs_1_.refs_2_, f32[32,128]{1,0:T(8,128)S(1)} %get-tuple-element.10.refs_3_.small_ref, ...), custom_call_target="tpu_custom_call" | custom-call | bytes 20000000 | tf_op jit(solution)/shard_map/interior/pallas_call | solution.py:545
  23.1 3.9 %collective-permute-done.4.share_ref = f32[64,128]{1,0:T(8,128)S(1)} collective-permute-done((f32[64,128]{1,0:T(8,128)S(1)}, f32[64,128]{1,0:T(8,128)S(1)}, u32[]{:S(2)}, u32[]{:S(2)}) %collective-permute-start.4) | collective-permute-done | bytes 32800 | tf_op jit(solution)/shard_map/ppermute | solution.py:511
  27.0 0.0 collective-permute-done.3.up_ref
  27.0 0.4 %final.1.own_ref = f32[128,128]{1,0:T(8,128)S(1)} custom-call(f32[32,128]{1,0:T(8,128)S(1)} %get-tuple-element.10.refs_3_.small_ref, f32[128,128]{1,0:T(8,128)S(1)} %get-tuple-element.11.refs_4_.half_ref, f32[2144,128]{1,0:T(8,128)S(1)} %get-tuple-element.13.kept_ref, f32[128,128]{1,0:T(8,128)S(1)} %get-tuple-element.14.inner_ref, ...), custom_call_target="tpu_custom_call" | custom-call | bytes 2000000 | tf_op jit(solution)/shard_map/final/pallas_call | solution.py:553
  27.4 0.1 collective-permute-start.5
  27.4 1.2 %collective-permute-done.5.other_ref = f32[128,128]{1,0:T(8,128)S(1)} collective-permute-done((f32[128,128]{1,0:T(8,128)S(1)}, f32[128,128]{1,0:T(8,128)S(1)}, u32[]{:S(2)}, u32[]{:S(2)}) %collective-permute-start.5) | collective-permute-done | bytes 65568 | tf_op jit(solution)/shard_map/ppermute | solution.py:511
  28.7 0.6 %gradient.1 = f32[128,128]{1,0:T(8,128)} custom-call(f32[128,128]{1,0:T(8,128)S(1)} %final.1.own_ref, f32[128,128]{1,0:T(8,128)S(1)} %collective-permute-done.5.other_ref), custom_call_target="tpu_custom_call" | custom-call | bytes 500000 | tf_op jit(solution)/shard_map/gradient/pallas_call | solution.py:557
Async XLA Ops:
  0.0 6.4 %copy-start = (f32[1,2,2,6,32,2,256]{6,5,4,3,2,1,0:T(2,128)S(1)}, f32[1,2,2,6,32,2,256]{6,5,4,3,2,1,0:T(2,128)}, u32[]{:S(2)}) copy-start(f32[1,2,2,6,32,2,256]{6,5,4,3,2,1,0:T(2,128)} %param.6) | copy-start | bytes 4718596
  0.0 6.4 %copy-start.1 = (s32[32,2,256]{2,1,0:T(2,128)S(1)}, s32[32,2,256]{2,1,0:T(2,128)}, u32[]{:S(2)}) copy-start(s32[32,2,256]{2,1,0:T(2,128)} %param.7) | copy-start | bytes 196612
  0.0 8.2 %copy-start.2 = (f32[1,2,2,2]{3,2,1,0:T(2,128)S(1)}, f32[1,2,2,2]{3,2,1,0:T(2,128)}, u32[]{:S(2)}) copy-start(f32[1,2,2,2]{3,2,1,0:T(2,128)} %wave_ref.1) | copy-start | bytes 100
  0.0 8.2 %copy-start.3 = (f32[8]{0:T(128)S(1)}, f32[8]{0:T(128)}, u32[]{:S(2)}) copy-start(f32[8]{0:T(128)} %table_ref.1) | copy-start | bytes 100
  0.0 8.2 %copy-start.4 = (f32[2]{0:T(128)S(1)}, f32[2]{0:T(128)}, u32[]{:S(2)}) copy-start(f32[2]{0:T(128)} %phase_ref.1) | copy-start | bytes 28
  0.0 8.2 %copy-start.5 = (s32[1,2]{1,0:T(1,128)S(1)}, s32[1,2]{1,0:T(1,128)}, u32[]{:S(2)}) copy-start(s32[1,2]{1,0:T(1,128)} %cells_ref.1) | copy-start | bytes 28
  1.3 11.8 %collective-permute-start.1 = (f32[512,128]{1,0:T(8,128)S(1)}, f32[512,128]{1,0:T(8,128)S(1)}, u32[]{:S(2)}, u32[]{:S(2)}) collective-permute-start(f32[512,128]{1,0:T(8,128)S(1)} %faces.1.order_ref), channel_id=1, source_target_pairs={{0,12},{4,0},{8,4},{12,8},{1,13},{5,1},{9,5},{13,9},{2,14},{6,2},{... | collective-permute-start | bytes 786440 | tf_op jit(solution)/shard_map/ppermute | solution.py:511
  6.7 4.0 %collective-permute-start = (f32[64,128]{1,0:T(8,128)S(1)}, f32[64,128]{1,0:T(8,128)S(1)}, u32[]{:S(2)}, u32[]{:S(2)}) collective-permute-start(f32[64,128]{1,0:T(8,128)S(1)} %edges.1.order_ref), channel_id=1, source_target_pairs={{0,2},{2,0},{1,3},{3,1},{4,6},{6,4},{5,7},{7,5},{8,10},{10,8},{9,1... | collective-permute-start | bytes 98312 | tf_op jit(solution)/shard_map/ppermute | solution.py:511
  11.3 9.0 %collective-permute-start.2 = (f32[608,128]{1,0:T(8,128)S(1)}, f32[608,128]{1,0:T(8,128)S(1)}, u32[]{:S(2)}, u32[]{:S(2)}) collective-permute-start(f32[608,128]{1,0:T(8,128)S(1)} %lower.1), channel_id=1, source_target_pairs={{0,12},{4,0},{8,4},{12,8},{1,13},{5,1},{9,5},{13,9},{2,14},{6,2},{... | collective-permute-start | bytes 933896 | tf_op jit(solution)/shard_map/ppermute | solution.py:511
  13.4 13.6 %collective-permute-start.3 = (f32[544,128]{1,0:T(8,128)S(1)}, f32[544,128]{1,0:T(8,128)S(1)}, u32[]{:S(2)}, u32[]{:S(2)}) collective-permute-start(f32[544,128]{1,0:T(8,128)S(1)} %upper.1), channel_id=1, source_target_pairs={{0,4},{4,8},{8,12},{12,0},{1,5},{5,9},{9,13},{13,1},{2,6},{6,10},{... | collective-permute-start | bytes 835592 | tf_op jit(solution)/shard_map/ppermute | solution.py:511
  21.2 5.8 %collective-permute-start.4 = (f32[64,128]{1,0:T(8,128)S(1)}, f32[64,128]{1,0:T(8,128)S(1)}, u32[]{:S(2)}, u32[]{:S(2)}) collective-permute-start(f32[64,128]{1,0:T(8,128)S(1)} %share.1), channel_id=1, source_target_pairs={{0,4},{4,8},{8,12},{12,0},{1,5},{5,9},{9,13},{13,1},{2,6},{6,10},{... | collective-permute-start | bytes 98312 | tf_op jit(solution)/shard_map/ppermute | solution.py:511
  27.4 1.3 %collective-permute-start.5 = (f32[128,128]{1,0:T(8,128)S(1)}, f32[128,128]{1,0:T(8,128)S(1)}, u32[]{:S(2)}, u32[]{:S(2)}) collective-permute-start(f32[128,128]{1,0:T(8,128)S(1)} %final.1.own_ref), channel_id=1, source_target_pairs={{0,1},{1,0},{2,3},{3,2},{4,5},{5,4},{6,7},{7,6},{8,9},{9,8},{10,11... | collective-permute-start | bytes 196616 | tf_op jit(solution)/shard_map/ppermute | solution.py:511

commit v4 on v3

--- a/solution.py
+++ b/solution.py
@@ -9,6 +9,7 @@
 
 COURANT = 0.5
 LANES = 128
+MATERIAL_MOVE = 95
 EDGE = 4
 
 
@@ -30,6 +31,24 @@
 
 def unpack_edge(packed, spot):
     return pltpu.roll(packed, LANES - EDGE * spot - 2, 1)
+
+
+def folded(packed, width):
+    groups = LANES // width
+    rows = packed.shape[0] // groups
+    lane = lax.broadcasted_iota(jnp.int32, (rows, LANES), 1)
+    result = packed[0:rows]
+    for group in range(1, groups):
+        moved = pltpu.roll(packed[group * rows:(group + 1) * rows], group * width, 1)
+        result = jnp.where(lane // width == group, moved, result)
+    return result
+
+
+def unfolded(values, width):
+    groups = LANES // width
+    return jnp.concatenate(
+        [values] + [pltpu.roll(values, LANES - group * width, 1) for group in range(1, groups)], axis=0
+    )
 
 
 class Shifts:
@@ -271,7 +290,7 @@
     local = started(dims, two, *given, edge_ref)
     local.material = [material_ref[local.rows(0, t), :].astype(jnp.float32) for t in range(tiles)]
     half = local.half(0)
-    edges = [None] * 17
+    edges = [None] * 16
     for run in range(2):
         low = [local.load(run, comp, 0) for comp in range(6)]
         nearer = [local.load(run, comp, 1) for comp in (1, 2)]
@@ -285,10 +304,11 @@
                 store_tiles(down_ref, unit, value, tiles, nz)
                 edges[unit] = initial[tiles]
                 edges[8 + unit] = value[tiles]
-    edges[16] = unpack_edge(local.edge(0), 24)
     store_tiles(down_ref, 8, local.material, tiles, nz)
-    at = 9 * tiles * nz
-    down_ref[at:at + nz, :] = pack_edges(edges, local.shifts.lane)
+    packed = pack_edges(edges, local.shifts.lane)
+    column = pltpu.roll(unpack_edge(local.edge(0), 24), LANES - MATERIAL_MOVE, 1)
+    packed = jnp.where(local.shifts.lane == EDGE * 8, column, packed)
+    down_ref[9 * tiles * nz:, :] = folded(packed, 64)
 
 
 def upper_kernel(dims, two, *refs):
@@ -304,8 +324,7 @@
             for which, value in ((0, hy), (1, hz)):
                 store_tiles(up_ref, (run * 2 + part) * 2 + which, value, tiles, nz)
                 edges.append(value[tiles])
-    at = 8 * tiles * nz
-    up_ref[at:at + nz, :] = pack_edges(edges, local.shifts.lane)
+    up_ref[8 * tiles * nz:, :] = folded(pack_edges(edges, local.shifts.lane), 32)
 
 
 def halo(local, ref, edge, first_spot, run, which, row):
@@ -324,14 +343,14 @@
     nz, tiles = local.nz, local.tiles
     own = [down_ref[(8 * tiles + t) * nz:(8 * tiles + t + 1) * nz, :] for t in range(tiles)]
     levels = local.levels()
-    return [COURANT * inverse_eps(value, levels) for value in own + [unpack_edge(edge, 16)]]
+    return [COURANT * inverse_eps(value, levels) for value in own + [pltpu.roll(edge, MATERIAL_MOVE, 1)]]
 
 
 def share_kernel(dims, two, *refs):
     nz, width_x, tiles = dims
     *given, face_ref, down_ref, share_ref, edge_ref = refs
     local = started(dims, two, *given, edge_ref)
-    edge = down_ref[9 * tiles * nz:(9 * tiles + 1) * nz, :]
+    edge = unfolded(down_ref[9 * tiles * nz:, :], 64)
     half = local.half(width_x - 1)
     above = half_above(local, down_ref, edge)
     kept_e, kept_h = {}, {}
@@ -375,10 +394,10 @@
 
 def interior_kernel(dims, two, *refs):
     nz, width_x, tiles = dims
-    *given, face_ref, down_ref, kept_ref, cross_ref, edge_ref = refs
+    *given, face_ref, down_ref, _, kept_ref, cross_ref, edge_ref = refs
     local = started(dims, two, *given, edge_ref)
     every, own, layers = range(tiles + 1), range(tiles), range(width_x)
-    edge = down_ref[9 * tiles * nz:(9 * tiles + 1) * nz, :]
+    edge = unfolded(down_ref[9 * tiles * nz:, :], 64)
     half = [local.half(x) for x in layers]
     above = half_above(local, down_ref, edge)
     kept_one, kept_two = {}, {}
@@ -432,7 +451,7 @@
         cross_ref[local.rows(0, t), :] = half[0][t]
 
 
-def final_kernel(dims, small_ref, half_ref, kept_ref, inner_ref, up_ref, share_ref, cross_ref):
+def final_kernel(dims, small_ref, half_ref, kept_ref, inner_ref, up_ref, *cross_refs):
     nz, width_x, tiles = dims
     local = Local(dims, None, None, small_ref, half_ref, None)
     shifts = local.shifts
@@ -443,7 +462,7 @@
 
     half = [tile(kept_ref, 32, t) for t in every]
     next_half = [tile(half_ref, 1, t) for t in own]
-    edge = up_ref[8 * tiles * nz:(8 * tiles + 1) * nz, :]
+    edge = unfolded(up_ref[8 * tiles * nz:, :], 32)
     one, two, next_one, next_add = [[{} for _ in range(3)] for _ in range(4)]
     for run in range(2):
         under = [halo(local, up_ref, edge, 0, run, which, BACK) for which in range(2)]
@@ -470,18 +489,33 @@
                 next_one[comp][run, part] = [tile(kept_ref, pair * 8 + 5 + comp, t) for t in own]
                 next_add[comp][run, part] = [next_half[t] * value[t] for t in own]
     for t in own:
-        total = share_ref[t * nz:(t + 1) * nz, :]
-        for comp in range(3):
-            total = total + both(one[comp], two[comp], t)
-        cross_ref[local.rows(0, t), :] = -half[t] * total
-        total = both(next_one[1], next_add[1], t) + both(next_one[2], next_add[2], t)
-        cross_ref[local.rows(1, t), :] = inner_ref[local.rows(1, t), :] - next_half[t] * total
-        for x in range(2, width_x):
-            cross_ref[local.rows(x, t), :] = inner_ref[local.rows(x, t), :]
-
-
-def sum_kernel(own_ref, other_ref, out_ref):
-    out_ref[...] = own_ref[...] + other_ref[...]
+        for x in range(width_x):
+            if x == 0:
+                total = 0.0
+                for comp in range(3):
+                    total = total + both(one[comp], two[comp], t)
+                total = -half[t] * total
+            else:
+                total = inner_ref[local.rows(x, t), :]
+                if x == 1:
+                    total = total - next_half[t] * (
+                        both(next_one[1], next_add[1], t) + both(next_one[2], next_add[2], t)
+                    )
+            cross_refs[x * tiles + t][...] = total
+
+
+def sum_kernel(dims, half_ref, own_share_ref, other_share_ref, *refs):
+    nz, width_x, tiles = dims
+    *parts, out_ref = refs
+    count = width_x * tiles
+    for x in range(width_x):
+        for t in range(tiles):
+            index = x * tiles + t
+            total = parts[index][...] + parts[count + index][...]
+            if x == 0:
+                span = slice(t * nz, (t + 1) * nz)
+                total = total - half_ref[span, :] * (own_share_ref[span, :] + other_share_ref[span, :])
+            out_ref[pl.ds(t * width_x + x, nz, stride=tiles * width_x), :] = total
 
 
 VMEM = pl.BlockSpec(memory_space=pltpu.VMEM)
@@ -546,15 +580,27 @@
             functools.partial(kernel, dims, two), name, specs + [VMEM] * len(more), rows, cost, scratch
         )(*given, *more)
 
-    down = moved(stage(lower_kernel, "lower", 20_000_000, [9 * unit + nz], material)[0], "gx", -1)
-    up = moved(stage(upper_kernel, "upper", 20_000_000, [8 * unit + nz], face)[0], "gx", 1)
-    share = moved(stage(share_kernel, "share", 20_000_000, [unit], face, down)[0], "gx", 1)
-    kept, inner = stage(interior_kernel, "interior", 20_000_000, [33 * unit + nz, rows], face, down)
-    (cross,) = call(functools.partial(final_kernel, dims), "final", [VMEM] * 6, [rows], 2_000_000)(
-        small, half, kept, inner, up, share
+    down = moved(stage(lower_kernel, "lower", 20_000_000, [9 * unit + nz // 2], material)[0], "gx", -1)
+    up = moved(stage(upper_kernel, "upper", 20_000_000, [8 * unit + nz // 4], face)[0], "gx", 1)
+    (share,) = stage(share_kernel, "share", 20_000_000, [unit], face, down)
+    count_x, count_src = lax.axis_size("gx"), lax.axis_size("src")
+    own_share = moved(share, "gx", 1)
+    other_share = lax.ppermute(
+        share, ("gx", "src"),
+        [
+            (x * count_src + s, (x + 1) % count_x * count_src + (s + 1) % count_src)
+            for x in range(count_x)
+            for s in range(count_src)
+        ],
     )
-    other = moved(cross, "src", 1)
-    (out,) = call(sum_kernel, "gradient", [VMEM, VMEM], [rows], 500_000)(cross, other)
+    kept, inner = stage(interior_kernel, "interior", 40_000_000, [33 * unit + nz, rows], face, down, share)
+    cross = call(
+        functools.partial(final_kernel, dims), "final", [VMEM] * 5, [nz] * (width_x * tiles), 1_000_000
+    )(small, half, kept, inner, up)
+    other = [moved(value, "src", 1) for value in cross]
+    (out,) = call(
+        functools.partial(sum_kernel, dims), "gradient", [VMEM] * (3 + 2 * len(other)), [rows], 10_000
+    )(half, own_share, other_share, *cross, *other)
     return out.reshape(nz, tiles, width_x, LANES).transpose(0, 2, 1, 3).reshape(nz, width_x, width_y)
 
 

time: 29.5 us -> 28.8 us (0.976)
  waiting for transfers between devices: 14.5 us -> 12.9 us
  starting transfers between devices: 7.81 us -> 8.56 us
    ppermute x6 -> x9, waiting for transfers between devices: 14.5 us -> 12.9 us  [moved(): lax.ppermute(value, axis, [(source, (source + steps) % count) for source...]
    ppermute x6 -> x9, starting transfers between devices: 7.81 us -> 8.5 us  [moved(): lax.ppermute(value, axis, [(source, (source + steps) % count) for source...]
  transfers between devices with their start and end apart: 6 -> 10, of which waited for: 5 -> 9; matrix products, arithmetic and copies ran while one was open for 0% -> 0% of each run, Pallas kernels for 16% -> 18%
where the time goes in v4:
time: 28.8 us; the launch traced here: 28.6 us
  waiting for transfers between devices  12.9 us (45%)
  starting transfers between devices  8.56 us (30%)
  Pallas kernels  7.09 us (25%)
    ppermute x9, waiting for transfers between devices, moved(): lax.ppermute(value, axis, [(source, (source + steps) % count) for source...  12.9 us
    ppermute x9, starting transfers between devices, moved(): lax.ppermute(value, axis, [(source, (source + steps) % count) for source...  8.5 us
    pallas_call x4, Pallas kernels, stage(): call(functools.partial(kernel, dims, two), name, specs + [VMEM] * len(mor...  3.79 us
    pallas_call x1, Pallas kernels, local(): call(functools.partial(face_kernel, dims), 'faces', [HBM], [8 * unit], 10...  1.25 us
    pallas_call x1, Pallas kernels, local(): call(functools.partial(prepare_kernel, dims), 'prepare', [VMEM] * 2 + [SM...  0.67 us
    pallas_call x1, Pallas kernels, local(): call(functools.partial(sum_kernel, dims), 'gradient', [VMEM] * (3 + 2 * l...  0.64 us
  transfers between devices with their start and end apart: 10, of which 9 were waited for; matrix products, arithmetic and copies ran while one was open for 0% of the time, Pallas kernels for 18%

profile of v4, /device:TPU:0, one launch (start us, length us, event | category | flops | bytes accessed | tf_op | source)
XLA Modules:
  0.0 28.6 jit_solution(11613724252071790293)
XLA Ops:
  0.0 0.0 copy-start
  0.0 0.0 copy-start.1
  0.0 0.0 copy-start.2
  0.0 0.0 copy-start.3
  0.0 0.0 copy-start.4
  0.0 0.0 copy-start.5
  0.0 1.3 %faces.1.order_ref = f32[512,128]{1,0:T(8,128)S(1)} custom-call(f32[24,128,128]{2,1,0:T(8,128)} %bitcast.15), custom_call_target="tpu_custom_call" | custom-call | bytes 100000 | tf_op jit(solution)/shard_map/faces/pallas_call | solution.py:559
  1.3 5.1 %collective-permute-start.1 = (f32[512,128]{1,0:T(8,128)S(1)}, f32[512,128]{1,0:T(8,128)S(1)}, u32[]{:S(2)}, u32[]{:S(2)}) collective-permute-start(f32[512,128]{1,0:T(8,128)S(1)} %faces.1.order_ref), channel_id=1, source_target_pairs={{0,12},{4,0},{8,4},{12,8},{1,13},{5,1},{9,5},{13,9},{2,14},{6,2},{... | collective-permute-start | bytes 786440 | tf_op jit(solution)/shard_map/ppermute | solution.py:545
  6.4 0.0 copy-done
  6.4 0.0 copy-done.1
  6.4 0.3 edges.1.order_ref
  6.7 1.6 %collective-permute-start = (f32[64,128]{1,0:T(8,128)S(1)}, f32[64,128]{1,0:T(8,128)S(1)}, u32[]{:S(2)}, u32[]{:S(2)}) collective-permute-start(f32[64,128]{1,0:T(8,128)S(1)} %edges.1.order_ref), channel_id=1, source_target_pairs={{0,2},{2,0},{1,3},{3,1},{4,6},{6,4},{5,7},{7,5},{8,10},{10,8},{9,1... | collective-permute-start | bytes 98312 | tf_op jit(solution)/shard_map/ppermute | solution.py:545
  8.2 0.0 copy-done.2
  8.2 0.0 copy-done.3
  8.2 0.0 copy-done.4
  8.2 0.0 copy-done.5
  8.3 0.7 %prepare.1 = (f32[32,128]{1,0:T(8,128)S(1)}, f32[128,128]{1,0:T(8,128)S(1)}, f32[384,128]{1,0:T(8,128)S(1)}) custom-call(f32[64,128]{1,0:T(8,128)S(1)} %edges.1.order_ref, s32[128,128]{1,0:T(8,128)S(1)} %bitcast.22, f32[8]{0:T(128)S(1)} %copy-done.3, f32[2]{0:T(128)S(1)} %copy-done.4, s32[1,2]{1,0:T(1,128)S(1)} %copy-done.5, f32[1,2,2,2]{3,2,1,0:T(2,128)S(1)} %copy-done.2), custom_call_target="tpu_custom_call" | custom-call | bytes 20000000 | tf_op jit(solution)/shard_map/prepare/pallas_call | solution.py:567
  8.9 1.7 %collective-permute-done.refs_1_.refs_2_ = f32[64,128]{1,0:T(8,128)S(1)} collective-permute-done((f32[64,128]{1,0:T(8,128)S(1)}, f32[64,128]{1,0:T(8,128)S(1)}, u32[]{:S(2)}, u32[]{:S(2)}) %collective-permute-start) | collective-permute-done | bytes 32800 | tf_op jit(solution)/shard_map/ppermute | solution.py:545
  10.7 0.7 %lower.1 = f32[592,128]{1,0:T(8,128)S(1)} custom-call(f32[24,128,128]{2,1,0:T(8,128)S(1)} %bitcast.17, f32[64,128]{1,0:T(8,128)S(1)} %collective-permute-done.refs_1_.refs_2_, f32[64,128]{1,0:T(8,128)S(1)} %collective-permute-done.refs_1_.refs_2_, f32[32,128]{1,0:T(8,128)S(1)} %get-tuple-element.15.refs_3_.small_ref, ...), custom_call_target="tpu_custom_call" | custom-call | bytes 20000000 | tf_op jit(solution)/shard_map/lower/pallas_call | solution.py:579
  11.4 0.5 %collective-permute-start.2 = (f32[592,128]{1,0:T(8,128)S(1)}, f32[592,128]{1,0:T(8,128)S(1)}, u32[]{:S(2)}, u32[]{:S(2)}) collective-permute-start(f32[592,128]{1,0:T(8,128)S(1)} %lower.1), channel_id=1, source_target_pairs={{0,12},{4,0},{8,4},{12,8},{1,13},{5,1},{9,5},{13,9},{2,14},{6,2},{... | collective-permute-start | bytes 909320 | tf_op jit(solution)/shard_map/ppermute | solution.py:545
  11.8 1.3 %collective-permute-done.1.refs_6_ = f32[512,128]{1,0:T(8,128)S(1)} collective-permute-done((f32[512,128]{1,0:T(8,128)S(1)}, f32[512,128]{1,0:T(8,128)S(1)}, u32[]{:S(2)}, u32[]{:S(2)}) %collective-permute-start.1) | collective-permute-done | bytes 262176 | tf_op jit(solution)/shard_map/ppermute | solution.py:545
  13.1 0.3 %upper.1 = f32[520,128]{1,0:T(8,128)S(1)} custom-call(f32[24,128,128]{2,1,0:T(8,128)S(1)} %bitcast.18, f32[64,128]{1,0:T(8,128)S(1)} %collective-permute-done.refs_1_.refs_2_, f32[64,128]{1,0:T(8,128)S(1)} %collective-permute-done.refs_1_.refs_2_, f32[32,128]{1,0:T(8,128)S(1)} %get-tuple-element.15.refs_3_.small_ref, ...), custom_call_target="tpu_custom_call" | custom-call | bytes 20000000 | tf_op jit(solution)/shard_map/upper/pallas_call | solution.py:579
  13.4 0.5 %collective-permute-start.5 = (f32[520,128]{1,0:T(8,128)S(1)}, f32[520,128]{1,0:T(8,128)S(1)}, u32[]{:S(2)}, u32[]{:S(2)}) collective-permute-start(f32[520,128]{1,0:T(8,128)S(1)} %upper.1), channel_id=1, source_target_pairs={{0,4},{4,8},{8,12},{12,0},{1,5},{5,9},{9,13},{13,1},{2,6},{6,10},{... | collective-permute-start | bytes 798728 | tf_op jit(solution)/shard_map/ppermute | solution.py:545
  13.9 6.2 %collective-permute-done.2.refs_7_ = f32[592,128]{1,0:T(8,128)S(1)} collective-permute-done((f32[592,128]{1,0:T(8,128)S(1)}, f32[592,128]{1,0:T(8,128)S(1)}, u32[]{:S(2)}, u32[]{:S(2)}) %collective-permute-start.2) | collective-permute-done | bytes 303136 | tf_op jit(solution)/shard_map/ppermute | solution.py:545
  20.2 0.9 %share.1.refs_8_ = f32[64,128]{1,0:T(8,128)S(1)} custom-call(f32[24,128,128]{2,1,0:T(8,128)S(1)} %bitcast.19, f32[64,128]{1,0:T(8,128)S(1)} %collective-permute-done.refs_1_.refs_2_, f32[64,128]{1,0:T(8,128)S(1)} %collective-permute-done.refs_1_.refs_2_, f32[32,128]{1,0:T(8,128)S(1)} %get-tuple-element.15.refs_3_.small_ref, ...), custom_call_target="tpu_custom_call" | custom-call | bytes 20000000 | tf_op jit(solution)/shard_map/share/pallas_call | solution.py:579
  21.0 0.1 collective-permute-start.3
  21.1 0.1 collective-permute-start.4
  21.2 1.9 %interior.1 = (f32[2144,128]{1,0:T(8,128)S(1)}, f32[128,128]{1,0:T(8,128)S(1)}) custom-call(f32[24,128,128]{2,1,0:T(8,128)S(1)} %bitcast.20, f32[64,128]{1,0:T(8,128)S(1)} %collective-permute-done.refs_1_.refs_2_, f32[64,128]{1,0:T(8,128)S(1)} %collective-permute-done.refs_1_.refs_2_, f32[32,128]{1,0:T(8,128)S(1)} %get-tuple-element.15.refs_3_.small_ref, ...), custom_call_target="tpu_custom_call" | custom-call | bytes 40000000 | tf_op jit(solution)/shard_map/interior/pallas_call | solution.py:579
  23.1 2.4 %collective-permute-done.5.up_ref = f32[520,128]{1,0:T(8,128)S(1)} collective-permute-done((f32[520,128]{1,0:T(8,128)S(1)}, f32[520,128]{1,0:T(8,128)S(1)}, u32[]{:S(2)}, u32[]{:S(2)}) %collective-permute-start.5) | collective-permute-done | bytes 266272 | tf_op jit(solution)/shard_map/ppermute | solution.py:545
  25.4 0.5 %final.1 = (f32[32,128]{1,0:T(8,128)S(1)}, f32[32,128]{1,0:T(8,128)S(1)}, f32[32,128]{1,0:T(8,128)S(1)}, f32[32,128]{1,0:T(8,128)S(1)}) custom-call(f32[32,128]{1,0:T(8,128)S(1)} %get-tuple-element.15.refs_3_.small_ref, f32[128,128]{1,0:T(8,128)S(1)} %get-tuple-element.14.refs_4_.half_ref, f32[2144,128]{1,0:T(8,128)S(1)} %get-tuple-element.17.kept_ref, ...), custom_call_target="tpu_custom_call" | custom-call | bytes 1000000 | tf_op jit(solution)/shard_map/final/pallas_call | solution.py:597
  25.9 0.1 collective-permute-start.6
  26.0 0.5 %collective-permute-start.7 = (f32[32,128]{1,0:T(8,128)S(1)}, f32[32,128]{1,0:T(8,128)S(1)}, u32[]{:S(2)}, u32[]{:S(2)}) collective-permute-start(f32[32,128]{1,0:T(8,128)S(1)} %get-tuple-element.20.refs_1_), channel_id=1, source_target_pairs={{0,1},{1,0},{2,3},{3,2},{4,5},{5,4},{6,7},{7,6},{8,9},{9,8},{10,11... | collective-permute-start | bytes 49160 | tf_op jit(solution)/shard_map/ppermute | solution.py:545
  26.5 0.1 collective-permute-start.8
  26.5 0.3 collective-permute-done.3.own_share_ref
  26.8 0.2 collective-permute-start.9
  27.0 0.0 collective-permute-done.4.other_share_ref
  27.0 0.2 collective-permute-done.6.refs_4_
  27.1 0.2 collective-permute-done.7.refs_5_
  27.3 0.3 %collective-permute-done.8.refs_6_ = f32[32,128]{1,0:T(8,128)S(1)} collective-permute-done((f32[32,128]{1,0:T(8,128)S(1)}, f32[32,128]{1,0:T(8,128)S(1)}, u32[]{:S(2)}, u32[]{:S(2)}) %collective-permute-start.8) | collective-permute-done | bytes 16416 | tf_op jit(solution)/shard_map/ppermute | solution.py:545
  27.6 0.3 %collective-permute-done.9.refs_7_ = f32[32,128]{1,0:T(8,128)S(1)} collective-permute-done((f32[32,128]{1,0:T(8,128)S(1)}, f32[32,128]{1,0:T(8,128)S(1)}, u32[]{:S(2)}, u32[]{:S(2)}) %collective-permute-start.9) | collective-permute-done | bytes 16416 | tf_op jit(solution)/shard_map/ppermute | solution.py:545
  28.0 0.6 %gradient.1 = f32[128,128]{1,0:T(8,128)} custom-call(f32[128,128]{1,0:T(8,128)S(1)} %get-tuple-element.14.refs_4_.half_ref, f32[64,128]{1,0:T(8,128)S(1)} %collective-permute-done.3.own_share_ref, f32[64,128]{1,0:T(8,128)S(1)} %collective-permute-done.4.other_share_ref, f32[32,128]{1,0:T(8,128)S(1)} %get-tuple-element.19.refs_0_, ...), custom_call_target="tpu_custom_call" | custom-call | bytes 10000 | tf_op jit(solution)/shard_map/gradient/pallas_call | solution.py:601
Async XLA Ops:
  0.0 6.4 %copy-start = (f32[1,2,2,6,32,2,256]{6,5,4,3,2,1,0:T(2,128)S(1)}, f32[1,2,2,6,32,2,256]{6,5,4,3,2,1,0:T(2,128)}, u32[]{:S(2)}) copy-start(f32[1,2,2,6,32,2,256]{6,5,4,3,2,1,0:T(2,128)} %param.6) | copy-start | bytes 4718596
  0.0 6.4 %copy-start.1 = (s32[32,2,256]{2,1,0:T(2,128)S(1)}, s32[32,2,256]{2,1,0:T(2,128)}, u32[]{:S(2)}) copy-start(s32[32,2,256]{2,1,0:T(2,128)} %param.7) | copy-start | bytes 196612
  0.0 8.2 %copy-start.2 = (f32[1,2,2,2]{3,2,1,0:T(2,128)S(1)}, f32[1,2,2,2]{3,2,1,0:T(2,128)}, u32[]{:S(2)}) copy-start(f32[1,2,2,2]{3,2,1,0:T(2,128)} %wave_ref.1) | copy-start | bytes 100
  0.0 8.2 %copy-start.3 = (f32[8]{0:T(128)S(1)}, f32[8]{0:T(128)}, u32[]{:S(2)}) copy-start(f32[8]{0:T(128)} %table_ref.1) | copy-start | bytes 100
  0.0 8.2 %copy-start.4 = (f32[2]{0:T(128)S(1)}, f32[2]{0:T(128)}, u32[]{:S(2)}) copy-start(f32[2]{0:T(128)} %phase_ref.1) | copy-start | bytes 28
  0.0 8.2 %copy-start.5 = (s32[1,2]{1,0:T(1,128)S(1)}, s32[1,2]{1,0:T(1,128)}, u32[]{:S(2)}) copy-start(s32[1,2]{1,0:T(1,128)} %cells_ref.1) | copy-start | bytes 28
  1.3 11.8 %collective-permute-start.1 = (f32[512,128]{1,0:T(8,128)S(1)}, f32[512,128]{1,0:T(8,128)S(1)}, u32[]{:S(2)}, u32[]{:S(2)}) collective-permute-start(f32[512,128]{1,0:T(8,128)S(1)} %faces.1.order_ref), channel_id=1, source_target_pairs={{0,12},{4,0},{8,4},{12,8},{1,13},{5,1},{9,5},{13,9},{2,14},{6,2},{... | collective-permute-start | bytes 786440 | tf_op jit(solution)/shard_map/ppermute | solution.py:545
  6.7 4.0 %collective-permute-start = (f32[64,128]{1,0:T(8,128)S(1)}, f32[64,128]{1,0:T(8,128)S(1)}, u32[]{:S(2)}, u32[]{:S(2)}) collective-permute-start(f32[64,128]{1,0:T(8,128)S(1)} %edges.1.order_ref), channel_id=1, source_target_pairs={{0,2},{2,0},{1,3},{3,1},{4,6},{6,4},{5,7},{7,5},{8,10},{10,8},{9,1... | collective-permute-start | bytes 98312 | tf_op jit(solution)/shard_map/ppermute | solution.py:545
  11.4 8.8 %collective-permute-start.2 = (f32[592,128]{1,0:T(8,128)S(1)}, f32[592,128]{1,0:T(8,128)S(1)}, u32[]{:S(2)}, u32[]{:S(2)}) collective-permute-start(f32[592,128]{1,0:T(8,128)S(1)} %lower.1), channel_id=1, source_target_pairs={{0,12},{4,0},{8,4},{12,8},{1,13},{5,1},{9,5},{13,9},{2,14},{6,2},{... | collective-permute-start | bytes 909320 | tf_op jit(solution)/shard_map/ppermute | solution.py:545
  13.4 12.0 %collective-permute-start.5 = (f32[520,128]{1,0:T(8,128)S(1)}, f32[520,128]{1,0:T(8,128)S(1)}, u32[]{:S(2)}, u32[]{:S(2)}) collective-permute-start(f32[520,128]{1,0:T(8,128)S(1)} %upper.1), channel_id=1, source_target_pairs={{0,4},{4,8},{8,12},{12,0},{1,5},{5,9},{9,13},{13,1},{2,6},{6,10},{... | collective-permute-start | bytes 798728 | tf_op jit(solution)/shard_map/ppermute | solution.py:545
  21.0 5.8 %collective-permute-start.3 = (f32[64,128]{1,0:T(8,128)S(1)}, f32[64,128]{1,0:T(8,128)S(1)}, u32[]{:S(2)}, u32[]{:S(2)}) collective-permute-start(f32[64,128]{1,0:T(8,128)S(1)} %share.1.refs_8_), channel_id=1, source_target_pairs={{0,4},{4,8},{8,12},{12,0},{1,5},{5,9},{9,13},{13,1},{2,6},{6,10},{... | collective-permute-start | bytes 98312 | tf_op jit(solution)/shard_map/ppermute | solution.py:545
  21.1 5.9 %collective-permute-start.4 = (f32[64,128]{1,0:T(8,128)S(1)}, f32[64,128]{1,0:T(8,128)S(1)}, u32[]{:S(2)}, u32[]{:S(2)}) collective-permute-start(f32[64,128]{1,0:T(8,128)S(1)} %share.1.refs_8_), channel_id=1, source_target_pairs={{0,5},{1,4},{4,9},{5,8},{8,13},{9,12},{12,1},{13,0},{2,7},{3,6},{6... | collective-permute-start | bytes 98312 | tf_op jit(solution)/shard_map/ppermute | solution.py:588
  25.9 1.2 %collective-permute-start.6 = (f32[32,128]{1,0:T(8,128)S(1)}, f32[32,128]{1,0:T(8,128)S(1)}, u32[]{:S(2)}, u32[]{:S(2)}) collective-permute-start(f32[32,128]{1,0:T(8,128)S(1)} %get-tuple-element.19.refs_0_), channel_id=1, source_target_pairs={{0,1},{1,0},{2,3},{3,2},{4,5},{5,4},{6,7},{7,6},{8,9},{9,8},{10,11... | collective-permute-start | bytes 49160 | tf_op jit(solution)/shard_map/ppermute | solution.py:545
  26.0 1.3 %collective-permute-start.7 = (f32[32,128]{1,0:T(8,128)S(1)}, f32[32,128]{1,0:T(8,128)S(1)}, u32[]{:S(2)}, u32[]{:S(2)}) collective-permute-start(f32[32,128]{1,0:T(8,128)S(1)} %get-tuple-element.20.refs_1_), channel_id=1, source_target_pairs={{0,1},{1,0},{2,3},{3,2},{4,5},{5,4},{6,7},{7,6},{8,9},{9,8},{10,11... | collective-permute-start | bytes 49160 | tf_op jit(solution)/shard_map/ppermute | solution.py:545
  26.5 1.2 %collective-permute-start.8 = (f32[32,128]{1,0:T(8,128)S(1)}, f32[32,128]{1,0:T(8,128)S(1)}, u32[]{:S(2)}, u32[]{:S(2)}) collective-permute-start(f32[32,128]{1,0:T(8,128)S(1)} %get-tuple-element.21.refs_2_), channel_id=1, source_target_pairs={{0,1},{1,0},{2,3},{3,2},{4,5},{5,4},{6,7},{7,6},{8,9},{9,8},{10,11... | collective-permute-start | bytes 49160 | tf_op jit(solution)/shard_map/ppermute | solution.py:545
  26.8 1.2 %collective-permute-start.9 = (f32[32,128]{1,0:T(8,128)S(1)}, f32[32,128]{1,0:T(8,128)S(1)}, u32[]{:S(2)}, u32[]{:S(2)}) collective-permute-start(f32[32,128]{1,0:T(8,128)S(1)} %get-tuple-element.22.refs_3_), channel_id=1, source_target_pairs={{0,1},{1,0},{2,3},{3,2},{4,5},{5,4},{6,7},{7,6},{8,9},{9,8},{10,11... | collective-permute-start | bytes 49160 | tf_op jit(solution)/shard_map/ppermute | solution.py:545

commit v5 on v4

--- a/solution.py
+++ b/solution.py
@@ -346,9 +346,40 @@
     return [COURANT * inverse_eps(value, levels) for value in own + [pltpu.roll(edge, MATERIAL_MOVE, 1)]]
 
 
+def wide(ref, unit, nz, count):
+    return [ref[(unit * count + t) * nz:(unit * count + t + 1) * nz, :] for t in range(count)]
+
+
+def early_kernel(dims, two, *refs):
+    nz, width_x, tiles = dims
+    *given, _, early_ref, edge_ref = refs
+    local = started(dims, two, *given, edge_ref)
+    every = range(tiles + 1)
+    half = [local.half(x) for x in range(width_x - 1)]
+    for run in range(2):
+        sources = [local.source(run, 0, x) for x in range(width_x - 1)]
+        fields = [[local.load(run, comp, x) for x in range(width_x - 1)] for comp in range(6)]
+        highest = [local.load(run, comp, width_x - 1) for comp in (1, 2)]
+        for part in range(2):
+            pair = run * 2 + part
+            under_y = [COURANT * value for value in fields[2][0][part]]
+            under_z = [-COURANT * value for value in fields[1][0][part]]
+            for x in range(width_x - 1):
+                ex, ey, ez, hx, hy, hz = [fields[comp][x][part] for comp in range(6)]
+                if x < width_x - 2:
+                    ey_x, ez_x = fields[1][x + 1][part], fields[2][x + 1][part]
+                else:
+                    ey_x, ez_x = highest[0][part], highest[1][part]
+                hx, hy, hz = small_steps(local, ex, ey, ez, hx, hy, hz, ey_x, ez_x)
+                new = grown(local, ex, ey, ez, hx, hy, hz, under_y, under_z, half[x], sources[x][part], tiles + 1)
+                for comp, value in enumerate((*new, hx, hy, hz)):
+                    store_tiles(early_ref, (pair * (width_x - 1) + x) * 6 + comp, value, tiles + 1, nz)
+                under_y, under_z = hy, hz
+
+
 def share_kernel(dims, two, *refs):
     nz, width_x, tiles = dims
-    *given, face_ref, down_ref, share_ref, edge_ref = refs
+    *given, face_ref, down_ref, early_ref, share_ref, high_ref, edge_ref = refs
     local = started(dims, two, *given, edge_ref)
     edge = unfolded(down_ref[9 * tiles * nz:, :], 64)
     half = local.half(width_x - 1)
@@ -356,15 +387,15 @@
     kept_e, kept_h = {}, {}
     every = range(tiles + 1)
     for run in range(2):
-        low = [local.load(run, comp, width_x - 2) for comp in range(6)]
         high = [local.load(run, comp, width_x - 1) for comp in range(6)]
         source = local.source(run, 0, width_x - 1)
         early = [halo(local, face_ref, edge, 0, run, which, AHEAD) for which in range(2)]
         later = [halo(local, down_ref, edge, 8, run, which, AHEAD) for which in range(2)]
         for part in range(2):
+            pair = run * 2 + part
             ex, ey, ez, hx, hy, hz = [high[comp][part] for comp in range(6)]
-            low_x, low_y, low_z, _, low_hy, low_hz = [low[comp][part] for comp in range(6)]
-            _, low_hy, low_hz = small_steps(local, low_x, low_y, low_z, None, low_hy, low_hz, ey, ez)
+            low = (pair * (width_x - 1) + width_x - 2) * 6
+            low_hy, low_hz = [wide(early_ref, low + comp, nz, tiles + 1) for comp in (4, 5)]
             hx, hy, hz = small_steps(local, ex, ey, ez, hx, hy, hz, early[0][part], early[1][part])
             ex, ey, ez = grown(local, ex, ey, ez, hx, hy, hz, low_hy, low_hz, half, source[part], tiles + 1)
             above_y = [later[0][part][t] + above[t] * hz[t] for t in every]
@@ -372,6 +403,8 @@
             _, hy, hz = small_steps(local, ex, ey, ez, None, hy, hz, above_y, above_z)
             kept_e[run, part] = (above_y, above_z)
             kept_h[run, part] = (hy, hz)
+            for comp, value in enumerate((ex, ey, ez, hx, hy, hz)):
+                store_tiles(high_ref, pair * 6 + comp, value, tiles + 1, nz)
     for t in range(tiles):
         total = 0.0
         for run in range(2):
@@ -394,43 +427,34 @@
 
 def interior_kernel(dims, two, *refs):
     nz, width_x, tiles = dims
-    *given, face_ref, down_ref, _, kept_ref, cross_ref, edge_ref = refs
+    *given, early_ref, high_ref, _, kept_ref, cross_ref, edge_ref = refs
     local = started(dims, two, *given, edge_ref)
+    shifts = local.shifts
     every, own, layers = range(tiles + 1), range(tiles), range(width_x)
-    edge = unfolded(down_ref[9 * tiles * nz:, :], 64)
     half = [local.half(x) for x in layers]
-    above = half_above(local, down_ref, edge)
     kept_one, kept_two = {}, {}
     for run in range(2):
-        sources = [[local.source(run, step, x) for x in layers] for step in range(2)]
-        fields = [[local.load(run, comp, x) for x in layers] for comp in range(6)]
-        early = [halo(local, face_ref, edge, 0, run, which, AHEAD) for which in range(2)]
-        later = [halo(local, down_ref, edge, 8, run, which, AHEAD) for which in range(2)]
+        sources = [local.source(run, 1, x) for x in layers]
         for part in range(2):
-            ex, ey, ez, hx, hy, hz = [[fields[comp][x][part] for x in layers] for comp in range(6)]
-            under_y = [COURANT * ez[0][t] for t in every]
-            under_z = [-COURANT * ey[0][t] for t in every]
-            above_y, above_z = early[0][part], early[1][part]
-            for step in range(2):
-                ey_x, ez_x = ey[1:] + [above_y], ez[1:] + [above_z]
-                for x in layers:
-                    hx[x], hy[x], hz[x] = small_steps(
-                        local, ex[x], ey[x], ez[x], hx[x], hy[x], hz[x], ey_x[x], ez_x[x]
-                    )
-                if step == 0:
-                    above_y = [later[0][part][t] + above[t] * hz[-1][t] for t in every]
-                    above_z = [later[1][part][t] - above[t] * hy[-1][t] for t in every]
+            pair = run * 2 + part
+            fields = []
+            for x in range(width_x - 1):
+                first = (pair * (width_x - 1) + x) * 6
+                fields.append([wide(early_ref, first + comp, nz, tiles + 1) for comp in range(6)])
+            fields.append([wide(high_ref, pair * 6 + comp, nz, tiles + 1) for comp in range(6)])
+            hy_x, hz_x = None, None
+            for x in layers:
+                ex, ey, ez, hx, hy, hz = fields[x]
+                if x < width_x - 1:
+                    hx, hy, hz = small_steps(local, ex, ey, ez, hx, hy, hz, fields[x + 1][1], fields[x + 1][2])
                 else:
-                    under_y, under_z = None, None
-                for x in layers:
-                    hy_x, hz_x = (under_y, under_z) if x == 0 else (hy[x - 1], hz[x - 1])
-                    ex[x], ey[x], ez[x] = grown(
-                        local, ex[x], ey[x], ez[x], hx[x], hy[x], hz[x], hy_x, hz_x, half[x], sources[step][x][part],
-                        tiles if step else tiles + 1,
-                    )
-                for x in layers:
-                    for comp, value in enumerate((ex[x], ey[x], ez[x])):
-                        (kept_two if step else kept_one).setdefault((comp, x), {})[run, part] = value
+                    ez_y = shifts.y_up(ez)
+                    hx = [hx[t] - COURANT * (ez_y[t] - ez[t] - (shifts.z_up(ey[t]) - ey[t])) for t in every]
+                new = grown(local, ex, ey, ez, hx, hy, hz, hy_x, hz_x, half[x], sources[x][part], tiles)
+                hy_x, hz_x = hy, hz
+                for comp in range(3):
+                    kept_one.setdefault((comp, x), {})[run, part] = fields[x][comp]
+                    kept_two.setdefault((comp, x), {})[run, part] = new[comp]
     for pair in range(4):
         where = (pair // 2, pair % 2)
         for comp in range(3):
@@ -501,19 +525,17 @@
                     total = total - next_half[t] * (
                         both(next_one[1], next_add[1], t) + both(next_one[2], next_add[2], t)
                     )
-            cross_refs[x * tiles + t][...] = total
+            cross_refs[x][t * nz:(t + 1) * nz, :] = total
 
 
 def sum_kernel(dims, half_ref, own_share_ref, other_share_ref, *refs):
     nz, width_x, tiles = dims
     *parts, out_ref = refs
-    count = width_x * tiles
     for x in range(width_x):
         for t in range(tiles):
-            index = x * tiles + t
-            total = parts[index][...] + parts[count + index][...]
+            span = slice(t * nz, (t + 1) * nz)
+            total = parts[x][span, :] + parts[width_x + x][span, :]
             if x == 0:
-                span = slice(t * nz, (t + 1) * nz)
                 total = total - half_ref[span, :] * (own_share_ref[span, :] + other_share_ref[span, :])
             out_ref[pl.ds(t * width_x + x, nz, stride=tiles * width_x), :] = total
 
@@ -582,7 +604,9 @@
 
     down = moved(stage(lower_kernel, "lower", 20_000_000, [9 * unit + nz // 2], material)[0], "gx", -1)
     up = moved(stage(upper_kernel, "upper", 20_000_000, [8 * unit + nz // 4], face)[0], "gx", 1)
-    (share,) = stage(share_kernel, "share", 20_000_000, [unit], face, down)
+    wide_unit = (tiles + 1) * nz
+    (early,) = stage(early_kernel, "early", 20_000_000, [24 * (width_x - 1) * wide_unit], face)
+    share, high = stage(share_kernel, "share", 20_000_000, [unit, 24 * wide_unit], face, down, early)
     count_x, count_src = lax.axis_size("gx"), lax.axis_size("src")
     own_share = moved(share, "gx", 1)
     other_share = lax.ppermute(
@@ -593,9 +617,9 @@
             for s in range(count_src)
         ],
     )
-    kept, inner = stage(interior_kernel, "interior", 40_000_000, [33 * unit + nz, rows], face, down, share)
+    kept, inner = stage(interior_kernel, "interior", 40_000_000, [33 * unit + nz, rows], early, high, share)
     cross = call(
-        functools.partial(final_kernel, dims), "final", [VMEM] * 5, [nz] * (width_x * tiles), 1_000_000
+        functools.partial(final_kernel, dims), "final", [VMEM] * 5, [unit] * width_x, 1_000_000
     )(small, half, kept, inner, up)
     other = [moved(value, "src", 1) for value in cross]
     (out,) = call(

time: 28.8 us -> 28.1 us (0.976)
  Pallas kernels: 7.09 us -> 6.63 us
    pallas_call x4 -> x5, Pallas kernels: 3.79 us -> 3.37 us  [stage(): call(functools.partial(kernel, dims, two), name, specs + [VMEM] * len(mor...]
    ppermute x9 -> x7, starting transfers between devices: 8.5 us -> 8.24 us  [moved(): lax.ppermute(value, axis, [(source, (source + steps) % count) for source...]
    ppermute x9 -> x7, waiting for transfers between devices: 12.9 us -> 12.9 us  [moved(): lax.ppermute(value, axis, [(source, (source + steps) % count) for source...]
  transfers between devices with their start and end apart: 10 -> 8, of which waited for: 9 -> 7; matrix products, arithmetic and copies ran while one was open for 0% -> 0% of each run, Pallas kernels for 18% -> 17%
where the time goes in v5:
time: 28.1 us; the launch traced here: 27.9 us
  waiting for transfers between devices  12.9 us (46%)
  starting transfers between devices  8.3 us (30%)
  Pallas kernels  6.63 us (24%)
    ppermute x7, waiting for transfers between devices, moved(): lax.ppermute(value, axis, [(source, (source + steps) % count) for source...  12.9 us
    ppermute x7, starting transfers between devices, moved(): lax.ppermute(value, axis, [(source, (source + steps) % count) for source...  8.24 us
    pallas_call x5, Pallas kernels, stage(): call(functools.partial(kernel, dims, two), name, specs + [VMEM] * len(mor...  3.37 us
    pallas_call x1, Pallas kernels, local(): call(functools.partial(face_kernel, dims), 'faces', [HBM], [8 * unit], 10...  1.25 us
    pallas_call x1, Pallas kernels, local(): call(functools.partial(prepare_kernel, dims), 'prepare', [VMEM] * 2 + [SM...  0.67 us
    pallas_call x1, Pallas kernels, local(): call(functools.partial(sum_kernel, dims), 'gradient', [VMEM] * (3 + 2 * l...  0.64 us
  transfers between devices with their start and end apart: 8, of which 7 were waited for; matrix products, arithmetic and copies ran while one was open for 0% of the time, Pallas kernels for 17%

profile of v5, /device:TPU:0, one launch (start us, length us, event | category | flops | bytes accessed | tf_op | source)
XLA Modules:
  0.0 27.9 jit_solution(15434603671509972052)
XLA Ops:
  0.0 0.0 copy-start
  0.0 0.0 copy-start.1
  0.0 1.3 %faces.1.order_ref = f32[512,128]{1,0:T(8,128)S(1)} custom-call(f32[24,128,128]{2,1,0:T(8,128)} %bitcast.15), custom_call_target="tpu_custom_call" | custom-call | bytes 100000 | tf_op jit(solution)/shard_map/faces/pallas_call | solution.py:581
  1.3 0.0 copy-start.2
  1.3 0.0 copy-start.3
  1.3 0.0 copy-start.4
  1.3 0.0 copy-start.5
  1.3 5.1 %collective-permute-start.1 = (f32[512,128]{1,0:T(8,128)S(1)}, f32[512,128]{1,0:T(8,128)S(1)}, u32[]{:S(2)}, u32[]{:S(2)}) collective-permute-start(f32[512,128]{1,0:T(8,128)S(1)} %faces.1.order_ref), channel_id=1, source_target_pairs={{0,12},{4,0},{8,4},{12,8},{1,13},{5,1},{9,5},{13,9},{2,14},{6,2},{... | collective-permute-start | bytes 786440 | tf_op jit(solution)/shard_map/ppermute | solution.py:567
  6.4 0.0 copy-done
  6.4 0.0 copy-done.1
  6.4 0.3 edges.1.order_ref
  6.7 1.6 %collective-permute-start = (f32[64,128]{1,0:T(8,128)S(1)}, f32[64,128]{1,0:T(8,128)S(1)}, u32[]{:S(2)}, u32[]{:S(2)}) collective-permute-start(f32[64,128]{1,0:T(8,128)S(1)} %edges.1.order_ref), channel_id=1, source_target_pairs={{0,2},{2,0},{1,3},{3,1},{4,6},{6,4},{5,7},{7,5},{8,10},{10,8},{9,1... | collective-permute-start | bytes 98312 | tf_op jit(solution)/shard_map/ppermute | solution.py:567
  8.3 0.0 copy-done.2
  8.3 0.0 copy-done.3
  8.3 0.0 copy-done.4
  8.3 0.0 copy-done.5
  8.3 0.7 %prepare.1 = (f32[32,128]{1,0:T(8,128)S(1)}, f32[128,128]{1,0:T(8,128)S(1)}, f32[384,128]{1,0:T(8,128)S(1)}) custom-call(f32[64,128]{1,0:T(8,128)S(1)} %edges.1.order_ref, s32[128,128]{1,0:T(8,128)S(1)} %bitcast.23, f32[8]{0:T(128)S(1)} %copy-done.3, f32[2]{0:T(128)S(1)} %copy-done.4, s32[1,2]{1,0:T(1,128)S(1)} %copy-done.5, f32[1,2,2,2]{3,2,1,0:T(2,128)S(1)} %copy-done.2), custom_call_target="tpu_custom_call" | custom-call | bytes 20000000 | tf_op jit(solution)/shard_map/prepare/pallas_call | solution.py:589
  9.0 1.7 %collective-permute-done.refs_1_.refs_2_ = f32[64,128]{1,0:T(8,128)S(1)} collective-permute-done((f32[64,128]{1,0:T(8,128)S(1)}, f32[64,128]{1,0:T(8,128)S(1)}, u32[]{:S(2)}, u32[]{:S(2)}) %collective-permute-start) | collective-permute-done | bytes 32800 | tf_op jit(solution)/shard_map/ppermute | solution.py:567
  10.7 0.7 %lower.1 = f32[592,128]{1,0:T(8,128)S(1)} custom-call(f32[24,128,128]{2,1,0:T(8,128)S(1)} %bitcast.17, f32[64,128]{1,0:T(8,128)S(1)} %collective-permute-done.refs_1_.refs_2_, f32[64,128]{1,0:T(8,128)S(1)} %collective-permute-done.refs_1_.refs_2_, f32[32,128]{1,0:T(8,128)S(1)} %get-tuple-element.15.refs_3_.small_ref, ...), custom_call_target="tpu_custom_call" | custom-call | bytes 20000000 | tf_op jit(solution)/shard_map/lower/pallas_call | solution.py:601
  11.4 0.5 %collective-permute-start.2 = (f32[592,128]{1,0:T(8,128)S(1)}, f32[592,128]{1,0:T(8,128)S(1)}, u32[]{:S(2)}, u32[]{:S(2)}) collective-permute-start(f32[592,128]{1,0:T(8,128)S(1)} %lower.1), channel_id=1, source_target_pairs={{0,12},{4,0},{8,4},{12,8},{1,13},{5,1},{9,5},{13,9},{2,14},{6,2},{... | collective-permute-start | bytes 909320 | tf_op jit(solution)/shard_map/ppermute | solution.py:567
  11.9 1.3 %collective-permute-done.1.refs_6_ = f32[512,128]{1,0:T(8,128)S(1)} collective-permute-done((f32[512,128]{1,0:T(8,128)S(1)}, f32[512,128]{1,0:T(8,128)S(1)}, u32[]{:S(2)}, u32[]{:S(2)}) %collective-permute-start.1) | collective-permute-done | bytes 262176 | tf_op jit(solution)/shard_map/ppermute | solution.py:567
  13.1 0.3 %upper.1 = f32[520,128]{1,0:T(8,128)S(1)} custom-call(f32[24,128,128]{2,1,0:T(8,128)S(1)} %bitcast.18, f32[64,128]{1,0:T(8,128)S(1)} %collective-permute-done.refs_1_.refs_2_, f32[64,128]{1,0:T(8,128)S(1)} %collective-permute-done.refs_1_.refs_2_, f32[32,128]{1,0:T(8,128)S(1)} %get-tuple-element.15.refs_3_.small_ref, ...), custom_call_target="tpu_custom_call" | custom-call | bytes 20000000 | tf_op jit(solution)/shard_map/upper/pallas_call | solution.py:601
  13.5 0.5 %collective-permute-start.5 = (f32[520,128]{1,0:T(8,128)S(1)}, f32[520,128]{1,0:T(8,128)S(1)}, u32[]{:S(2)}, u32[]{:S(2)}) collective-permute-start(f32[520,128]{1,0:T(8,128)S(1)} %upper.1), channel_id=1, source_target_pairs={{0,4},{4,8},{8,12},{12,0},{1,5},{5,9},{9,13},{13,1},{2,6},{6,10},{... | collective-permute-start | bytes 798728 | tf_op jit(solution)/shard_map/ppermute | solution.py:567
  13.9 0.7 %early.1.refs_8_.refs_6_ = f32[2304,128]{1,0:T(8,128)S(1)} custom-call(f32[24,128,128]{2,1,0:T(8,128)S(1)} %bitcast.19, f32[64,128]{1,0:T(8,128)S(1)} %collective-permute-done.refs_1_.refs_2_, f32[64,128]{1,0:T(8,128)S(1)} %collective-permute-done.refs_1_.refs_2_, f32[32,128]{1,0:T(8,128)S(1)} %get-tuple-element.15.refs_3_.small_ref, ...), custom_call_target="tpu_custom_call" | custom-call | bytes 20000000 | tf_op jit(solution)/shard_map/early/pallas_call | solution.py:601
  14.6 5.6 %collective-permute-done.2.refs_7_ = f32[592,128]{1,0:T(8,128)S(1)} collective-permute-done((f32[592,128]{1,0:T(8,128)S(1)}, f32[592,128]{1,0:T(8,128)S(1)}, u32[]{:S(2)}, u32[]{:S(2)}) %collective-permute-start.2) | collective-permute-done | bytes 303136 | tf_op jit(solution)/shard_map/ppermute | solution.py:567
  20.2 0.9 %share.1 = (f32[64,128]{1,0:T(8,128)S(1)}, f32[2304,128]{1,0:T(8,128)S(1)}) custom-call(f32[24,128,128]{2,1,0:T(8,128)S(1)} %bitcast.20, f32[64,128]{1,0:T(8,128)S(1)} %collective-permute-done.refs_1_.refs_2_, f32[64,128]{1,0:T(8,128)S(1)} %collective-permute-done.refs_1_.refs_2_, f32[32,128]{1,0:T(8,128)S(1)} %get-tuple-element.15.refs_3_.small_ref, ...), custom_call_target="tpu_custom_call" | custom-call | bytes 20000000 | tf_op jit(solution)/shard_map/share/pallas_call | solution.py:601
  21.0 0.1 collective-permute-start.3
  21.1 0.1 collective-permute-start.4
  21.2 0.8 %interior.1 = (f32[2144,128]{1,0:T(8,128)S(1)}, f32[128,128]{1,0:T(8,128)S(1)}) custom-call(f32[24,128,128]{2,1,0:T(8,128)S(1)} %bitcast.21, f32[64,128]{1,0:T(8,128)S(1)} %collective-permute-done.refs_1_.refs_2_, f32[64,128]{1,0:T(8,128)S(1)} %collective-permute-done.refs_1_.refs_2_, f32[32,128]{1,0:T(8,128)S(1)} %get-tuple-element.15.refs_3_.small_ref, ...), custom_call_target="tpu_custom_call" | custom-call | bytes 40000000 | tf_op jit(solution)/shard_map/interior/pallas_call | solution.py:601
  22.0 3.5 %collective-permute-done.5.up_ref = f32[520,128]{1,0:T(8,128)S(1)} collective-permute-done((f32[520,128]{1,0:T(8,128)S(1)}, f32[520,128]{1,0:T(8,128)S(1)}, u32[]{:S(2)}, u32[]{:S(2)}) %collective-permute-start.5) | collective-permute-done | bytes 266272 | tf_op jit(solution)/shard_map/ppermute | solution.py:567
  25.4 0.4 %final.1 = (f32[64,128]{1,0:T(8,128)S(1)}, f32[64,128]{1,0:T(8,128)S(1)}) custom-call(f32[32,128]{1,0:T(8,128)S(1)} %get-tuple-element.15.refs_3_.small_ref, f32[128,128]{1,0:T(8,128)S(1)} %get-tuple-element.14.refs_4_.half_ref, f32[2144,128]{1,0:T(8,128)S(1)} %get-tuple-element.19.kept_ref, f32[128,128]{1,0:T(8,128)S(1)} %get-tuple-element.20.inner_ref, ...), custom_call_target="tpu_custom_call" | custom-call | bytes 1000000 | tf_op jit(solution)/shard_map/final/pallas_call | solution.py:621
  25.9 0.1 collective-permute-start.6
  25.9 0.5 %collective-permute-start.7 = (f32[64,128]{1,0:T(8,128)S(1)}, f32[64,128]{1,0:T(8,128)S(1)}, u32[]{:S(2)}, u32[]{:S(2)}) collective-permute-start(f32[64,128]{1,0:T(8,128)S(1)} %get-tuple-element.22.refs_1_), channel_id=1, source_target_pairs={{0,1},{1,0},{2,3},{3,2},{4,5},{5,4},{6,7},{7,6},{8,9},{9,8},{10,11... | collective-permute-start | bytes 98312 | tf_op jit(solution)/shard_map/ppermute | solution.py:567
  26.4 0.4 %collective-permute-done.3.own_share_ref = f32[64,128]{1,0:T(8,128)S(1)} collective-permute-done((f32[64,128]{1,0:T(8,128)S(1)}, f32[64,128]{1,0:T(8,128)S(1)}, u32[]{:S(2)}, u32[]{:S(2)}) %collective-permute-start.3) | collective-permute-done | bytes 32800 | tf_op jit(solution)/shard_map/ppermute | solution.py:567
  26.8 0.0 collective-permute-done.4.other_share_ref
  26.8 0.3 %collective-permute-done.6.refs_2_ = f32[64,128]{1,0:T(8,128)S(1)} collective-permute-done((f32[64,128]{1,0:T(8,128)S(1)}, f32[64,128]{1,0:T(8,128)S(1)}, u32[]{:S(2)}, u32[]{:S(2)}) %collective-permute-start.6) | collective-permute-done | bytes 32800 | tf_op jit(solution)/shard_map/ppermute | solution.py:567
  27.1 0.2 collective-permute-done.7.refs_3_
  27.3 0.6 %gradient.1 = f32[128,128]{1,0:T(8,128)} custom-call(f32[128,128]{1,0:T(8,128)S(1)} %get-tuple-element.14.refs_4_.half_ref, f32[64,128]{1,0:T(8,128)S(1)} %collective-permute-done.3.own_share_ref, f32[64,128]{1,0:T(8,128)S(1)} %collective-permute-done.4.other_share_ref, f32[64,128]{1,0:T(8,128)S(1)} %get-tuple-element.21.refs_0_, ...), custom_call_target="tpu_custom_call" | custom-call | bytes 10000 | tf_op jit(solution)/shard_map/gradient/pallas_call | solution.py:625
Async XLA Ops:
  0.0 6.4 %copy-start = (f32[1,2,2,6,32,2,256]{6,5,4,3,2,1,0:T(2,128)S(1)}, f32[1,2,2,6,32,2,256]{6,5,4,3,2,1,0:T(2,128)}, u32[]{:S(2)}) copy-start(f32[1,2,2,6,32,2,256]{6,5,4,3,2,1,0:T(2,128)} %param.6) | copy-start | bytes 4718596
  0.0 6.4 %copy-start.1 = (s32[32,2,256]{2,1,0:T(2,128)S(1)}, s32[32,2,256]{2,1,0:T(2,128)}, u32[]{:S(2)}) copy-start(s32[32,2,256]{2,1,0:T(2,128)} %param.7) | copy-start | bytes 196612
  1.3 7.0 %copy-start.2 = (f32[1,2,2,2]{3,2,1,0:T(2,128)S(1)}, f32[1,2,2,2]{3,2,1,0:T(2,128)}, u32[]{:S(2)}) copy-start(f32[1,2,2,2]{3,2,1,0:T(2,128)} %wave_ref.1) | copy-start | bytes 100
  1.3 7.0 %copy-start.3 = (f32[8]{0:T(128)S(1)}, f32[8]{0:T(128)}, u32[]{:S(2)}) copy-start(f32[8]{0:T(128)} %table_ref.1) | copy-start | bytes 100
  1.3 7.0 %copy-start.4 = (f32[2]{0:T(128)S(1)}, f32[2]{0:T(128)}, u32[]{:S(2)}) copy-start(f32[2]{0:T(128)} %phase_ref.1) | copy-start | bytes 28
  1.3 7.0 %copy-start.5 = (s32[1,2]{1,0:T(1,128)S(1)}, s32[1,2]{1,0:T(1,128)}, u32[]{:S(2)}) copy-start(s32[1,2]{1,0:T(1,128)} %cells_ref.1) | copy-start | bytes 28
  1.3 11.8 %collective-permute-start.1 = (f32[512,128]{1,0:T(8,128)S(1)}, f32[512,128]{1,0:T(8,128)S(1)}, u32[]{:S(2)}, u32[]{:S(2)}) collective-permute-start(f32[512,128]{1,0:T(8,128)S(1)} %faces.1.order_ref), channel_id=1, source_target_pairs={{0,12},{4,0},{8,4},{12,8},{1,13},{5,1},{9,5},{13,9},{2,14},{6,2},{... | collective-permute-start | bytes 786440 | tf_op jit(solution)/shard_map/ppermute | solution.py:567
  6.7 4.0 %collective-permute-start = (f32[64,128]{1,0:T(8,128)S(1)}, f32[64,128]{1,0:T(8,128)S(1)}, u32[]{:S(2)}, u32[]{:S(2)}) collective-permute-start(f32[64,128]{1,0:T(8,128)S(1)} %edges.1.order_ref), channel_id=1, source_target_pairs={{0,2},{2,0},{1,3},{3,1},{4,6},{6,4},{5,7},{7,5},{8,10},{10,8},{9,1... | collective-permute-start | bytes 98312 | tf_op jit(solution)/shard_map/ppermute | solution.py:567
  11.4 8.8 %collective-permute-start.2 = (f32[592,128]{1,0:T(8,128)S(1)}, f32[592,128]{1,0:T(8,128)S(1)}, u32[]{:S(2)}, u32[]{:S(2)}) collective-permute-start(f32[592,128]{1,0:T(8,128)S(1)} %lower.1), channel_id=1, source_target_pairs={{0,12},{4,0},{8,4},{12,8},{1,13},{5,1},{9,5},{13,9},{2,14},{6,2},{... | collective-permute-start | bytes 909320 | tf_op jit(solution)/shard_map/ppermute | solution.py:567
  13.5 12.0 %collective-permute-start.5 = (f32[520,128]{1,0:T(8,128)S(1)}, f32[520,128]{1,0:T(8,128)S(1)}, u32[]{:S(2)}, u32[]{:S(2)}) collective-permute-start(f32[520,128]{1,0:T(8,128)S(1)} %upper.1), channel_id=1, source_target_pairs={{0,4},{4,8},{8,12},{12,0},{1,5},{5,9},{9,13},{13,1},{2,6},{6,10},{... | collective-permute-start | bytes 798728 | tf_op jit(solution)/shard_map/ppermute | solution.py:567
  21.0 5.8 %collective-permute-start.3 = (f32[64,128]{1,0:T(8,128)S(1)}, f32[64,128]{1,0:T(8,128)S(1)}, u32[]{:S(2)}, u32[]{:S(2)}) collective-permute-start(f32[64,128]{1,0:T(8,128)S(1)} %get-tuple-element.17.refs_8_), channel_id=1, source_target_pairs={{0,4},{4,8},{8,12},{12,0},{1,5},{5,9},{9,13},{13,1},{2,6},{6,10},{... | collective-permute-start | bytes 98312 | tf_op jit(solution)/shard_map/ppermute | solution.py:567
  21.1 5.7 %collective-permute-start.4 = (f32[64,128]{1,0:T(8,128)S(1)}, f32[64,128]{1,0:T(8,128)S(1)}, u32[]{:S(2)}, u32[]{:S(2)}) collective-permute-start(f32[64,128]{1,0:T(8,128)S(1)} %get-tuple-element.17.refs_8_), channel_id=1, source_target_pairs={{0,5},{1,4},{4,9},{5,8},{8,13},{9,12},{12,1},{13,0},{2,7},{3,6},{6... | collective-permute-start | bytes 98312 | tf_op jit(solution)/shard_map/ppermute | solution.py:612
  25.9 1.3 %collective-permute-start.6 = (f32[64,128]{1,0:T(8,128)S(1)}, f32[64,128]{1,0:T(8,128)S(1)}, u32[]{:S(2)}, u32[]{:S(2)}) collective-permute-start(f32[64,128]{1,0:T(8,128)S(1)} %get-tuple-element.21.refs_0_), channel_id=1, source_target_pairs={{0,1},{1,0},{2,3},{3,2},{4,5},{5,4},{6,7},{7,6},{8,9},{9,8},{10,11... | collective-permute-start | bytes 98312 | tf_op jit(solution)/shard_map/ppermute | solution.py:567
  25.9 1.4 %collective-permute-start.7 = (f32[64,128]{1,0:T(8,128)S(1)}, f32[64,128]{1,0:T(8,128)S(1)}, u32[]{:S(2)}, u32[]{:S(2)}) collective-permute-start(f32[64,128]{1,0:T(8,128)S(1)} %get-tuple-element.22.refs_1_), channel_id=1, source_target_pairs={{0,1},{1,0},{2,3},{3,2},{4,5},{5,4},{6,7},{7,6},{8,9},{9,8},{10,11... | collective-permute-start | bytes 98312 | tf_op jit(solution)/shard_map/ppermute | solution.py:567
